TPU v7x, 256 devices: a whole 4x4x8 slice. The times are simulated.
256 devices in a mesh: seq: 32 (over z, y), head: 4 (over x), rep: 2 (over core).
Axes of the slice: x: 4, y: 4, z: 8, core: 2. Of those that a mesh axis runs over, the one named last changes fastest.
Arguments:
- queries: bfloat16 [16384, 2048], P(('rep', 'seq'), 'head'), parts along dimension 0, may hold values from -5 to 5
- keys: bfloat16 [16384, 2048], P(('rep', 'seq'), 'head'), parts along dimension 0, may hold values from -5 to 5
- values: bfloat16 [16384, 2048], P(('rep', 'seq'), 'head'), parts along dimension 0, may hold values from -4 to 4
- cotangent: bfloat16 [16384, 2048], P(('rep', 'seq'), 'head'), parts along dimension 0, may hold values from -4 to 4
Outputs:
- attended: bfloat16 [16384, 2048], P(('rep', 'seq'), 'head'), parts along dimension 0
- grad_queries: bfloat16 [16384, 2048], P(('rep', 'seq'), 'head'), parts along dimension 0
- grad_keys: bfloat16 [16384, 2048], P(('rep', 'seq'), 'head'), parts along dimension 0
- grad_values: bfloat16 [16384, 2048], P(('rep', 'seq'), 'head'), parts along dimension 0
There are 2 independent parts, one for each index of `rep`. A program takes and returns all parts, laid end to end along the dimension named above; each array names one. Nothing has to cross between parts.
All inputs are finite; a program needn't handle non-finite values.
Results may differ from a plain program's by a relative error of at most 0.012.
Values may be sent and summed in bfloat16 or wider, within the bound.
No kernel may reach another device: no remote copies, remote signals or barrier semaphores. Data moves between devices by JAX's collectives and lax.ppermute only.
A program may use at most 128 MiB of HBM per device.

v0:
```python
import math

import jax
import jax.numpy as jnp
from jax import lax
from jax.sharding import PartitionSpec as P

HEAD_DIM = 128
BLOCK = 128


ROOT_HALF = 0.7071067811865476


def partner_2(array, axis, distance):
    return lax.ppermute(array, axis, [(i, i ^ 1 << distance) for i in range(lax.axis_size(axis))])


def padded(block, sides, width):
    for axis, dim in sides:
        count = lax.axis_size(axis)
        forward = [(i, i + 1) for i in range(count - 1)]
        backward = [(target, source) for source, target in forward]
        low = lax.ppermute(
            lax.slice_in_dim(block, block.shape[dim] - width, None, axis=dim), axis, forward
        )
        high = lax.ppermute(lax.slice_in_dim(block, 0, width, axis=dim), axis, backward)
        block = jnp.concatenate([low, block, high], axis=dim)
    return block


def shifted(value, axis, steps):
    count = lax.axis_size(axis)
    leading, last = (max(0, -steps), min(count, count - steps))
    return lax.ppermute(value, axis, [(source, source + steps) for source in range(leading, last)])


def pooled(stacked):
    paired = stacked.astype(jnp.float32).reshape(
        stacked.shape[0], stacked.shape[1] // 2, 2, stacked.shape[2]
    )
    return ((paired[:, :, 0] + paired[:, :, 1]) * ROOT_HALF).astype(jnp.bfloat16)


def spread(gradients):
    return jnp.repeat(gradients * ROOT_HALF, 2, axis=1)


def lower_half(position, which_bit):
    return position // (1 << which_bit) % 2 == 0


def climb(summary, position, level_count):
    group_keys = summary
    received = []
    for which_bit in range(level_count):
        partner = partner_2(group_keys, "seq", which_bit)
        received.append(partner)
        if which_bit + 1 < level_count:
            leading = lower_half(position, which_bit)
            group_keys = pooled(
                jnp.where(
                    leading,
                    jnp.concatenate([group_keys, partner], axis=1),
                    jnp.concatenate([partner, group_keys], axis=1),
                )
            )
    return received


def descend(partner_grads, position, level_count):
    carried = None
    for which_bit in reversed(range(level_count)):
        outgoing = partner_grads[which_bit]
        kept_half = None
        if carried is not None:
            widened = spread(carried)
            half_rows = widened.shape[1] // 2
            leading = lower_half(position, which_bit)
            kept_half = jnp.where(leading, widened[:, :half_rows], widened[:, half_rows:])
            outgoing = outgoing + jnp.where(leading, widened[:, half_rows:], widened[:, :half_rows])
        returned = partner_2(outgoing, "seq", which_bit)
        carried = returned if kept_half is None else kept_half + returned
    return carried


def attend_head(queries, cotangent, near_keys, near_values, far_keys, far_values, allowed):
    block_count, near_width, head_dim = near_keys.shape
    block_rows = queries.shape[0] // block_count
    score_scale = 1.0 / math.sqrt(head_dim)
    q_blocks = queries.reshape(block_count, block_rows, head_dim)
    c_blocks = cotangent.reshape(block_count, block_rows, head_dim)
    near_score = (
        jnp.einsum("jbd,jkd->jbk", q_blocks, near_keys, preferred_element_type=jnp.float32)
        * score_scale
    )
    near_score = jnp.where(allowed, near_score, -jnp.inf)
    far_score = (
        jnp.einsum("jbd,kd->jbk", q_blocks, far_keys, preferred_element_type=jnp.float32)
        * score_scale
    )
    highest = jnp.maximum(
        jnp.max(near_score, axis=2, keepdims=True), jnp.max(far_score, axis=2, keepdims=True)
    )
    near_raised = jnp.exp(near_score - highest)
    far_raised = jnp.exp(far_score - highest)
    denominator = jnp.sum(near_raised, axis=2, keepdims=True) + jnp.sum(
        far_raised, axis=2, keepdims=True
    )
    near_prob = near_raised / denominator
    far_prob = far_raised / denominator
    near_weight = near_prob.astype(jnp.bfloat16)
    far_weight = far_prob.astype(jnp.bfloat16)
    output = jnp.einsum(
        "jbk,jkd->jbd", near_weight, near_values, preferred_element_type=jnp.float32
    ) + jnp.einsum("jbk,kd->jbd", far_weight, far_values, preferred_element_type=jnp.float32)
    row_dot = jnp.sum(c_blocks.astype(jnp.float32) * output, axis=2, keepdims=True)
    near_pgrad = jnp.einsum(
        "jbd,jkd->jbk", c_blocks, near_values, preferred_element_type=jnp.float32
    )
    far_pgrad = jnp.einsum("jbd,kd->jbk", c_blocks, far_values, preferred_element_type=jnp.float32)
    near_sgrad = (near_prob * (near_pgrad - row_dot) * score_scale).astype(jnp.bfloat16)
    far_sgrad = (far_prob * (far_pgrad - row_dot) * score_scale).astype(jnp.bfloat16)
    query_grad = jnp.einsum(
        "jbk,jkd->jbd", near_sgrad, near_keys, preferred_element_type=jnp.float32
    ) + jnp.einsum("jbk,kd->jbd", far_sgrad, far_keys, preferred_element_type=jnp.float32)
    near_kgrad = jnp.einsum(
        "jbk,jbd->jkd", near_sgrad, q_blocks, preferred_element_type=jnp.float32
    )
    near_vgrad = jnp.einsum(
        "jbk,jbd->jkd", near_weight, c_blocks, preferred_element_type=jnp.float32
    )
    far_kgrad = jnp.einsum("jbk,jbd->kd", far_sgrad, q_blocks, preferred_element_type=jnp.float32)
    far_vgrad = jnp.einsum("jbk,jbd->kd", far_weight, c_blocks, preferred_element_type=jnp.float32)
    total_rows = block_count * block_rows
    return (
        output.reshape(total_rows, head_dim),
        query_grad.reshape(total_rows, head_dim),
        near_kgrad,
        near_vgrad,
        far_kgrad,
        far_vgrad,
    )


def per_device(queries, keys, values, cotangent):
    tok_rows, columns = queries.shape
    block_rows = BLOCK
    block_count = tok_rows // block_rows
    local_levels = block_count.bit_length() - 1
    head_count = columns // HEAD_DIM
    position = lax.axis_index("seq")
    device_count = lax.axis_size("seq")
    cross_levels = device_count.bit_length() - 1
    last_index = device_count - 1
    stacked = jnp.stack([keys, values])
    edged = padded(stacked, (("seq", 1),), block_rows)
    levels = [stacked]
    height = 0
    levels.append(pooled(levels[-1]))
    summary = levels[local_levels]
    partners = climb(summary, position, cross_levels)
    far_pair = jnp.concatenate(partners, axis=1)
    block_keys = []
    for block_no in range(block_count):
        pieces = edged[:, block_no * block_rows : (block_no + 3) * block_rows]
        block_keys.append(pieces)
    near_pair = jnp.stack(block_keys, axis=1)
    near_width = near_pair.shape[2]
    column_ids = jnp.arange(near_width)[None, :]
    block_ids = jnp.arange(block_count)[:, None]
    allowed = ((column_ids >= block_rows) | (block_ids > 0) | (position > 0)) & (
        (column_ids < 2 * block_rows)
        | (column_ids >= 3 * block_rows)
        | (block_ids < block_count - 1)
        | (position < last_index)
    )
    allowed = allowed[:, None, :]
    outputs = []
    for head_no in range(head_count):
        head_cols = slice(head_no * HEAD_DIM, (head_no + 1) * HEAD_DIM)
        outputs.append(
            attend_head(
                queries[:, head_cols],
                cotangent[:, head_cols],
                near_pair[0, :, :, head_cols],
                near_pair[1, :, :, head_cols],
                far_pair[0, :, head_cols],
                far_pair[1, :, head_cols],
                allowed,
            )
        )
    merged = [
        jnp.concatenate([result_set[member] for result_set in outputs], axis=-1)
        for member in range(6)
    ]
    attended, grad_query, near_kgrad, near_vgrad, far_kgrad, far_vgrad = merged
    near_grads = jnp.stack([near_kgrad, near_vgrad])
    far_grads = jnp.stack([far_kgrad, far_vgrad])
    fine_grads = near_grads.reshape(2, block_count, 3, block_rows, columns)
    ext_blocks = jnp.zeros((2, block_count + 2, block_rows, columns), jnp.float32)
    for offset_no in range(3):
        ext_blocks = ext_blocks.at[:, offset_no : offset_no + block_count].add(
            fine_grads[:, :, offset_no]
        )
    ext_grads = ext_blocks.reshape(2, (block_count + 2) * block_rows, columns)
    from_right = shifted(ext_grads[:, :block_rows].astype(jnp.bfloat16), "seq", -1).astype(
        jnp.float32
    )
    from_left = shifted(ext_grads[:, -block_rows:].astype(jnp.bfloat16), "seq", 1).astype(
        jnp.float32
    )
    own_grads = ext_grads[:, block_rows:-block_rows]
    own_grads = own_grads.at[:, :block_rows].add(from_left)
    own_grads = own_grads.at[:, -block_rows:].add(from_right)
    partner_grads = [
        far_grads[:, height * block_rows : (height + 1) * block_rows]
        for height in range(cross_levels)
    ]
    summary_grads = descend(partner_grads, position, cross_levels)
    full_grads = own_grads + spread(summary_grads)
    return (
        attended.astype(jnp.bfloat16),
        grad_query.astype(jnp.bfloat16),
        full_grads[0].astype(jnp.bfloat16),
        full_grads[1].astype(jnp.bfloat16),
    )


def solution(mesh):
    in_specs = (
        P(("rep", "seq"), "head"),
        P(("rep", "seq"), "head"),
        P(("rep", "seq"), "head"),
        P(("rep", "seq"), "head"),
    )
    out_specs = (
        P(("rep", "seq"), "head"),
        P(("rep", "seq"), "head"),
        P(("rep", "seq"), "head"),
        P(("rep", "seq"), "head"),
    )
    return jax.shard_map(
        per_device, mesh=mesh, in_specs=in_specs, out_specs=out_specs, check_vma=False
    )
```

profile of v0, /device:TPU:6, one launch (start us, length us, event | category | flops | bytes accessed | tf_op | source)
XLA Modules:
  0.0 228.8 jit_solution(8236996452904174687)
XLA Ops:
  3.1 1.7 collective-permute-start.2
  4.8 1.3 collective-permute-start.1
  6.1 4.6 %collective-permute-start = (bf16[2,128,512]{2,1,0:T(8,128)(2,1)S(1)}, bf16[2,128,512]{2,1,0:T(8,128)(2,1)S(1)}, u32[]{:S(2)}, u32[]{:S(2)}) collective-permute-start(bf16[2,128,512]{2,1,0:T(8,128)(2,1)S(1)} %get-tuple-element.92), channel_id=1, source_target_pairs={{0,8},{8,16},{16,24},{24,32},{32,40},{40,48},{48,56},{56,64},{64,7... | collective-permute-start | bytes 786440 | tf_op jit(solution)/shard_map/ppermute | solution.py:24
  14.0 3.3 %collective-permute-start.3 = (bf16[2,128,512]{2,1,0:T(8,128)(2,1)S(1)}, bf16[2,128,512]{2,1,0:T(8,128)(2,1)S(1)}, u32[]{:S(2)}, u32[]{:S(2)}) collective-permute-start(bf16[2,128,512]{2,1,0:T(8,128)(2,1)S(1)} %fusion.97), channel_id=1, source_target_pairs={{0,16},{8,24},{16,0},{24,8},{32,48},{40,56},{48,32},{56,40},{64,80... | collective-permute-start | bytes 786440 | tf_op jit(solution)/shard_map/ppermute | solution.py:16
  18.3 1.6 fusion.173
  19.9 5.0 %collective-permute-done.3 = bf16[2,128,512]{2,1,0:T(8,128)(2,1)S(1)} collective-permute-done((bf16[2,128,512]{2,1,0:T(8,128)(2,1)S(1)}, bf16[2,128,512]{2,1,0:T(8,128)(2,1)S(1)}, u32[]{:S(2)}, u32[]{:S(2)}) %collective-permute-start.3) | collective-permute-done | bytes 262176 | tf_op jit(solution)/shard_map/ppermute | solution.py:16
  27.2 2.9 %collective-permute-start.4 = (bf16[2,128,512]{2,1,0:T(8,128)(2,1)S(1)}, bf16[2,128,512]{2,1,0:T(8,128)(2,1)S(1)}, u32[]{:S(2)}, u32[]{:S(2)}) collective-permute-start(bf16[2,128,512]{2,1,0:T(8,128)(2,1)S(1)} %fusion.98), channel_id=1, source_target_pairs={{0,32},{8,40},{16,48},{24,56},{32,0},{40,8},{48,16},{56,24},{64,96... | collective-permute-start | bytes 786440 | tf_op jit(solution)/shard_map/ppermute | solution.py:16
  30.5 4.6 %collective-permute-done.4 = bf16[2,128,512]{2,1,0:T(8,128)(2,1)S(1)} collective-permute-done((bf16[2,128,512]{2,1,0:T(8,128)(2,1)S(1)}, bf16[2,128,512]{2,1,0:T(8,128)(2,1)S(1)}, u32[]{:S(2)}, u32[]{:S(2)}) %collective-permute-start.4) | collective-permute-done | bytes 262176 | tf_op jit(solution)/shard_map/ppermute | solution.py:16
  37.4 3.4 %collective-permute-start.5 = (bf16[2,128,512]{2,1,0:T(8,128)(2,1)S(1)}, bf16[2,128,512]{2,1,0:T(8,128)(2,1)S(1)}, u32[]{:S(2)}, u32[]{:S(2)}) collective-permute-start(bf16[2,128,512]{2,1,0:T(8,128)(2,1)S(1)} %fusion.99), channel_id=1, source_target_pairs={{0,64},{8,72},{16,80},{24,88},{32,96},{40,104},{48,112},{56,120},{... | collective-permute-start | bytes 786440 | tf_op jit(solution)/shard_map/ppermute | solution.py:16
  42.5 8.3 %collective-permute-done.5 = bf16[2,128,512]{2,1,0:T(8,128)(2,1)S(1)} collective-permute-done((bf16[2,128,512]{2,1,0:T(8,128)(2,1)S(1)}, bf16[2,128,512]{2,1,0:T(8,128)(2,1)S(1)}, u32[]{:S(2)}, u32[]{:S(2)}) %collective-permute-start.5) | collective-permute-done | bytes 262176 | tf_op jit(solution)/shard_map/ppermute | solution.py:16
  52.6 1.8 reshape.461
  55.5 7.7 %collective-permute-start.6 = (bf16[2,128,512]{2,1,0:T(8,128)(2,1)S(1)}, bf16[2,128,512]{2,1,0:T(8,128)(2,1)S(1)}, u32[]{:S(2)}, u32[]{:S(2)}) collective-permute-start(bf16[2,128,512]{2,1,0:T(8,128)(2,1)S(1)} %fusion.100), channel_id=1, source_target_pairs={{0,128},{8,136},{16,144},{24,152},{32,160},{40,168},{48,176},{56,1... | collective-permute-start | bytes 786440 | tf_op jit(solution)/shard_map/ppermute | solution.py:16
  63.3 11.6 %collective-permute-done.6 = bf16[2,128,512]{2,1,0:T(8,128)(2,1)S(1)} collective-permute-done((bf16[2,128,512]{2,1,0:T(8,128)(2,1)S(1)}, bf16[2,128,512]{2,1,0:T(8,128)(2,1)S(1)}, u32[]{:S(2)}, u32[]{:S(2)}) %collective-permute-start.6) | collective-permute-done | bytes 262176 | tf_op jit(solution)/shard_map/ppermute | solution.py:16
  97.2 1.6 copy.110
  100.2 1.6 copy.101
  103.3 3.2 %collective-permute-start.9 = (f32[2,128,512]{1,2,0:T(8,128)S(1)}, f32[2,128,512]{1,2,0:T(8,128)S(1)}, u32[]{:S(2)}, u32[]{:S(2)}) collective-permute-start(f32[2,128,512]{1,2,0:T(8,128)S(1)} %fusion.67), channel_id=1, source_target_pairs={{0,128},{8,136},{16,144},{24,152},{32,160},{40,168},{48,176},{56,1... | collective-permute-start | bytes 1572872 | tf_op jit(solution)/shard_map/ppermute | solution.py:16
  106.5 1.6 scatter-add.16
  108.2 2.5 %fusion.51 = f32[2,4,128,512]{3,2,1,0:T(8,128)} fusion(f32[2,4,128,512]{3,2,1,0:T(8,128)} %scatter-add.16, f32[1,2,3,128,512]{4,3,2,1,0:T(8,128)S(1)} %bitcast.332, f32[1,2,3,128,512]{4,3,2,1,0:T(8,128)S(1)} %bitcast.329), kind=kLoop, calls=%fused_computation.113 | loop fusion | flops 524288 | bytes 5242880 | tf_op jit(solution)/shard_map/scatter-add | solution.py:203
  111.8 2.4 %fusion.56 = f32[2,4,128,512]{3,2,1,0:T(8,128)} fusion(f32[2,4,128,512]{3,2,1,0:T(8,128)} %fusion.51, f32[1,2,3,128,512]{4,3,2,1,0:T(8,128)S(1)} %bitcast.330, f32[1,2,3,128,512]{4,3,2,1,0:T(8,128)S(1)} %bitcast.333), kind=kLoop, calls=%fused_computation.119 | loop fusion | flops 524288 | bytes 5242880 | tf_op jit(solution)/shard_map/scatter-add | solution.py:203
  114.2 14.7 %collective-permute-done.9 = f32[2,128,512]{1,2,0:T(8,128)S(1)} collective-permute-done((f32[2,128,512]{1,2,0:T(8,128)S(1)}, f32[2,128,512]{1,2,0:T(8,128)S(1)}, u32[]{:S(2)}, u32[]{:S(2)}) %collective-permute-start.9) | collective-permute-done | bytes 524320 | tf_op jit(solution)/shard_map/ppermute | solution.py:16
  129.8 1.3 copy.129
  131.3 1.3 fusion.159
  132.7 1.2 copy.200
  133.9 2.0 copy.201
  137.2 1.8 bitcast_convert_fusion
  139.8 21.9 %collective-permute-done.10 = f32[2,128,512]{1,2,0:T(8,128)S(1)} collective-permute-done((f32[2,128,512]{1,2,0:T(8,128)S(1)}, f32[2,128,512]{1,2,0:T(8,128)S(1)}, u32[]{:S(2)}, u32[]{:S(2)}) %collective-permute-start.10) | collective-permute-done | bytes 524320 | tf_op jit(solution)/shard_map/ppermute | solution.py:16
  162.6 1.3 copy.132
  164.1 1.3 fusion.158
  165.5 1.2 copy.202
  166.7 2.0 copy.203
  168.8 1.2 fusion.71
  171.0 1.3 collective-permute-start.8
  172.3 5.3 %collective-permute-start.7 = (bf16[2,128,512]{2,1,0:T(8,128)(2,1)}, bf16[2,128,512]{2,1,0:T(8,128)(2,1)}, u32[]{:S(2)}, u32[]{:S(2)}) collective-permute-start(bf16[2,128,512]{2,1,0:T(8,128)(2,1)} %get-tuple-element.78), channel_id=1, source_target_pairs={{0,8},{8,16},{16,24},{24,32},{32,40},{40,48},{48,56},{56,64},{64,7... | collective-permute-start | bytes 786440 | tf_op jit(solution)/shard_map/ppermute | solution.py:35
  177.6 1.8 fusion.44
  179.4 1.8 fusion.45
  181.3 3.6 %collective-permute-done.11 = f32[2,128,512]{1,2,0:T(8,128)S(1)} collective-permute-done((f32[2,128,512]{1,2,0:T(8,128)S(1)}, f32[2,128,512]{1,2,0:T(8,128)S(1)}, u32[]{:S(2)}, u32[]{:S(2)}) %collective-permute-start.11) | collective-permute-done | bytes 524320 | tf_op jit(solution)/shard_map/ppermute | solution.py:16
  185.8 1.3 copy.135
  187.3 1.3 fusion.157
  188.6 1.2 copy.204
  189.9 2.0 copy.205
  196.5 10.3 %collective-permute-done.12 = f32[2,128,512]{1,2,0:T(8,128)S(1)} collective-permute-done((f32[2,128,512]{1,2,0:T(8,128)S(1)}, f32[2,128,512]{1,2,0:T(8,128)S(1)}, u32[]{:S(2)}, u32[]{:S(2)}) %collective-permute-start.12) | collective-permute-done | bytes 524320 | tf_op jit(solution)/shard_map/ppermute | solution.py:16
  207.7 1.3 copy.138
  209.3 1.3 fusion.156
  210.6 1.2 copy.206
  211.9 2.0 copy.207
  215.9 1.3 slice.420
  217.2 1.2 fusion.74
  219.6 6.7 %collective-permute-done.13 = f32[2,128,512]{1,2,0:T(8,128)S(1)} collective-permute-done((f32[2,128,512]{1,2,0:T(8,128)S(1)}, f32[2,128,512]{1,2,0:T(8,128)S(1)}, u32[]{:S(2)}, u32[]{:S(2)}) %collective-permute-start.13) | collective-permute-done | bytes 524320 | tf_op jit(solution)/shard_map/ppermute | solution.py:16
  (276 shorter events, 59.7 us)
Async XLA Ops:
  2.9 7.8 %copy-start.61 = (bf16[256,512]{1,0:T(8,128)(2,1)S(1)}, bf16[256,512]{1,0:T(8,128)(2,1)}, u32[]{:S(2)}) copy-start(bf16[256,512]{1,0:T(8,128)(2,1)} %param.14) | copy-start | bytes 786436
  2.9 7.9 %copy-start.62 = (bf16[256,512]{1,0:T(8,128)(2,1)S(1)}, bf16[256,512]{1,0:T(8,128)(2,1)}, u32[]{:S(2)}) copy-start(bf16[256,512]{1,0:T(8,128)(2,1)} %param.17) | copy-start | bytes 786436
  3.1 9.3 %collective-permute-start.2 = (bf16[2,128,512]{2,1,0:T(8,128)(2,1)S(1)}, bf16[2,128,512]{2,1,0:T(8,128)(2,1)S(1)}, u32[]{:S(2)}, u32[]{:S(2)}) collective-permute-start(bf16[2,128,512]{2,1,0:T(8,128)(2,1)S(1)} %fusion.102), channel_id=1, source_target_pairs={{0,8},{8,0},{16,24},{24,16},{32,40},{40,32},{48,56},{56,48},{64,72... | collective-permute-start | bytes 786440 | tf_op jit(solution)/shard_map/ppermute | solution.py:16
  4.8 12.5 %collective-permute-start.1 = (bf16[2,128,512]{2,1,0:T(8,128)(2,1)S(1)}, bf16[2,128,512]{2,1,0:T(8,128)(2,1)S(1)}, u32[]{:S(2)}, u32[]{:S(2)}) collective-permute-start(bf16[2,128,512]{2,1,0:T(8,128)(2,1)S(1)} %get-tuple-element.91), channel_id=1, source_target_pairs={{8,0},{16,8},{24,16},{32,24},{40,32},{48,40},{56,48},{64,56},{72,6... | collective-permute-start | bytes 786440 | tf_op jit(solution)/shard_map/ppermute | solution.py:27
  6.1 11.2 %collective-permute-start = (bf16[2,128,512]{2,1,0:T(8,128)(2,1)S(1)}, bf16[2,128,512]{2,1,0:T(8,128)(2,1)S(1)}, u32[]{:S(2)}, u32[]{:S(2)}) collective-permute-start(bf16[2,128,512]{2,1,0:T(8,128)(2,1)S(1)} %get-tuple-element.92), channel_id=1, source_target_pairs={{0,8},{8,16},{16,24},{24,32},{32,40},{40,48},{48,56},{56,64},{64,7... | collective-permute-start | bytes 786440 | tf_op jit(solution)/shard_map/ppermute | solution.py:24
  10.8 7.5 %copy-start.22 = (bf16[256,128]{1,0:T(8,128)(2,1)}, bf16[256,128]{1,0:T(8,128)(2,1)S(1)}, u32[]{:S(2)}) copy-start(bf16[256,128]{1,0:T(8,128)(2,1)S(1)} %get-tuple-element.97) | copy-start | bytes 196612
  10.8 19.3 %copy-start.20 = (bf16[256,128]{1,0:T(8,128)(2,1)}, bf16[256,128]{1,0:T(8,128)(2,1)S(1)}, u32[]{:S(2)}) copy-start(bf16[256,128]{1,0:T(8,128)(2,1)S(1)} %get-tuple-element.98) | copy-start | bytes 196612
  14.0 10.9 %collective-permute-start.3 = (bf16[2,128,512]{2,1,0:T(8,128)(2,1)S(1)}, bf16[2,128,512]{2,1,0:T(8,128)(2,1)S(1)}, u32[]{:S(2)}, u32[]{:S(2)}) collective-permute-start(bf16[2,128,512]{2,1,0:T(8,128)(2,1)S(1)} %fusion.97), channel_id=1, source_target_pairs={{0,16},{8,24},{16,0},{24,8},{32,48},{40,56},{48,32},{56,40},{64,80... | collective-permute-start | bytes 786440 | tf_op jit(solution)/shard_map/ppermute | solution.py:16
  18.3 11.8 %copy-start.16 = (bf16[1,2,384,128]{3,2,1,0:T(8,128)(2,1)}, bf16[1,2,384,128]{3,2,1,0:T(8,128)(2,1)S(1)}, u32[]{:S(2)}) copy-start(bf16[1,2,384,128]{3,2,1,0:T(8,128)(2,1)S(1)} %get-tuple-element.65) | copy-start | bytes 589828
  18.3 12.0 %copy-start.14 = (bf16[1,2,384,128]{3,2,1,0:T(8,128)(2,1)}, bf16[1,2,384,128]{3,2,1,0:T(8,128)(2,1)S(1)}, u32[]{:S(2)}) copy-start(bf16[1,2,384,128]{3,2,1,0:T(8,128)(2,1)S(1)} %get-tuple-element.66) | copy-start | bytes 589828
  18.3 23.2 %copy-start.12 = (bf16[1,2,384,128]{3,2,1,0:T(8,128)(2,1)}, bf16[1,2,384,128]{3,2,1,0:T(8,128)(2,1)S(1)}, u32[]{:S(2)}) copy-start(bf16[1,2,384,128]{3,2,1,0:T(8,128)(2,1)S(1)} %get-tuple-element.68) | copy-start | bytes 589828
  27.2 7.9 %collective-permute-start.4 = (bf16[2,128,512]{2,1,0:T(8,128)(2,1)S(1)}, bf16[2,128,512]{2,1,0:T(8,128)(2,1)S(1)}, u32[]{:S(2)}, u32[]{:S(2)}) collective-permute-start(bf16[2,128,512]{2,1,0:T(8,128)(2,1)S(1)} %fusion.98), channel_id=1, source_target_pairs={{0,32},{8,40},{16,48},{24,56},{32,0},{40,8},{48,16},{56,24},{64,96... | collective-permute-start | bytes 786440 | tf_op jit(solution)/shard_map/ppermute | solution.py:16
  36.9 3.9 %copy-start.42 = (bf16[2,128,512]{2,1,0:T(8,128)(2,1)S(1)}, bf16[2,128,512]{2,1,0:T(8,128)(2,1)}, u32[]{:S(2)}) copy-start(bf16[2,128,512]{2,1,0:T(8,128)(2,1)} %copy-done.41) | copy-start | bytes 786436
  37.4 13.3 %collective-permute-start.5 = (bf16[2,128,512]{2,1,0:T(8,128)(2,1)S(1)}, bf16[2,128,512]{2,1,0:T(8,128)(2,1)S(1)}, u32[]{:S(2)}, u32[]{:S(2)}) collective-permute-start(bf16[2,128,512]{2,1,0:T(8,128)(2,1)S(1)} %fusion.99), channel_id=1, source_target_pairs={{0,64},{8,72},{16,80},{24,88},{32,96},{40,104},{48,112},{56,120},{... | collective-permute-start | bytes 786440 | tf_op jit(solution)/shard_map/ppermute | solution.py:16
  54.5 8.7 %copy-start.6 = (bf16[2,640,512]{2,1,0:T(8,128)(2,1)S(1)}, bf16[2,640,512]{2,1,0:T(8,128)(2,1)}, u32[]{:S(2)}) copy-start(bf16[2,640,512]{2,1,0:T(8,128)(2,1)} %constant_dynamic-update-slice_fusion.4) | copy-start | bytes 3932164
  54.5 8.7 %copy-start.44 = (bf16[2,128,512]{2,1,0:T(8,128)(2,1)S(1)}, bf16[2,128,512]{2,1,0:T(8,128)(2,1)}, u32[]{:S(2)}) copy-start(bf16[2,128,512]{2,1,0:T(8,128)(2,1)} %copy-done.43) | copy-start | bytes 786436
  54.5 8.7 %copy-start.46 = (bf16[2,128,512]{2,1,0:T(8,128)(2,1)S(1)}, bf16[2,128,512]{2,1,0:T(8,128)(2,1)}, u32[]{:S(2)}) copy-start(bf16[2,128,512]{2,1,0:T(8,128)(2,1)} %copy-done.45) | copy-start | bytes 786436
  55.3 7.9 %copy-start.48 = (bf16[2,128,512]{2,1,0:T(8,128)(2,1)S(1)}, bf16[2,128,512]{2,1,0:T(8,128)(2,1)}, u32[]{:S(2)}) copy-start(bf16[2,128,512]{2,1,0:T(8,128)(2,1)} %copy-done.47) | copy-start | bytes 786436
  55.5 19.4 %collective-permute-start.6 = (bf16[2,128,512]{2,1,0:T(8,128)(2,1)S(1)}, bf16[2,128,512]{2,1,0:T(8,128)(2,1)S(1)}, u32[]{:S(2)}, u32[]{:S(2)}) collective-permute-start(bf16[2,128,512]{2,1,0:T(8,128)(2,1)S(1)} %fusion.100), channel_id=1, source_target_pairs={{0,128},{8,136},{16,144},{24,152},{32,160},{40,168},{48,176},{56,1... | collective-permute-start | bytes 786440 | tf_op jit(solution)/shard_map/ppermute | solution.py:16
  63.2 12.3 %copy-start.21 = (bf16[256,128]{1,0:T(8,128)(2,1)S(1)}, bf16[256,128]{1,0:T(8,128)(2,1)}, u32[]{:S(2)}) copy-start(bf16[256,128]{1,0:T(8,128)(2,1)} %copy-done.20) | copy-start | bytes 196612
  63.3 12.5 %copy-start.23 = (bf16[256,128]{1,0:T(8,128)(2,1)S(1)}, bf16[256,128]{1,0:T(8,128)(2,1)}, u32[]{:S(2)}) copy-start(bf16[256,128]{1,0:T(8,128)(2,1)} %copy-done.22) | copy-start | bytes 196612
  74.9 16.6 %copy-start.7 = (bf16[2,640,512]{2,1,0:T(8,128)(2,1)}, bf16[2,640,512]{2,1,0:T(8,128)(2,1)S(1)}, u32[]{:S(2)}) copy-start(bf16[2,640,512]{2,1,0:T(8,128)(2,1)S(1)} %constant_dynamic-update-slice_fusion) | copy-start | bytes 3932164
  79.5 13.3 %copy-start.33 = (bf16[2,128,640]{1,2,0:T(8,128)(2,1)}, bf16[2,128,640]{1,2,0:T(8,128)(2,1)S(1)}, u32[]{:S(2)}) copy-start(bf16[2,128,640]{1,2,0:T(8,128)(2,1)S(1)} %fusion.16) | copy-start | bytes 983044
  84.9 8.8 %copy-start.37 = (bf16[2,128,640]{1,2,0:T(8,128)(2,1)}, bf16[2,128,640]{1,2,0:T(8,128)(2,1)S(1)}, u32[]{:S(2)}) copy-start(bf16[2,128,640]{1,2,0:T(8,128)(2,1)S(1)} %fusion.17) | copy-start | bytes 983044
  85.2 9.6 %copy-start.51 = (bf16[2,128,384]{1,2,0:T(8,128)(2,1)}, bf16[2,128,384]{1,2,0:T(8,128)(2,1)S(1)}, u32[]{:S(2)}) copy-start(bf16[2,128,384]{1,2,0:T(8,128)(2,1)S(1)} %fusion.41) | copy-start | bytes 589828
  87.6 8.4 %copy-start.53 = (bf16[2,128,384]{1,2,0:T(8,128)(2,1)}, bf16[2,128,384]{1,2,0:T(8,128)(2,1)S(1)}, u32[]{:S(2)}) copy-start(bf16[2,128,384]{1,2,0:T(8,128)(2,1)S(1)} %fusion.42) | copy-start | bytes 589828
  87.9 7.1 %copy-start.35 = (bf16[2,128,640]{1,2,0:T(8,128)(2,1)}, bf16[2,128,640]{1,2,0:T(8,128)(2,1)S(1)}, u32[]{:S(2)}) copy-start(bf16[2,128,640]{1,2,0:T(8,128)(2,1)S(1)} %fusion.18) | copy-start | bytes 983044
  91.8 7.0 %copy-start.39 = (bf16[2,128,640]{1,2,0:T(8,128)(2,1)}, bf16[2,128,640]{1,2,0:T(8,128)(2,1)S(1)}, u32[]{:S(2)}) copy-start(bf16[2,128,640]{1,2,0:T(8,128)(2,1)S(1)} %fusion.19) | copy-start | bytes 983044
  103.2 3.2 %copy-start = (f32[2,384,512]{2,1,0:T(8,128)S(1)}, f32[2,384,512]{2,1,0:T(8,128)}, u32[]{:S(2)}) copy-start(f32[2,384,512]{2,1,0:T(8,128)} %copy.110) | copy-start | bytes 4718596
  103.3 25.7 %collective-permute-start.9 = (f32[2,128,512]{1,2,0:T(8,128)S(1)}, f32[2,128,512]{1,2,0:T(8,128)S(1)}, u32[]{:S(2)}, u32[]{:S(2)}) collective-permute-start(f32[2,128,512]{1,2,0:T(8,128)S(1)} %fusion.67), channel_id=1, source_target_pairs={{0,128},{8,136},{16,144},{24,152},{32,160},{40,168},{48,176},{56,1... | collective-permute-start | bytes 1572872 | tf_op jit(solution)/shard_map/ppermute | solution.py:16
  108.2 3.4 %copy-start.15 = (bf16[1,2,384,128]{3,2,1,0:T(8,128)(2,1)S(1)}, bf16[1,2,384,128]{3,2,1,0:T(8,128)(2,1)}, u32[]{:S(2)}) copy-start(bf16[1,2,384,128]{3,2,1,0:T(8,128)(2,1)} %copy-done.14) | copy-start | bytes 589828
  108.2 3.4 %copy-start.54 = (bf16[2,128,384]{1,2,0:T(8,128)(2,1)S(1)}, bf16[2,128,384]{1,2,0:T(8,128)(2,1)}, u32[]{:S(2)}) copy-start(bf16[2,128,384]{1,2,0:T(8,128)(2,1)} %copy-done.53) | copy-start | bytes 589828
  137.1 24.6 %copy-start.5 = (f32[2,128,512]{1,2,0:T(8,128)S(1)}, f32[2,128,512]{1,2,0:T(8,128)}, u32[]{:S(2)}) copy-start(f32[2,128,512]{1,2,0:T(8,128)} %copy.201) | copy-start | bytes 1572868
  137.1 24.6 %collective-permute-start.10 = (f32[2,128,512]{1,2,0:T(8,128)S(1)}, f32[2,128,512]{1,2,0:T(8,128)S(1)}, u32[]{:S(2)}, u32[]{:S(2)}) collective-permute-start(f32[2,128,512]{1,2,0:T(8,128)S(1)} %fusion.69), channel_id=1, source_target_pairs={{0,64},{8,72},{16,80},{24,88},{32,96},{40,104},{48,112},{56,120},{... | collective-permute-start | bytes 1572872 | tf_op jit(solution)/shard_map/ppermute | solution.py:16
  168.8 8.8 %copy-start.34 = (bf16[2,128,640]{1,2,0:T(8,128)(2,1)S(1)}, bf16[2,128,640]{1,2,0:T(8,128)(2,1)}, u32[]{:S(2)}) copy-start(bf16[2,128,640]{1,2,0:T(8,128)(2,1)} %copy-done.33) | copy-start | bytes 983044
  168.8 8.8 %copy-start.58 = (f32[2,128,128]{2,1,0:T(8,128)S(1)}, f32[2,128,128]{2,1,0:T(8,128)}, u32[]{:S(2)}) copy-start(f32[2,128,128]{2,1,0:T(8,128)} %fusion.129) | copy-start | bytes 393220
  168.8 10.7 %copy-start.38 = (bf16[2,128,640]{1,2,0:T(8,128)(2,1)S(1)}, bf16[2,128,640]{1,2,0:T(8,128)(2,1)}, u32[]{:S(2)}) copy-start(bf16[2,128,640]{1,2,0:T(8,128)(2,1)} %copy-done.37) | copy-start | bytes 983044
  168.8 10.7 %copy-start.59 = (f32[2,128,128]{2,1,0:T(8,128)S(1)}, f32[2,128,128]{2,1,0:T(8,128)}, u32[]{:S(2)}) copy-start(f32[2,128,128]{2,1,0:T(8,128)} %fusion.123) | copy-start | bytes 393220
  170.0 14.9 %copy-start.3 = (f32[2,128,512]{1,2,0:T(8,128)S(1)}, f32[2,128,512]{1,2,0:T(8,128)}, u32[]{:S(2)}) copy-start(f32[2,128,512]{1,2,0:T(8,128)} %copy.203) | copy-start | bytes 1572868
  170.0 14.9 %collective-permute-start.11 = (f32[2,128,512]{1,2,0:T(8,128)S(1)}, f32[2,128,512]{1,2,0:T(8,128)S(1)}, u32[]{:S(2)}, u32[]{:S(2)}) collective-permute-start(f32[2,128,512]{1,2,0:T(8,128)S(1)} %fusion.71), channel_id=1, source_target_pairs={{0,32},{8,40},{16,48},{24,56},{32,0},{40,8},{48,16},{56,24},{64,96... | collective-permute-start | bytes 1572872 | tf_op jit(solution)/shard_map/ppermute | solution.py:16
  171.0 47.4 %collective-permute-start.8 = (bf16[2,128,512]{2,1,0:T(8,128)(2,1)}, bf16[2,128,512]{2,1,0:T(8,128)(2,1)}, u32[]{:S(2)}, u32[]{:S(2)}) collective-permute-start(bf16[2,128,512]{2,1,0:T(8,128)(2,1)} %get-tuple-element.77), channel_id=1, source_target_pairs={{8,0},{16,8},{24,16},{32,24},{40,32},{48,40},{56,48},{64,56},{72,6... | collective-permute-start | bytes 786440 | tf_op jit(solution)/shard_map/ppermute | solution.py:35
  172.3 44.9 %collective-permute-start.7 = (bf16[2,128,512]{2,1,0:T(8,128)(2,1)}, bf16[2,128,512]{2,1,0:T(8,128)(2,1)}, u32[]{:S(2)}, u32[]{:S(2)}) collective-permute-start(bf16[2,128,512]{2,1,0:T(8,128)(2,1)} %get-tuple-element.78), channel_id=1, source_target_pairs={{0,8},{8,16},{16,24},{24,32},{32,40},{40,48},{48,56},{56,64},{64,7... | collective-permute-start | bytes 786440 | tf_op jit(solution)/shard_map/ppermute | solution.py:35
  191.9 3.3 %copy-start.40 = (bf16[2,128,640]{1,2,0:T(8,128)(2,1)S(1)}, bf16[2,128,640]{1,2,0:T(8,128)(2,1)}, u32[]{:S(2)}) copy-start(bf16[2,128,640]{1,2,0:T(8,128)(2,1)} %copy-done.39) | copy-start | bytes 983044
  192.0 3.3 %copy-start.60 = (f32[2,128,128]{2,1,0:T(8,128)S(1)}, f32[2,128,128]{2,1,0:T(8,128)}, u32[]{:S(2)}) copy-start(f32[2,128,128]{2,1,0:T(8,128)} %fusion.111) | copy-start | bytes 393220
  193.2 13.7 %copy-start.4 = (f32[2,128,512]{1,2,0:T(8,128)S(1)}, f32[2,128,512]{1,2,0:T(8,128)}, u32[]{:S(2)}) copy-start(f32[2,128,512]{1,2,0:T(8,128)} %copy.205) | copy-start | bytes 1572868
  193.2 13.7 %collective-permute-start.12 = (f32[2,128,512]{1,2,0:T(8,128)S(1)}, f32[2,128,512]{1,2,0:T(8,128)S(1)}, u32[]{:S(2)}, u32[]{:S(2)}) collective-permute-start(f32[2,128,512]{1,2,0:T(8,128)S(1)} %fusion.66), channel_id=1, source_target_pairs={{0,16},{8,24},{16,0},{24,8},{32,48},{40,56},{48,32},{56,40},{64,80... | collective-permute-start | bytes 1572872 | tf_op jit(solution)/shard_map/ppermute | solution.py:16
  215.1 11.2 %collective-permute-start.13 = (f32[2,128,512]{1,2,0:T(8,128)S(1)}, f32[2,128,512]{1,2,0:T(8,128)S(1)}, u32[]{:S(2)}, u32[]{:S(2)}) collective-permute-start(f32[2,128,512]{1,2,0:T(8,128)S(1)} %fusion.72), channel_id=1, source_target_pairs={{0,8},{8,0},{16,24},{24,16},{32,40},{40,32},{48,56},{56,48},{64,72... | collective-permute-start | bytes 1572872 | tf_op jit(solution)/shard_map/ppermute | solution.py:16
  217.2 9.1 %copy-start.2 = (f32[2,128,512]{1,2,0:T(8,128)S(1)}, f32[2,128,512]{1,2,0:T(8,128)}, u32[]{:S(2)}) copy-start(f32[2,128,512]{1,2,0:T(8,128)} %copy.207) | copy-start | bytes 1572868
  (36 other events, 51.9 us)
where the time goes:
time: 230 us; the launch traced here: 229 us
  waiting for transfers between devices  87.4 us (38%)
  local copies, waits for them, and re-layouts  49.2 us (21%)
  starting transfers between devices  34.8 us (15%)
  matrix products  30.7 us (13%)
  other arithmetic  24.6 us (11%)
    ppermute x10, waiting for transfers between devices, partner_2(): lax.ppermute(array, axis, [(i, i ^ 1 << distance) for i in range(lax.axis...  87.4 us
    ppermute x10, starting transfers between devices, partner_2(): lax.ppermute(array, axis, [(i, i ^ 1 << distance) for i in range(lax.axis...  22.4 us
    unnamed x152, local copies, waits for them, and re-layouts  19.5 us
    ppermute x2, starting transfers between devices, shifted(): lax.ppermute(value, axis, [(source, source + steps) for source in range(l...  6.54 us
    dot_general x4, matrix products, attend_head(): jnp.einsum('jbk,kd->jbd', far_sgrad, far_keys, preferred_element_type=jnp...  6.1 us
    slice x4, local copies, waits for them, and re-layouts, descend(): widened[:, :half_rows]  5.31 us
    mul x5, local copies, waits for them, and re-layouts, spread(): return jnp.repeat(gradients * ROOT_HALF, 2, axis=1)  5.28 us
    scatter-add x2, other arithmetic, per_device(): ext_blocks.at[:, offset_no:offset_no + block_count]  4.89 us
  transfers between devices with their start and end apart: 14, of which 10 were waited for; matrix products, arithmetic and copies ran while one was open for 20% of the time, Pallas kernels for 0%

commit v1 on v0

v1 whole, which is shorter than its diff:
```python
import functools
import math

import jax
import jax.numpy as jnp
from jax import lax
from jax.experimental import pallas as pl
from jax.experimental.pallas import tpu as pltpu
from jax.sharding import Mesh
from jax.sharding import PartitionSpec as P

D = 128
B = 128
NY = 4
NZ = 8
PIECE = 2 * B
PLANE = NY * PIECE
ROOT_HALF = 0.7071067811865476
SCALE = 1.0 / math.sqrt(D)
SCALE_LOG2E = SCALE * math.log2(math.e)
BF = jnp.bfloat16
F32 = jnp.float32

EXT = PLANE + 2 * B
AT1 = EXT
AT2 = AT1 + PLANE // 2
AT3 = AT2 + PLANE // 4
ROWS = AT3 + 3 * B

Z_SIDE = [(0, 6), (1, 7), (2, 4), (3, 5)]
TOP = Z_SIDE + [(b, a) for a, b in Z_SIDE]


def dot(a, b, ca=1, cb=0):
    return lax.dot_general(a, b, (((ca,), (cb,)), ((), ())), preferred_element_type=F32)


def pair_sum(rows):
    r = lax.broadcasted_iota(jnp.int32, (rows, 2 * rows), 0)
    c = lax.broadcasted_iota(jnp.int32, (rows, 2 * rows), 1)
    return (lax.shift_right_logical(c, 1) == r).astype(F32).astype(BF)


def repeat_matrix(rows, log):
    r = lax.broadcasted_iota(jnp.int32, (rows << log, rows), 0)
    c = lax.broadcasted_iota(jnp.int32, (rows << log, rows), 1)
    return (lax.shift_right_logical(r, log) == c).astype(F32).astype(BF)


def pool(matrix, x):
    return (dot(matrix, x) * ROOT_HALF).astype(BF)


def expand(matrix, x):
    high = x.astype(BF)
    low = (x - high.astype(F32)).astype(BF)
    return dot(matrix, high) + dot(matrix, low)


def piece_at(index):
    return pl.ds(pl.multiple_of(index * PIECE, PIECE), PIECE)


def head_at(index):
    return pl.ds(pl.multiple_of(index * D, D), D)


def pack_kernel(at_ref, left_ref, right_ref, *outs):
    y = at_ref[0]
    for d in range(NY):
        head = lax.rem(y + d, NY)
        outs[d][:, :D] = left_ref[:, head_at(head)]
        outs[d][:, D:] = right_ref[:, head_at(head)]


def pool_kernel(at_ref, k0, k1, k2, k3, all_ref, one_ref, two_ref, three_ref, low_ref, high_ref):
    y = at_ref[0]
    for d, ref in enumerate((k0, k1, k2, k3)):
        all_ref[piece_at(lax.rem(y - d + NY, NY)), :] = ref[...]
    matrix = pair_sum(B)
    for n in range(4):
        one_ref[n * B : (n + 1) * B] = pool(matrix, all_ref[n * PIECE : (n + 1) * PIECE])
    for n in range(2):
        two_ref[n * B : (n + 1) * B] = pool(matrix, one_ref[n * PIECE : (n + 1) * PIECE])
    three_ref[...] = pool(matrix, two_ref[...])
    low_ref[...] = all_ref[:B]
    high_ref[...] = all_ref[PLANE - B :]


def climb_kernel(which, at_ref, own_ref, other_ref, out_ref):
    bit = lax.rem(lax.shift_right_logical(at_ref[1], which), 2)
    half = B // 2
    matrix = pair_sum(half)
    out_ref[pl.ds(pl.multiple_of(bit * half, half), half), :] = pool(matrix, own_ref[...])
    out_ref[pl.ds(pl.multiple_of((1 - bit) * half, half), half), :] = pool(matrix, other_ref[...])


def attend_kernel(
    at_ref, kv, one, two, edge_low, edge_high, far3, far4, far5, q0, q1, q2, q3,
    og0, og1, og2, og3, g_low, g_high, g5, g4, g3, g_own, g_one, g_two,
    keys, vals, keys_t, vals_t, qc, og, grads,
):
    y = at_ref[0]
    z = at_ref[1]
    for d, ref in enumerate((q0, q1, q2, q3)):
        qc[piece_at(lax.rem(y - d + NY, NY)), :] = ref[...]
    at = 0
    for ref in (edge_low, kv, edge_high, one, two, far3, far4, far5):
        rows = ref.shape[0]
        keys[at : at + rows, :] = ref[:, :D]
        vals[at : at + rows, :] = ref[:, D:]
        at += rows
    for n in range(ROWS // B):
        cut = slice(n * B, (n + 1) * B)
        keys_t[:, cut] = keys[cut, :].T
        vals_t[:, cut] = vals[cut, :].T
    grads[...] = jnp.zeros_like(grads)

    second = lax.broadcasted_iota(jnp.int32, (B, PIECE), 1) >= B

    def visit(i, _):
        near = pl.multiple_of(i * PIECE, PIECE)
        pieces = (
            (near, 4 * B),
            (pl.multiple_of(AT1 + (i ^ 1) * B, B), B),
            (pl.multiple_of(AT2 + (lax.shift_right_logical(i, 1) ^ 1) * B, B), B),
            (AT3, 3 * B),
        )
        q = qc[piece_at(i), :D]
        c = qc[piece_at(i), D:]
        scores = [dot(keys[pl.ds(a, n), :], q, 1, 1) for a, n in pieces]
        no_low = (z == 0) & (i == 0)
        no_high = (z == NZ - 1) & (i == NY - 1)
        first = jnp.where(second | no_low, -jnp.inf, scores[0][:B])
        last = jnp.where(second, jnp.where(no_high, -jnp.inf, scores[0][3 * B :]), -jnp.inf)
        scores[0] = jnp.concatenate([first, scores[0][B : 3 * B], last], axis=0)
        top = functools.reduce(jnp.maximum, [jnp.max(s, axis=0, keepdims=True) for s in scores])
        raised = [jnp.exp2((s - top) * SCALE_LOG2E) for s in scores]
        total = functools.reduce(jnp.add, [jnp.sum(e, axis=0, keepdims=True) for e in raised])
        inverse = 1.0 / total
        probs = [e * inverse for e in raised]
        weights = [p.astype(BF) for p in probs]
        pgrads = [dot(vals[pl.ds(a, n), :], c, 1, 1) for a, n in pieces]
        row_dot = functools.reduce(
            jnp.add,
            [jnp.sum(w.astype(F32) * g, axis=0, keepdims=True) for w, g in zip(weights, pgrads)],
        )
        sgrads = [(p * (g - row_dot) * SCALE).astype(BF) for p, g in zip(probs, pgrads)]
        out_t = functools.reduce(
            jnp.add, [dot(vals_t[:, pl.ds(a, n)], w) for (a, n), w in zip(pieces, weights)]
        )
        qg_t = functools.reduce(
            jnp.add, [dot(keys_t[:, pl.ds(a, n)], s) for (a, n), s in zip(pieces, sgrads)]
        )
        og[piece_at(i), :D] = out_t.T.astype(BF)
        og[piece_at(i), D:] = qg_t.T.astype(BF)
        for (a, n), w, s in zip(pieces, weights, sgrads):
            grads[pl.ds(a, n), :D] += dot(s, q)
            grads[pl.ds(a, n), D:] += dot(w, c)
        return 0

    lax.fori_loop(0, NY, visit, 0)
    for d, ref in enumerate((og0, og1, og2, og3)):
        ref[...] = og[piece_at(lax.rem(y + d, NY)), :]
    g_low[...] = grads[:B].astype(BF)
    g_high[...] = grads[EXT - B : EXT].astype(BF)
    g3[...] = grads[AT3 : AT3 + B]
    g4[...] = grads[AT3 + B : AT3 + 2 * B]
    g5[...] = grads[AT3 + 2 * B :].astype(BF)
    g_own[...] = grads[B : EXT - B]
    g_one[...] = grads[AT1:AT2]
    g_two[...] = grads[AT2:AT3]


def local_kernel(own_ref, one_ref, two_ref, out_ref):
    matrix = repeat_matrix(B, 1)
    for n in range(2):
        two = expand(matrix, two_ref[n * B : (n + 1) * B] * ROOT_HALF)
        for m in range(2):
            k = 2 * n + m
            one = one_ref[k * B : (k + 1) * B] + two[m * B : (m + 1) * B]
            cut = slice(k * PIECE, (k + 1) * PIECE)
            out_ref[cut] = own_ref[cut] + expand(matrix, one * ROOT_HALF)


def halves(bit):
    half = B // 2
    own = pl.ds(pl.multiple_of(bit * half, half), half)
    other = pl.ds(pl.multiple_of((1 - bit) * half, half), half)
    return own, other


def descend_top_kernel(at_ref, back_ref, mine_ref, send_ref, keep_ref):
    own, other = halves(lax.rem(lax.shift_right_logical(at_ref[1], 1), 2))
    matrix = repeat_matrix(B // 2, 1)
    send_ref[...] = (mine_ref[...] + dot(matrix, back_ref[other, :]) * ROOT_HALF).astype(BF)
    keep_ref[...] = dot(matrix, back_ref[own, :]) * ROOT_HALF


def descend_kernel(at_ref, back_ref, kept_ref, mine_ref, send_ref, keep_ref):
    own, other = halves(lax.rem(at_ref[1], 2))
    matrix = repeat_matrix(B // 2, 1)

    def half_of(cut):
        return expand(matrix, (kept_ref[cut, :] + back_ref[cut, :].astype(F32)) * ROOT_HALF)

    send_ref[...] = (mine_ref[...] + half_of(other)).astype(BF)
    keep_ref[...] = half_of(own)


def final_kernel(at_ref, own_ref, low_ref, high_ref, back_ref, kept_ref, f0, f1, f2, f3, total):
    y = at_ref[0]
    matrix = repeat_matrix(B // NY, 3)
    up = (kept_ref[...] + back_ref[...].astype(F32)) * (ROOT_HALF * 0.5)
    for n in range(NY):
        rows = B // NY
        cut = slice(n * PIECE, (n + 1) * PIECE)
        total[cut] = own_ref[cut] + expand(matrix, up[n * rows : (n + 1) * rows])
    total[:B] += low_ref[...].astype(F32)
    total[PLANE - B :] += high_ref[...].astype(F32)
    for d, ref in enumerate((f0, f1, f2, f3)):
        ref[...] = total[piece_at(lax.rem(y + d, NY)), :].astype(BF)


def unpack_kernel(at_ref, r0, r1, r2, r3, left_ref, right_ref):
    y = at_ref[0]
    for d, ref in enumerate((r0, r1, r2, r3)):
        head = head_at(lax.rem(y - d + NY, NY))
        left_ref[:, head] = ref[:, :D]
        right_ref[:, head] = ref[:, D:]


def call(kernel, ins, outs, scratch=(), scalars=True, flops=10**6):
    vmem = pl.BlockSpec(memory_space=pltpu.VMEM)
    smem = pl.BlockSpec(memory_space=pltpu.SMEM)
    arrays = ins[1:] if scalars else ins
    size = sum(a.size * a.dtype.itemsize for a in arrays)
    size += sum(math.prod(s) * jnp.dtype(t).itemsize for s, t in outs)
    return pl.pallas_call(
        kernel,
        out_shape=[jax.ShapeDtypeStruct(s, t) for s, t in outs],
        in_specs=([smem] if scalars else []) + [vmem] * len(arrays),
        out_specs=[vmem] * len(outs),
        scratch_shapes=list(scratch),
        compiler_params=pltpu.CompilerParams(vmem_limit_bytes=40 * 2**20),
        cost_estimate=pl.CostEstimate(flops=flops, bytes_accessed=size, transcendentals=0),
    )(*ins)


def around_y(pieces):
    got = [pieces[0]]
    for d in range(1, NY):
        got.append(lax.ppermute(pieces[d], "y", [(i, (i + d) % NY) for i in range(NY)]))
    return got


def over_z(array, bit):
    return lax.ppermute(array, "z", [(i, i ^ (1 << bit)) for i in range(NZ)])


def up_z(array):
    return lax.ppermute(array, "z", [(i, i + 1) for i in range(NZ - 1)])


def down_z(array):
    return lax.ppermute(array, "z", [(i + 1, i) for i in range(NZ - 1)])


def per_device(queries, keys, values, cotangent):
    at = jnp.stack([lax.axis_index("y"), lax.axis_index("z")]).astype(jnp.int32)
    piece = ((PIECE, 2 * D), BF)
    level = ((B, 2 * D), BF)
    wide = ((B, 2 * D), F32)
    kv = around_y(call(pack_kernel, [at, keys, values], [piece] * NY))
    qc = around_y(call(pack_kernel, [at, queries, cotangent], [piece] * NY))
    kv_all, one, two, three, low, high = call(
        pool_kernel,
        [at, *kv],
        [((PLANE, 2 * D), BF), ((PLANE // 2, 2 * D), BF), ((PLANE // 4, 2 * D), BF), level, level, level],
    )
    far3 = over_z(three, 0)
    edge_low = up_z(high)
    edge_high = down_z(low)
    (four,) = call(functools.partial(climb_kernel, 0), [at, three, far3], [level])
    far4 = over_z(four, 1)
    (five,) = call(functools.partial(climb_kernel, 1), [at, four, far4], [level])
    far5 = lax.ppermute(five, "z", TOP)
    *og, g_low, g_high, g5, g4, g3, g_own, g_one, g_two = call(
        attend_kernel,
        [at, kv_all, one, two, edge_low, edge_high, far3, far4, far5, *qc],
        [piece] * NY
        + [level, level, level, wide, wide]
        + [((PLANE, 2 * D), F32), ((PLANE // 2, 2 * D), F32), ((PLANE // 4, 2 * D), F32)],
        scratch=[
            pltpu.VMEM((ROWS, D), BF),
            pltpu.VMEM((ROWS, D), BF),
            pltpu.VMEM((D, ROWS), BF),
            pltpu.VMEM((D, ROWS), BF),
            pltpu.VMEM((PLANE, 2 * D), BF),
            pltpu.VMEM((PLANE, 2 * D), BF),
            pltpu.VMEM((ROWS, 2 * D), F32),
        ],
        flops=2 * 10**9,
    )
    back5 = lax.ppermute(g5, "z", TOP)
    from_low = up_z(g_high)
    from_high = down_z(g_low)
    og = around_y(og)
    send4, keep4 = call(descend_top_kernel, [at, back5, g4], [level, wide])
    back4 = over_z(send4, 1)
    send3, keep3 = call(descend_kernel, [at, back4, keep4, g3], [level, wide])
    back3 = over_z(send3, 0)
    (own,) = call(
        local_kernel, [g_own, g_one, g_two], [((PLANE, 2 * D), F32)], scalars=False
    )
    final = call(
        final_kernel,
        [at, own, from_low, from_high, back3, keep3],
        [piece] * NY,
        scratch=[pltpu.VMEM((PLANE, 2 * D), F32)],
    )
    final = around_y(final)
    whole = ((PIECE, NY * D), BF)
    attended, grad_queries = call(unpack_kernel, [at, *og], [whole] * 2)
    grad_keys, grad_values = call(unpack_kernel, [at, *final], [whole] * 2)
    return attended, grad_queries, grad_keys, grad_values


def solution(mesh):
    seq, head, rep = mesh.devices.shape
    split = Mesh(mesh.devices.reshape(NZ, NY, head, rep), ("z", "y", "head", "rep"))
    spec = P(("rep", "z", "y"), "head")
    return jax.shard_map(
        per_device, mesh=split, in_specs=(spec,) * 4, out_specs=(spec,) * 4, check_vma=False
    )
```

time: 230 us -> 82.5 us (0.36)
  waiting for transfers between devices: 87.4 us -> 11.7 us
  local copies, waits for them, and re-layouts: 49.2 us -> 1.91 us
  matrix products: 30.7 us -> 0 us
  other arithmetic: 24.6 us -> 0.08 us
  Pallas kernels: 0 us -> 17.6 us
  starting transfers between devices: 34.8 us -> 50 us
    ppermute x14 -> x22, waiting for transfers between devices: 87.4 us -> 11.7 us  [the longest x12 6.7 us: around_y(): lax.ppermute(pieces[d], 'y', [(i, (i + d) % NY) for i in range(NY)])]
    dot_general x48 -> x0, matrix products: 30.7 us -> none  [the longest x4 6.1 us: attend_head(): jnp.einsum('jbk,kd->jbd', far_sgrad, far_keys, preferred_element_type=jnp...]
    unnamed x152 -> x8, local copies, waits for them, and re-layouts: 19.5 us -> 1.91 us
    pallas_call x0 -> x12, Pallas kernels: none -> 17.6 us  [call(): pl.pallas_call(kernel, out_shape=[jax.ShapeDtypeStruct(s, t) for s, t in...]
    ppermute x14 -> x22, starting transfers between devices: 34.8 us -> 50 us  [the longest x12 20 us: around_y(): lax.ppermute(pieces[d], 'y', [(i, (i + d) % NY) for i in range(NY)])]
    slice x12 -> x0, local copies, waits for them, and re-layouts: 10.1 us -> none  [the longest x4 5.31 us: descend(): widened[:, :half_rows]]
    scatter-add x4 -> x0, other arithmetic: 7.2 us -> none  [the longest x2 4.89 us: per_device(): ext_blocks.at[:, offset_no:offset_no + block_count]]
    mul x5 -> x0, local copies, waits for them, and re-layouts: 5.28 us -> none  [spread(): return jnp.repeat(gradients * ROOT_HALF, 2, axis=1)]
  transfers between devices with their start and end apart: 14 -> 22, of which waited for: 10 -> 7; matrix products, arithmetic and copies ran while one was open for 20% -> 0% of each run, Pallas kernels for 0% -> 8%
where the time goes in v1:
time: 82.5 us; the launch traced here: 82.1 us
  starting transfers between devices  50 us (61%)
  Pallas kernels  17.6 us (21%)
  waiting for transfers between devices  11.7 us (14%)
  local copies, waits for them, and re-layouts  1.91 us (2%)
    ppermute x12, starting transfers between devices, around_y(): lax.ppermute(pieces[d], 'y', [(i, (i + d) % NY) for i in range(NY)])  20 us
    pallas_call x12, Pallas kernels, call(): pl.pallas_call(kernel, out_shape=[jax.ShapeDtypeStruct(s, t) for s, t in...  17.6 us
    ppermute x4, starting transfers between devices, over_z(): return lax.ppermute(array, 'z', [(i, i ^ 1 << bit) for i in range(NZ)])  10.1 us
    ppermute x2, starting transfers between devices, up_z(): return lax.ppermute(array, 'z', [(i, i + 1) for i in range(NZ - 1)])  7.16 us
    ppermute x12, waiting for transfers between devices, around_y(): lax.ppermute(pieces[d], 'y', [(i, (i + d) % NY) for i in range(NY)])  6.7 us
    ppermute x1, starting transfers between devices, per_device(): far5 = lax.ppermute(five, 'z', TOP)  5.3 us
    ppermute x1, starting transfers between devices, per_device(): back5 = lax.ppermute(g5, 'z', TOP)  4.84 us
    ppermute x2, starting transfers between devices, down_z(): return lax.ppermute(array, 'z', [(i + 1, i) for i in range(NZ - 1)])  2.58 us
  transfers between devices with their start and end apart: 22, of which 7 were waited for; matrix products, arithmetic and copies ran while one was open for 0% of the time, Pallas kernels for 8%

profile of v1, /device:TPU:6, one launch (start us, length us, event | category | flops | bytes accessed | tf_op | source)
XLA Modules:
  0.0 82.1 jit_solution(11253644122901679551)
XLA Ops:
  0.6 0.1 pad_add_fusion.at_ref
  0.7 0.9 %copy-done = bf16[256,512]{1,0:T(8,128)(2,1)S(1)} copy-done((bf16[256,512]{1,0:T(8,128)(2,1)S(1)}, bf16[256,512]{1,0:T(8,128)(2,1)}, u32[]{:S(2)}) %copy-start) | copy-done | bytes 262168
  1.7 0.9 %copy-done.1 = bf16[256,512]{1,0:T(8,128)(2,1)S(1)} copy-done((bf16[256,512]{1,0:T(8,128)(2,1)S(1)}, bf16[256,512]{1,0:T(8,128)(2,1)}, u32[]{:S(2)}) %copy-start.1) | copy-done | bytes 262168
  2.6 0.6 shard_map.75
  3.3 1.7 %collective-permute-start = (bf16[256,256]{1,0:T(8,128)(2,1)S(1)}, bf16[256,256]{1,0:T(8,128)(2,1)S(1)}, u32[]{:S(2)}, u32[]{:S(2)}) collective-permute-start(bf16[256,256]{1,0:T(8,128)(2,1)S(1)} %get-tuple-element.43), channel_id=1, source_target_pairs={{0,8},{8,16},{16,24},{24,0},{1,9},{9,17},{17,25},{25,1},{2,10},{10... | collective-permute-start | bytes 393224 | tf_op jit(solution)/shard_map/ppermute | solution.py:253
  4.9 2.9 %collective-permute-start.1 = (bf16[256,256]{1,0:T(8,128)(2,1)S(1)}, bf16[256,256]{1,0:T(8,128)(2,1)S(1)}, u32[]{:S(2)}, u32[]{:S(2)}) collective-permute-start(bf16[256,256]{1,0:T(8,128)(2,1)S(1)} %get-tuple-element.44), channel_id=1, source_target_pairs={{0,16},{8,24},{16,0},{24,8},{1,17},{9,25},{17,1},{25,9},{2,18},{10... | collective-permute-start | bytes 393224 | tf_op jit(solution)/shard_map/ppermute | solution.py:253
  7.8 1.3 %collective-permute-start.2 = (bf16[256,256]{1,0:T(8,128)(2,1)S(1)}, bf16[256,256]{1,0:T(8,128)(2,1)S(1)}, u32[]{:S(2)}, u32[]{:S(2)}) collective-permute-start(bf16[256,256]{1,0:T(8,128)(2,1)S(1)} %get-tuple-element.45), channel_id=1, source_target_pairs={{0,24},{8,0},{16,8},{24,16},{1,25},{9,1},{17,9},{25,17},{2,26},{10... | collective-permute-start | bytes 393224 | tf_op jit(solution)/shard_map/ppermute | solution.py:253
  9.2 0.7 collective-permute-done.k1
  9.9 4.0 %collective-permute-done.1.k2 = bf16[256,256]{1,0:T(8,128)(2,1)S(1)} collective-permute-done((bf16[256,256]{1,0:T(8,128)(2,1)S(1)}, bf16[256,256]{1,0:T(8,128)(2,1)S(1)}, u32[]{:S(2)}, u32[]{:S(2)}) %collective-permute-start.1) | collective-permute-done | bytes 131104 | tf_op jit(solution)/shard_map/ppermute | solution.py:253
  13.8 0.0 collective-permute-done.2.k3
  13.8 1.1 %shard_map.76 = (bf16[1024,256]{1,0:T(8,128)(2,1)S(1)}, bf16[512,256]{1,0:T(8,128)(2,1)S(1)}, bf16[256,256]{1,0:T(8,128)(2,1)S(1)}, bf16[128,256]{1,0:T(8,128)(2...) custom-call(s32[2]{0:T(128)S(1)} %pad_add_fusion.at_ref, bf16[256,256]{1,0:T(8,128)(2,1)S(1)} %get-tuple-element.42.k0, ...), custom_call_target="tpu_custom_call" | custom-call | flops 1000000 | bytes 1638400 | tf_op jit(solution)/shard_map/pallas_call | solution.py:239
  15.0 2.0 %collective-permute-start.5 = (bf16[128,256]{1,0:T(8,128)(2,1)S(1)}, bf16[128,256]{1,0:T(8,128)(2,1)S(1)}, u32[]{:S(2)}, u32[]{:S(2)}) collective-permute-start(bf16[128,256]{1,0:T(8,128)(2,1)S(1)} %get-tuple-element.51.own_ref), channel_id=1, source_target_pairs={{0,32},{32,0},{64,96},{96,64},{128,160},{160,128},{192,224},{224,1... | collective-permute-start | bytes 196616 | tf_op jit(solution)/shard_map/ppermute | solution.py:258
  17.0 0.6 shard_map.79
  17.6 1.3 %collective-permute-start.8 = (bf16[256,256]{1,0:T(8,128)(2,1)S(1)}, bf16[256,256]{1,0:T(8,128)(2,1)S(1)}, u32[]{:S(2)}, u32[]{:S(2)}) collective-permute-start(bf16[256,256]{1,0:T(8,128)(2,1)S(1)} %get-tuple-element.53), channel_id=1, source_target_pairs={{0,8},{8,16},{16,24},{24,0},{1,9},{9,17},{17,25},{25,1},{2,10},{10... | collective-permute-start | bytes 393224 | tf_op jit(solution)/shard_map/ppermute | solution.py:253
  18.9 0.4 collective-permute-done.5.other_ref.far3
  19.3 0.7 shard_map.77.own_ref
  20.0 3.4 %collective-permute-start.6 = (bf16[128,256]{1,0:T(8,128)(2,1)S(1)}, bf16[128,256]{1,0:T(8,128)(2,1)S(1)}, u32[]{:S(2)}, u32[]{:S(2)}) collective-permute-start(bf16[128,256]{1,0:T(8,128)(2,1)S(1)} %shard_map.77.own_ref), channel_id=1, source_target_pairs={{0,64},{32,96},{64,0},{96,32},{128,192},{160,224},{192,128},{224,1... | collective-permute-start | bytes 196616 | tf_op jit(solution)/shard_map/ppermute | solution.py:258
  23.4 2.6 %collective-permute-start.9 = (bf16[256,256]{1,0:T(8,128)(2,1)S(1)}, bf16[256,256]{1,0:T(8,128)(2,1)S(1)}, u32[]{:S(2)}, u32[]{:S(2)}) collective-permute-start(bf16[256,256]{1,0:T(8,128)(2,1)S(1)} %get-tuple-element.54), channel_id=1, source_target_pairs={{0,16},{8,24},{16,0},{24,8},{1,17},{9,25},{17,1},{25,9},{2,18},{10... | collective-permute-start | bytes 393224 | tf_op jit(solution)/shard_map/ppermute | solution.py:253
  25.9 1.3 %collective-permute-start.10 = (bf16[256,256]{1,0:T(8,128)(2,1)S(1)}, bf16[256,256]{1,0:T(8,128)(2,1)S(1)}, u32[]{:S(2)}, u32[]{:S(2)}) collective-permute-start(bf16[256,256]{1,0:T(8,128)(2,1)S(1)} %get-tuple-element.55), channel_id=1, source_target_pairs={{0,24},{8,0},{16,8},{24,16},{1,25},{9,1},{17,9},{25,17},{2,26},{10... | collective-permute-start | bytes 393224 | tf_op jit(solution)/shard_map/ppermute | solution.py:253
  27.3 3.8 %collective-permute-start.3 = (bf16[128,256]{1,0:T(8,128)(2,1)S(1)}, bf16[128,256]{1,0:T(8,128)(2,1)S(1)}, u32[]{:S(2)}, u32[]{:S(2)}) collective-permute-start(bf16[128,256]{1,0:T(8,128)(2,1)S(1)} %get-tuple-element.49), channel_id=1, source_target_pairs={{0,32},{32,64},{64,96},{96,128},{128,160},{160,192},{192,224},{1,3... | collective-permute-start | bytes 196616 | tf_op jit(solution)/shard_map/ppermute | solution.py:262
  31.1 1.3 %collective-permute-start.4 = (bf16[128,256]{1,0:T(8,128)(2,1)S(1)}, bf16[128,256]{1,0:T(8,128)(2,1)S(1)}, u32[]{:S(2)}, u32[]{:S(2)}) collective-permute-start(bf16[128,256]{1,0:T(8,128)(2,1)S(1)} %get-tuple-element.50), channel_id=1, source_target_pairs={{32,0},{64,32},{96,64},{128,96},{160,128},{192,160},{224,192},{33,... | collective-permute-start | bytes 196616 | tf_op jit(solution)/shard_map/ppermute | solution.py:266
  32.4 0.7 shard_map.78
  33.1 5.3 %collective-permute-start.7 = (bf16[128,256]{1,0:T(8,128)(2,1)S(1)}, bf16[128,256]{1,0:T(8,128)(2,1)S(1)}, u32[]{:S(2)}, u32[]{:S(2)}) collective-permute-start(bf16[128,256]{1,0:T(8,128)(2,1)S(1)} %shard_map.78), channel_id=1, source_target_pairs={{0,192},{32,224},{64,128},{96,160},{192,0},{224,32},{128,64},{160,... | collective-permute-start | bytes 196616 | tf_op jit(solution)/shard_map/ppermute | solution.py:287
  38.4 0.0 collective-permute-done.9.q2
  38.4 0.0 collective-permute-done.10.q3
  38.4 0.0 collective-permute-done.3.edge_low
  38.4 2.3 %collective-permute-done.7.far5 = bf16[128,256]{1,0:T(8,128)(2,1)S(1)} collective-permute-done((bf16[128,256]{1,0:T(8,128)(2,1)S(1)}, bf16[128,256]{1,0:T(8,128)(2,1)S(1)}, u32[]{:S(2)}, u32[]{:S(2)}) %collective-permute-start.7) | collective-permute-done | bytes 65568 | tf_op jit(solution)/shard_map/ppermute | solution.py:287
  40.7 7.4 %shard_map.80 = (bf16[256,256]{1,0:T(8,128)(2,1)S(1)}, bf16[256,256]{1,0:T(8,128)(2,1)S(1)}, bf16[256,256]{1,0:T(8,128)(2,1)S(1)}, bf16[256,256]{1,0:T(8,128)(2,...) custom-call(s32[2]{0:T(128)S(1)} %pad_add_fusion.at_ref, ...), custom_call_target="tpu_custom_call" | custom-call | flops 2000000000 | bytes 4587520 | tf_op jit(solution)/shard_map/pallas_call | solution.py:239
  48.2 4.8 %collective-permute-start.16 = (bf16[128,256]{1,0:T(8,128)(2,1)S(1)}, bf16[128,256]{1,0:T(8,128)(2,1)S(1)}, u32[]{:S(2)}, u32[]{:S(2)}) collective-permute-start(bf16[128,256]{1,0:T(8,128)(2,1)S(1)} %get-tuple-element.67), channel_id=1, source_target_pairs={{0,192},{32,224},{64,128},{96,160},{192,0},{224,32},{128,64},{160,... | collective-permute-start | bytes 196616 | tf_op jit(solution)/shard_map/ppermute | solution.py:305
  53.0 2.4 %collective-permute-done.16.back_ref = bf16[128,256]{1,0:T(8,128)(2,1)S(1)} collective-permute-done((bf16[128,256]{1,0:T(8,128)(2,1)S(1)}, bf16[128,256]{1,0:T(8,128)(2,1)S(1)}, u32[]{:S(2)}, u32[]{:S(2)}) %collective-permute-start.16) | collective-permute-done | bytes 65568 | tf_op jit(solution)/shard_map/ppermute | solution.py:305
  55.4 0.7 shard_map.83
  56.1 2.0 %collective-permute-start.17 = (bf16[128,256]{1,0:T(8,128)(2,1)S(1)}, bf16[128,256]{1,0:T(8,128)(2,1)S(1)}, u32[]{:S(2)}, u32[]{:S(2)}) collective-permute-start(bf16[128,256]{1,0:T(8,128)(2,1)S(1)} %get-tuple-element.69), channel_id=1, source_target_pairs={{0,64},{32,96},{64,0},{96,32},{128,192},{160,224},{192,128},{224,1... | collective-permute-start | bytes 196616 | tf_op jit(solution)/shard_map/ppermute | solution.py:258
  58.1 0.6 collective-permute-start.11
  58.7 3.3 %collective-permute-start.14 = (bf16[128,256]{1,0:T(8,128)(2,1)S(1)}, bf16[128,256]{1,0:T(8,128)(2,1)S(1)}, u32[]{:S(2)}, u32[]{:S(2)}) collective-permute-start(bf16[128,256]{1,0:T(8,128)(2,1)S(1)} %get-tuple-element.65), channel_id=1, source_target_pairs={{0,32},{32,64},{64,96},{96,128},{128,160},{160,192},{192,224},{1,3... | collective-permute-start | bytes 196616 | tf_op jit(solution)/shard_map/ppermute | solution.py:262
  62.1 1.3 %collective-permute-start.15 = (bf16[128,256]{1,0:T(8,128)(2,1)S(1)}, bf16[128,256]{1,0:T(8,128)(2,1)S(1)}, u32[]{:S(2)}, u32[]{:S(2)}) collective-permute-start(bf16[128,256]{1,0:T(8,128)(2,1)S(1)} %get-tuple-element.66), channel_id=1, source_target_pairs={{32,0},{64,32},{96,64},{128,96},{160,128},{192,160},{224,192},{33,... | collective-permute-start | bytes 196616 | tf_op jit(solution)/shard_map/ppermute | solution.py:266
  63.4 0.8 shard_map.84
  64.2 2.7 %collective-permute-start.18 = (bf16[128,256]{1,0:T(8,128)(2,1)S(1)}, bf16[128,256]{1,0:T(8,128)(2,1)S(1)}, u32[]{:S(2)}, u32[]{:S(2)}) collective-permute-start(bf16[128,256]{1,0:T(8,128)(2,1)S(1)} %get-tuple-element.72), channel_id=1, source_target_pairs={{0,32},{32,0},{64,96},{96,64},{128,160},{160,128},{192,224},{224,1... | collective-permute-start | bytes 196616 | tf_op jit(solution)/shard_map/ppermute | solution.py:258
  66.9 1.0 %collective-permute-start.12 = (bf16[256,256]{1,0:T(8,128)(2,1)S(1)}, bf16[256,256]{1,0:T(8,128)(2,1)S(1)}, u32[]{:S(2)}, u32[]{:S(2)}) collective-permute-start(bf16[256,256]{1,0:T(8,128)(2,1)S(1)} %get-tuple-element.58), channel_id=1, source_target_pairs={{0,16},{8,24},{16,0},{24,8},{1,17},{9,25},{17,1},{25,9},{2,18},{10... | collective-permute-start | bytes 393224 | tf_op jit(solution)/shard_map/ppermute | solution.py:253
  67.9 0.9 %shard_map.82.own_ref = f32[1024,256]{1,0:T(8,128)S(1)} custom-call(f32[1024,256]{1,0:T(8,128)S(1)} %get-tuple-element.62.own_ref, f32[512,256]{1,0:T(8,128)S(1)} %get-tuple-element.63.one_ref, f32[256,256]{1,0:T(8,128)S(1)} %get-tuple-element.64.two_ref), custom_call_target="tpu_custom_call" | custom-call | flops 1000000 | bytes 2883584 | tf_op jit(solution)/shard_map/pallas_call | solution.py:239
  68.8 2.2 %collective-permute-start.13 = (bf16[256,256]{1,0:T(8,128)(2,1)S(1)}, bf16[256,256]{1,0:T(8,128)(2,1)S(1)}, u32[]{:S(2)}, u32[]{:S(2)}) collective-permute-start(bf16[256,256]{1,0:T(8,128)(2,1)S(1)} %get-tuple-element.59), channel_id=1, source_target_pairs={{0,24},{8,0},{16,8},{24,16},{1,25},{9,1},{17,9},{25,17},{2,26},{10... | collective-permute-start | bytes 393224 | tf_op jit(solution)/shard_map/ppermute | solution.py:253
  71.0 1.1 %shard_map.85 = (bf16[256,256]{1,0:T(8,128)(2,1)S(1)}, bf16[256,256]{1,0:T(8,128)(2,1)S(1)}, bf16[256,256]{1,0:T(8,128)(2,1)S(1)}, bf16[256,256]{1,0:T(8,128)(2,1)S(1)}) custom-call(s32[2]{0:T(128)S(1)} %pad_add_fusion.at_ref, f32[1024,256]{1,0:T(8,128)S(1)} %shard_map.82.own_ref, bf16[128,256]{1,0:T(8,128)(2,1)S(1)} %collective-permute-done.14.low_ref, ...), custom_call_target="tpu_custom_call" | custom-call | flops 1000000 | bytes 1900544 | tf_op jit(solution)/shard_map/pallas_call | solution.py:239
  72.2 0.4 collective-permute-start.19
  72.6 2.1 %collective-permute-start.20 = (bf16[256,256]{1,0:T(8,128)(2,1)S(1)}, bf16[256,256]{1,0:T(8,128)(2,1)S(1)}, u32[]{:S(2)}, u32[]{:S(2)}) collective-permute-start(bf16[256,256]{1,0:T(8,128)(2,1)S(1)} %get-tuple-element.76), channel_id=1, source_target_pairs={{0,16},{8,24},{16,0},{24,8},{1,17},{9,25},{17,1},{25,9},{2,18},{10... | collective-permute-start | bytes 393224 | tf_op jit(solution)/shard_map/ppermute | solution.py:253
  74.7 2.5 %collective-permute-start.21 = (bf16[256,256]{1,0:T(8,128)(2,1)S(1)}, bf16[256,256]{1,0:T(8,128)(2,1)S(1)}, u32[]{:S(2)}, u32[]{:S(2)}) collective-permute-start(bf16[256,256]{1,0:T(8,128)(2,1)S(1)} %get-tuple-element.77), channel_id=1, source_target_pairs={{0,24},{8,0},{16,8},{24,16},{1,25},{9,1},{17,9},{25,17},{2,26},{10... | collective-permute-start | bytes 393224 | tf_op jit(solution)/shard_map/ppermute | solution.py:253
  77.2 1.4 %shard_map.81 = (bf16[256,512]{1,0:T(8,128)(2,1)}, bf16[256,512]{1,0:T(8,128)(2,1)}) custom-call(s32[2]{0:T(128)S(1)} %pad_add_fusion.at_ref, bf16[256,256]{1,0:T(8,128)(2,1)S(1)} %get-tuple-element.56.r0, bf16[256,256]{1,0:T(8,128)(2,1)S(1)} %collective-permute-done.11.r1, bf16[256,256]{1,0:T(8,128)(2,1)S(1)} %collective-permute-done.12.r2, ...), custom_call_target="tpu_custom_call" | custom-call | flops 1000000 | bytes 1048576 | tf_op jit(solution)/shard_map/pallas_call | solution.py:239
  78.7 1.2 %collective-permute-done.19.r1 = bf16[256,256]{1,0:T(8,128)(2,1)S(1)} collective-permute-done((bf16[256,256]{1,0:T(8,128)(2,1)S(1)}, bf16[256,256]{1,0:T(8,128)(2,1)S(1)}, u32[]{:S(2)}, u32[]{:S(2)}) %collective-permute-start.19) | collective-permute-done | bytes 131104 | tf_op jit(solution)/shard_map/ppermute | solution.py:253
  79.8 0.9 %collective-permute-done.21.r3 = bf16[256,256]{1,0:T(8,128)(2,1)S(1)} collective-permute-done((bf16[256,256]{1,0:T(8,128)(2,1)S(1)}, bf16[256,256]{1,0:T(8,128)(2,1)S(1)}, u32[]{:S(2)}, u32[]{:S(2)}) %collective-permute-start.21) | collective-permute-done | bytes 131104 | tf_op jit(solution)/shard_map/ppermute | solution.py:253
  80.7 1.4 %shard_map.86 = (bf16[256,512]{1,0:T(8,128)(2,1)}, bf16[256,512]{1,0:T(8,128)(2,1)}) custom-call(s32[2]{0:T(128)S(1)} %pad_add_fusion.at_ref, bf16[256,256]{1,0:T(8,128)(2,1)S(1)} %get-tuple-element.74.r0, bf16[256,256]{1,0:T(8,128)(2,1)S(1)} %collective-permute-done.19.r1, bf16[256,256]{1,0:T(8,128)(2,1)S(1)} %collective-permute-done.20.r2, ...), custom_call_target="tpu_custom_call" | custom-call | flops 1000000 | bytes 1048576 | tf_op jit(solution)/shard_map/pallas_call | solution.py:239
  (17 shorter events, 0.0 us)
Async XLA Ops:
  0.7 1.0 %copy-start = (bf16[256,512]{1,0:T(8,128)(2,1)S(1)}, bf16[256,512]{1,0:T(8,128)(2,1)}, u32[]{:S(2)}) copy-start(bf16[256,512]{1,0:T(8,128)(2,1)} %left_ref.2) | copy-start | bytes 786436
  1.7 0.9 %copy-start.1 = (bf16[256,512]{1,0:T(8,128)(2,1)S(1)}, bf16[256,512]{1,0:T(8,128)(2,1)}, u32[]{:S(2)}) copy-start(bf16[256,512]{1,0:T(8,128)(2,1)} %right_ref.2) | copy-start | bytes 786436
  3.3 6.6 %collective-permute-start = (bf16[256,256]{1,0:T(8,128)(2,1)S(1)}, bf16[256,256]{1,0:T(8,128)(2,1)S(1)}, u32[]{:S(2)}, u32[]{:S(2)}) collective-permute-start(bf16[256,256]{1,0:T(8,128)(2,1)S(1)} %get-tuple-element.43), channel_id=1, source_target_pairs={{0,8},{8,16},{16,24},{24,0},{1,9},{9,17},{17,25},{25,1},{2,10},{10... | collective-permute-start | bytes 393224 | tf_op jit(solution)/shard_map/ppermute | solution.py:253
  4.9 8.9 %collective-permute-start.1 = (bf16[256,256]{1,0:T(8,128)(2,1)S(1)}, bf16[256,256]{1,0:T(8,128)(2,1)S(1)}, u32[]{:S(2)}, u32[]{:S(2)}) collective-permute-start(bf16[256,256]{1,0:T(8,128)(2,1)S(1)} %get-tuple-element.44), channel_id=1, source_target_pairs={{0,16},{8,24},{16,0},{24,8},{1,17},{9,25},{17,1},{25,9},{2,18},{10... | collective-permute-start | bytes 393224 | tf_op jit(solution)/shard_map/ppermute | solution.py:253
  7.8 6.0 %collective-permute-start.2 = (bf16[256,256]{1,0:T(8,128)(2,1)S(1)}, bf16[256,256]{1,0:T(8,128)(2,1)S(1)}, u32[]{:S(2)}, u32[]{:S(2)}) collective-permute-start(bf16[256,256]{1,0:T(8,128)(2,1)S(1)} %get-tuple-element.45), channel_id=1, source_target_pairs={{0,24},{8,0},{16,8},{24,16},{1,25},{9,1},{17,9},{25,17},{2,26},{10... | collective-permute-start | bytes 393224 | tf_op jit(solution)/shard_map/ppermute | solution.py:253
  13.8 3.1 %copy-start.2 = (bf16[256,512]{1,0:T(8,128)(2,1)S(1)}, bf16[256,512]{1,0:T(8,128)(2,1)}, u32[]{:S(2)}) copy-start(bf16[256,512]{1,0:T(8,128)(2,1)} %left_ref.3) | copy-start | bytes 786436
  13.8 3.1 %copy-start.3 = (bf16[256,512]{1,0:T(8,128)(2,1)S(1)}, bf16[256,512]{1,0:T(8,128)(2,1)}, u32[]{:S(2)}) copy-start(bf16[256,512]{1,0:T(8,128)(2,1)} %right_ref.3) | copy-start | bytes 786436
  15.0 4.4 %collective-permute-start.5 = (bf16[128,256]{1,0:T(8,128)(2,1)S(1)}, bf16[128,256]{1,0:T(8,128)(2,1)S(1)}, u32[]{:S(2)}, u32[]{:S(2)}) collective-permute-start(bf16[128,256]{1,0:T(8,128)(2,1)S(1)} %get-tuple-element.51.own_ref), channel_id=1, source_target_pairs={{0,32},{32,0},{64,96},{96,64},{128,160},{160,128},{192,224},{224,1... | collective-permute-start | bytes 196616 | tf_op jit(solution)/shard_map/ppermute | solution.py:258
  17.6 15.5 %collective-permute-start.8 = (bf16[256,256]{1,0:T(8,128)(2,1)S(1)}, bf16[256,256]{1,0:T(8,128)(2,1)S(1)}, u32[]{:S(2)}, u32[]{:S(2)}) collective-permute-start(bf16[256,256]{1,0:T(8,128)(2,1)S(1)} %get-tuple-element.53), channel_id=1, source_target_pairs={{0,8},{8,16},{16,24},{24,0},{1,9},{9,17},{17,25},{25,1},{2,10},{10... | collective-permute-start | bytes 393224 | tf_op jit(solution)/shard_map/ppermute | solution.py:253
  20.0 11.1 %collective-permute-start.6 = (bf16[128,256]{1,0:T(8,128)(2,1)S(1)}, bf16[128,256]{1,0:T(8,128)(2,1)S(1)}, u32[]{:S(2)}, u32[]{:S(2)}) collective-permute-start(bf16[128,256]{1,0:T(8,128)(2,1)S(1)} %shard_map.77.own_ref), channel_id=1, source_target_pairs={{0,64},{32,96},{64,0},{96,32},{128,192},{160,224},{192,128},{224,1... | collective-permute-start | bytes 196616 | tf_op jit(solution)/shard_map/ppermute | solution.py:258
  23.4 15.0 %collective-permute-start.9 = (bf16[256,256]{1,0:T(8,128)(2,1)S(1)}, bf16[256,256]{1,0:T(8,128)(2,1)S(1)}, u32[]{:S(2)}, u32[]{:S(2)}) collective-permute-start(bf16[256,256]{1,0:T(8,128)(2,1)S(1)} %get-tuple-element.54), channel_id=1, source_target_pairs={{0,16},{8,24},{16,0},{24,8},{1,17},{9,25},{17,1},{25,9},{2,18},{10... | collective-permute-start | bytes 393224 | tf_op jit(solution)/shard_map/ppermute | solution.py:253
  25.9 12.5 %collective-permute-start.10 = (bf16[256,256]{1,0:T(8,128)(2,1)S(1)}, bf16[256,256]{1,0:T(8,128)(2,1)S(1)}, u32[]{:S(2)}, u32[]{:S(2)}) collective-permute-start(bf16[256,256]{1,0:T(8,128)(2,1)S(1)} %get-tuple-element.55), channel_id=1, source_target_pairs={{0,24},{8,0},{16,8},{24,16},{1,25},{9,1},{17,9},{25,17},{2,26},{10... | collective-permute-start | bytes 393224 | tf_op jit(solution)/shard_map/ppermute | solution.py:253
  27.3 11.1 %collective-permute-start.3 = (bf16[128,256]{1,0:T(8,128)(2,1)S(1)}, bf16[128,256]{1,0:T(8,128)(2,1)S(1)}, u32[]{:S(2)}, u32[]{:S(2)}) collective-permute-start(bf16[128,256]{1,0:T(8,128)(2,1)S(1)} %get-tuple-element.49), channel_id=1, source_target_pairs={{0,32},{32,64},{64,96},{96,128},{128,160},{160,192},{192,224},{1,3... | collective-permute-start | bytes 196616 | tf_op jit(solution)/shard_map/ppermute | solution.py:262
  31.1 7.3 %collective-permute-start.4 = (bf16[128,256]{1,0:T(8,128)(2,1)S(1)}, bf16[128,256]{1,0:T(8,128)(2,1)S(1)}, u32[]{:S(2)}, u32[]{:S(2)}) collective-permute-start(bf16[128,256]{1,0:T(8,128)(2,1)S(1)} %get-tuple-element.50), channel_id=1, source_target_pairs={{32,0},{64,32},{96,64},{128,96},{160,128},{192,160},{224,192},{33,... | collective-permute-start | bytes 196616 | tf_op jit(solution)/shard_map/ppermute | solution.py:266
  33.1 7.6 %collective-permute-start.7 = (bf16[128,256]{1,0:T(8,128)(2,1)S(1)}, bf16[128,256]{1,0:T(8,128)(2,1)S(1)}, u32[]{:S(2)}, u32[]{:S(2)}) collective-permute-start(bf16[128,256]{1,0:T(8,128)(2,1)S(1)} %shard_map.78), channel_id=1, source_target_pairs={{0,192},{32,224},{64,128},{96,160},{192,0},{224,32},{128,64},{160,... | collective-permute-start | bytes 196616 | tf_op jit(solution)/shard_map/ppermute | solution.py:287
  48.2 7.2 %collective-permute-start.16 = (bf16[128,256]{1,0:T(8,128)(2,1)S(1)}, bf16[128,256]{1,0:T(8,128)(2,1)S(1)}, u32[]{:S(2)}, u32[]{:S(2)}) collective-permute-start(bf16[128,256]{1,0:T(8,128)(2,1)S(1)} %get-tuple-element.67), channel_id=1, source_target_pairs={{0,192},{32,224},{64,128},{96,160},{192,0},{224,32},{128,64},{160,... | collective-permute-start | bytes 196616 | tf_op jit(solution)/shard_map/ppermute | solution.py:305
  56.1 7.3 %collective-permute-start.17 = (bf16[128,256]{1,0:T(8,128)(2,1)S(1)}, bf16[128,256]{1,0:T(8,128)(2,1)S(1)}, u32[]{:S(2)}, u32[]{:S(2)}) collective-permute-start(bf16[128,256]{1,0:T(8,128)(2,1)S(1)} %get-tuple-element.69), channel_id=1, source_target_pairs={{0,64},{32,96},{64,0},{96,32},{128,192},{160,224},{192,128},{224,1... | collective-permute-start | bytes 196616 | tf_op jit(solution)/shard_map/ppermute | solution.py:258
  58.1 16.6 %collective-permute-start.11 = (bf16[256,256]{1,0:T(8,128)(2,1)S(1)}, bf16[256,256]{1,0:T(8,128)(2,1)S(1)}, u32[]{:S(2)}, u32[]{:S(2)}) collective-permute-start(bf16[256,256]{1,0:T(8,128)(2,1)S(1)} %get-tuple-element.57), channel_id=1, source_target_pairs={{0,8},{8,16},{16,24},{24,0},{1,9},{9,17},{17,25},{25,1},{2,10},{10... | collective-permute-start | bytes 393224 | tf_op jit(solution)/shard_map/ppermute | solution.py:253
  58.7 10.1 %collective-permute-start.14 = (bf16[128,256]{1,0:T(8,128)(2,1)S(1)}, bf16[128,256]{1,0:T(8,128)(2,1)S(1)}, u32[]{:S(2)}, u32[]{:S(2)}) collective-permute-start(bf16[128,256]{1,0:T(8,128)(2,1)S(1)} %get-tuple-element.65), channel_id=1, source_target_pairs={{0,32},{32,64},{64,96},{96,128},{128,160},{160,192},{192,224},{1,3... | collective-permute-start | bytes 196616 | tf_op jit(solution)/shard_map/ppermute | solution.py:262
  62.1 9.0 %collective-permute-start.15 = (bf16[128,256]{1,0:T(8,128)(2,1)S(1)}, bf16[128,256]{1,0:T(8,128)(2,1)S(1)}, u32[]{:S(2)}, u32[]{:S(2)}) collective-permute-start(bf16[128,256]{1,0:T(8,128)(2,1)S(1)} %get-tuple-element.66), channel_id=1, source_target_pairs={{32,0},{64,32},{96,64},{128,96},{160,128},{192,160},{224,192},{33,... | collective-permute-start | bytes 196616 | tf_op jit(solution)/shard_map/ppermute | solution.py:266
  64.2 6.9 %collective-permute-start.18 = (bf16[128,256]{1,0:T(8,128)(2,1)S(1)}, bf16[128,256]{1,0:T(8,128)(2,1)S(1)}, u32[]{:S(2)}, u32[]{:S(2)}) collective-permute-start(bf16[128,256]{1,0:T(8,128)(2,1)S(1)} %get-tuple-element.72), channel_id=1, source_target_pairs={{0,32},{32,0},{64,96},{96,64},{128,160},{160,128},{192,224},{224,1... | collective-permute-start | bytes 196616 | tf_op jit(solution)/shard_map/ppermute | solution.py:258
  66.9 10.3 %collective-permute-start.12 = (bf16[256,256]{1,0:T(8,128)(2,1)S(1)}, bf16[256,256]{1,0:T(8,128)(2,1)S(1)}, u32[]{:S(2)}, u32[]{:S(2)}) collective-permute-start(bf16[256,256]{1,0:T(8,128)(2,1)S(1)} %get-tuple-element.58), channel_id=1, source_target_pairs={{0,16},{8,24},{16,0},{24,8},{1,17},{9,25},{17,1},{25,9},{2,18},{10... | collective-permute-start | bytes 393224 | tf_op jit(solution)/shard_map/ppermute | solution.py:253
  68.8 8.4 %collective-permute-start.13 = (bf16[256,256]{1,0:T(8,128)(2,1)S(1)}, bf16[256,256]{1,0:T(8,128)(2,1)S(1)}, u32[]{:S(2)}, u32[]{:S(2)}) collective-permute-start(bf16[256,256]{1,0:T(8,128)(2,1)S(1)} %get-tuple-element.59), channel_id=1, source_target_pairs={{0,24},{8,0},{16,8},{24,16},{1,25},{9,1},{17,9},{25,17},{2,26},{10... | collective-permute-start | bytes 393224 | tf_op jit(solution)/shard_map/ppermute | solution.py:253
  72.2 7.7 %collective-permute-start.19 = (bf16[256,256]{1,0:T(8,128)(2,1)S(1)}, bf16[256,256]{1,0:T(8,128)(2,1)S(1)}, u32[]{:S(2)}, u32[]{:S(2)}) collective-permute-start(bf16[256,256]{1,0:T(8,128)(2,1)S(1)} %get-tuple-element.75), channel_id=1, source_target_pairs={{0,8},{8,16},{16,24},{24,0},{1,9},{9,17},{17,25},{25,1},{2,10},{10... | collective-permute-start | bytes 393224 | tf_op jit(solution)/shard_map/ppermute | solution.py:253
  72.6 7.3 %collective-permute-start.20 = (bf16[256,256]{1,0:T(8,128)(2,1)S(1)}, bf16[256,256]{1,0:T(8,128)(2,1)S(1)}, u32[]{:S(2)}, u32[]{:S(2)}) collective-permute-start(bf16[256,256]{1,0:T(8,128)(2,1)S(1)} %get-tuple-element.76), channel_id=1, source_target_pairs={{0,16},{8,24},{16,0},{24,8},{1,17},{9,25},{17,1},{25,9},{2,18},{10... | collective-permute-start | bytes 393224 | tf_op jit(solution)/shard_map/ppermute | solution.py:253
  74.7 6.0 %collective-permute-start.21 = (bf16[256,256]{1,0:T(8,128)(2,1)S(1)}, bf16[256,256]{1,0:T(8,128)(2,1)S(1)}, u32[]{:S(2)}, u32[]{:S(2)}) collective-permute-start(bf16[256,256]{1,0:T(8,128)(2,1)S(1)} %get-tuple-element.77), channel_id=1, source_target_pairs={{0,24},{8,0},{16,8},{24,16},{1,25},{9,1},{17,9},{25,17},{2,26},{10... | collective-permute-start | bytes 393224 | tf_op jit(solution)/shard_map/ppermute | solution.py:253

commit v2 on v1

v2 whole, which is shorter than its diff:
```python
import functools
import math

import jax
import jax.numpy as jnp
from jax import lax
from jax.experimental import pallas as pl
from jax.experimental.pallas import tpu as pltpu
from jax.sharding import Mesh
from jax.sharding import PartitionSpec as P

D = 128
B = 128
HALF = B // 2
NY = 4
NZ = 8
PIECE = 2 * B
PLANE = NY * PIECE
SMALL = PIECE // 8
Y_ORDER = (1, 2, 3)
EARLY_OUT = False
POOL = 5 * 10**9
FINAL = 5*10**9
EARLY_STACK = True
ROOT_HALF = 0.7071067811865476
SCALE = 1.0 / math.sqrt(D)
SCALE_LOG2E = SCALE * math.log2(math.e)
BF = jnp.bfloat16
F32 = jnp.float32

AT1 = PLANE
AT2 = AT1 + PLANE // 2
AT3 = AT2 + PLANE // 4
COLS = AT3 + 2 * B
PAIR = 8 * B


def dot(a, b, ca=1, cb=0):
    return lax.dot_general(a, b, (((ca,), (cb,)), ((), ())), preferred_element_type=F32)


def pair_sum(rows):
    r = lax.broadcasted_iota(jnp.int32, (rows, 2 * rows), 0)
    c = lax.broadcasted_iota(jnp.int32, (rows, 2 * rows), 1)
    return (lax.shift_right_logical(c, 1) == r).astype(F32).astype(BF)


def repeat_matrix(rows, log):
    r = lax.broadcasted_iota(jnp.int32, (rows << log, rows), 0)
    c = lax.broadcasted_iota(jnp.int32, (rows << log, rows), 1)
    return (lax.shift_right_logical(r, log) == c).astype(F32).astype(BF)


def pool(matrix, x):
    return (dot(matrix, x) * ROOT_HALF).astype(BF)


def expand(matrix, x):
    high = x.astype(BF)
    low = (x - high.astype(F32)).astype(BF)
    return dot(matrix, high) + dot(matrix, low)


def part_at(index, size=PIECE):
    return pl.ds(pl.multiple_of(index * size, size), size)


def head_at(index):
    return pl.ds(pl.multiple_of(index * D, D), D)


def later(y, d):
    return lax.rem(y + d, NY)


def earlier(y, d):
    return lax.rem(y - d + NY, NY)


def pack_kernel(at_ref, left_hbm, right_hbm, *refs):
    outs, sems = refs[:NY], refs[-1]
    y = at_ref[0]
    copies = [
        pltpu.make_async_copy(
            src.at[:, head_at(later(y, d))], outs[d].at[:, n * D : (n + 1) * D], sems.at[d, n]
        )
        for d in range(NY)
        for n, src in enumerate((left_hbm, right_hbm))
    ]
    for copy in copies:
        copy.start()
    for copy in copies:
        copy.wait()


def stack_kernel(at_ref, left_hbm, right_hbm, out_ref, sems):
    copies = [
        pltpu.make_async_copy(
            src.at[:, h * D : (h + 1) * D],
            out_ref.at[h * PIECE : (h + 1) * PIECE, n * D : (n + 1) * D],
            sems.at[h, n],
        )
        for h in range(NY)
        for n, src in enumerate((left_hbm, right_hbm))
    ]
    for copy in copies:
        copy.start()
    for copy in copies:
        copy.wait()


def unstack_kernel(at_ref, in_ref, left_hbm, right_hbm, token_ref, sems):
    token_ref[...] = jnp.zeros_like(token_ref)
    copies = [
        pltpu.make_async_copy(
            in_ref.at[h * PIECE : (h + 1) * PIECE, n * D : (n + 1) * D],
            dst.at[:, h * D : (h + 1) * D],
            sems.at[h, n],
        )
        for h in range(NY)
        for n, dst in enumerate((left_hbm, right_hbm))
    ]
    for copy in copies:
        copy.start()
    for copy in copies:
        copy.wait()


def unpack_kernel(at_ref, *refs):
    pieces, left_hbm, right_hbm, sems = refs[:NY], refs[NY], refs[NY + 1], refs[-1]
    y = at_ref[0]
    copies = [
        pltpu.make_async_copy(
            pieces[d].at[:, n * D : (n + 1) * D], dst.at[:, head_at(earlier(y, d))], sems.at[d, n]
        )
        for d in range(NY)
        for n, dst in enumerate((left_hbm, right_hbm))
    ]
    for copy in copies:
        copy.start()
    for copy in copies:
        copy.wait()


def pool_kernel(at_ref, k0, k1, k2, k3, kv_ref, m1_ref, m2_ref, m3_ref, tail_ref):
    y = at_ref[0]
    odd = lax.rem(at_ref[1], 2)
    for d, ref in enumerate((k0, k1, k2, k3)):
        kv_ref[part_at(earlier(y, d)), :] = ref[...]
    matrix = pair_sum(B)
    one = [pool(matrix, kv_ref[n * PIECE : (n + 1) * PIECE]) for n in range(4)]
    two = [pool(matrix, jnp.concatenate(one[n : n + 2], axis=0)) for n in (0, 2)]
    three = pool(matrix, jnp.concatenate(two, axis=0))
    four = pool(matrix[:HALF, :B], three)
    facing = kv_ref[part_at((1 - odd) * (PLANE // B - 1), B), :]
    other = kv_ref[part_at(odd * (PLANE // B - 1), B), :]
    m1_ref[:B] = three
    m1_ref[B:] = facing
    m2_ref[...] = four
    m3_ref[:HALF] = four
    m3_ref[HALF:] = other
    tail_ref[:HALF] = four
    tail_ref[HALF:] = other


def quad_kernel(at_ref, tail_ref, three_1, four_2, four_3, top_ref):
    z = at_ref[1]
    matrix = pair_sum(HALF)
    small = matrix[: B // 4, :HALF]
    fours = (tail_ref[:HALF], pool(matrix, three_1[:B]), four_2[...], four_3[:HALF])
    for d, four in enumerate(fours):
        top_ref[part_at((z ^ d) & 3, SMALL), :] = pool(small, four)
    top_ref[B:] = tail_ref[HALF:]


def by_three(z):
    return lax.rem(lax.shift_right_logical(z + 1, 1), 2) == 1


def pieces_of(i):
    start = max(0, i * PIECE - B)
    stop = min(PLANE, i * PIECE + 3 * B)
    return (
        (start, stop - start, start - (i * PIECE - B)),
        (AT1 + (i ^ 1) * B, B, 4 * B),
        (AT2 + ((i >> 1) ^ 1) * B, B, 5 * B),
        (AT3, 2 * B, 6 * B),
    )


def summed(values):
    return functools.reduce(jnp.add, values)


def early_kernel(
    at_ref, kv, from_1, from_2, from_3, qc, keys_t, vals_t, raised, pgrads, stats, keys, vals
):
    matrix = pair_sum(B)
    one = [pool(matrix, kv[n * PIECE : (n + 1) * PIECE]) for n in range(4)]
    two = [pool(matrix, jnp.concatenate(one[n : n + 2], axis=0)) for n in (0, 2)]
    at = 0
    for part in (kv[...], *one, *two, from_1[:B], from_2[...], from_3[:HALF]):
        rows = part.shape[0]
        keys[at : at + rows, :] = part[:, :D]
        vals[at : at + rows, :] = part[:, D:]
        at += rows
    second = lax.broadcasted_iota(jnp.int32, (B, PIECE), 1) >= B
    for i in range(NY):
        lanes = slice(i * PIECE, (i + 1) * PIECE)
        q = qc[lanes, :D]
        c = qc[lanes, D:]
        pieces = pieces_of(i)
        scores = [dot(keys[a : a + n, :], q, 1, 1) for a, n, _ in pieces]
        near = [scores[0][m * B : (m + 1) * B] for m in range(pieces[0][1] // B)]
        if i > 0:
            near[0] = jnp.where(second, -jnp.inf, near[0])
        if i < NY - 1:
            near[-1] = jnp.where(second, near[-1], -jnp.inf)
        scores[0] = jnp.concatenate(near, axis=0)
        top = functools.reduce(jnp.maximum, [jnp.max(s, axis=0, keepdims=True) for s in scores])
        total = []
        weighted = []
        for (a, n, r), s in zip(pieces, scores):
            e = jnp.exp2((s - top) * SCALE_LOG2E)
            g = dot(vals[a : a + n, :], c, 1, 1)
            raised[i, r : r + n, :] = e
            pgrads[i, r : r + n, :] = g
            total.append(jnp.sum(e, axis=0, keepdims=True))
            weighted.append(jnp.sum(e * g, axis=0, keepdims=True))
        stats[0:1, lanes] = top
        stats[1:2, lanes] = summed(total)
        stats[2:3, lanes] = summed(weighted)
    for n in range(COLS // B):
        cut = slice(n * B, (n + 1) * B)
        keys_t[:, cut] = keys[cut, :].T
        vals_t[:, cut] = vals[cut, :].T


def late_kernel(
    at_ref, from_1, from_3, from_7, qc, stats, top_ref, g_facing, g_other, edges, found, w5, s5, ew, es
):
    z = at_ref[1]
    odd = lax.rem(z, 2)
    edges[1 - odd] = from_1[B:]
    edges[odd] = jnp.where(by_three(z), from_3[HALF:], from_7[B:])
    first = lax.broadcasted_iota(jnp.int32, (B, PIECE), 1) < B
    for i in range(NY):
        lanes = slice(i * PIECE, (i + 1) * PIECE)
        q = qc[lanes, :D]
        c = qc[lanes, D:]
        scores = [dot(from_7[:B, :D], q, 1, 1)]
        pgrads = [dot(from_7[:B, D:], c, 1, 1)]
        side = {0: 0, NY - 1: 1}.get(i)
        if side is not None:
            score = dot(edges[side, :, :D], q, 1, 1)
            seen = first & (z > 0) if side == 0 else jnp.logical_not(first) & (z < NZ - 1)
            scores.append(jnp.where(seen, score, -jnp.inf))
            pgrads.append(dot(edges[side, :, D:], c, 1, 1))
        before = stats[0:1, lanes]
        top = functools.reduce(
            jnp.maximum, [before] + [jnp.max(s, axis=0, keepdims=True) for s in scores]
        )
        raised = [jnp.exp2((s - top) * SCALE_LOG2E) for s in scores]
        shrink = jnp.exp2((before - top) * SCALE_LOG2E)
        total = shrink * stats[1:2, lanes] + summed(
            [jnp.sum(e, axis=0, keepdims=True) for e in raised]
        )
        weighted = shrink * stats[2:3, lanes] + summed(
            [jnp.sum(e * g, axis=0, keepdims=True) for e, g in zip(raised, pgrads)]
        )
        inverse = 1.0 / total
        row_dot = inverse * weighted
        found[0:1, lanes] = shrink * inverse
        found[1:2, lanes] = row_dot
        probs = [e * inverse for e in raised]
        sgrads = [(p * (g - row_dot) * SCALE).astype(BF) for p, g in zip(probs, pgrads)]
        w5[:, lanes] = probs[0].astype(BF)
        s5[:, lanes] = sgrads[0]
        if side is not None:
            ew[side] = probs[1].astype(BF)
            es[side] = sgrads[1]
    top_ref[:B, :D] = dot(s5[...], qc[:, :D]).astype(BF)
    top_ref[:B, D:] = dot(w5[...], qc[:, D:]).astype(BF)

    def edge_grads(side):
        lanes = part_at(side * (NY - 1))
        key = dot(es[side], qc[lanes, :D]).astype(BF)
        value = dot(ew[side], qc[lanes, D:]).astype(BF)
        return key, value

    g_facing[:, :D], g_facing[:, D:] = edge_grads(1 - odd)
    key, value = edge_grads(odd)
    top_ref[B:, :D] = key
    top_ref[B:, D:] = value
    g_other[:, :D] = key
    g_other[:, D:] = value


def rest_kernel(
    at_ref, keys_t, vals_t, raised, pgrads, qc, from_7, edges, found, w5, s5, ew, es,
    og, g4, g3, g_own, g_one, g_two, grads,
):
    grads[...] = jnp.zeros_like(grads)
    five_k = from_7[:B, :D].T
    five_v = from_7[:B, D:].T
    for i in range(NY):
        lanes = slice(i * PIECE, (i + 1) * PIECE)
        q = qc[lanes, :D]
        c = qc[lanes, D:]
        ratio = found[0:1, lanes]
        row_dot = found[1:2, lanes]
        out_t = [dot(five_v, w5[:, lanes])]
        qg_t = [dot(five_k, s5[:, lanes])]
        side = {0: 0, NY - 1: 1}.get(i)
        if side is not None:
            out_t.append(dot(edges[side, :, D:].T, ew[side]))
            qg_t.append(dot(edges[side, :, :D].T, es[side]))
        for a, n, r in pieces_of(i):
            p = raised[i, r : r + n, :] * ratio
            w = p.astype(BF)
            s = (p * (pgrads[i, r : r + n, :] - row_dot) * SCALE).astype(BF)
            out_t.append(dot(vals_t[:, a : a + n], w))
            qg_t.append(dot(keys_t[:, a : a + n], s))
            grads[a : a + n, :D] += dot(s, q)
            grads[a : a + n, D:] += dot(w, c)
        og[lanes, :D] = summed(out_t).T.astype(BF)
        og[lanes, D:] = summed(qg_t).T.astype(BF)
    g_own[...] = grads[:AT1]
    g_one[...] = grads[AT1:AT2]
    g_two[...] = grads[AT2:AT3]
    g3[...] = grads[AT3 : AT3 + B]
    g4[...] = grads[AT3 + B :]


def spread_kernel(
    at_ref, back_ref, g4_ref, g3_ref, facing_ref, other_ref, s1_ref, s2_ref, s3_ref, keep_ref
):
    z = at_ref[1]
    twice = repeat_matrix(B // 4, 1)
    fourfold = repeat_matrix(B // 4, 2)

    def rows(d):
        return back_ref[part_at((z ^ d) & 3, SMALL), :]

    s1_ref[:B] = (g3_ref[...] + dot(fourfold, rows(1)) * 0.5).astype(BF)
    s1_ref[B:] = facing_ref[...]
    s2_ref[...] = (g4_ref[:HALF] + dot(twice, rows(2)) * ROOT_HALF).astype(BF)
    s3_ref[:HALF] = (g4_ref[HALF:] + dot(twice, rows(3)) * ROOT_HALF).astype(BF)
    s3_ref[HALF:] = other_ref[...]
    keep_ref[...] = dot(fourfold, rows(0)) * 0.5


def local_kernel(at_ref, own_ref, one_ref, two_ref, out_ref, *_):
    matrix = repeat_matrix(B, 1)
    for n in range(2):
        two = expand(matrix, two_ref[n * B : (n + 1) * B] * ROOT_HALF)
        for m in range(2):
            k = 2 * n + m
            one = one_ref[k * B : (k + 1) * B] + two[m * B : (m + 1) * B]
            cut = slice(k * PIECE, (k + 1) * PIECE)
            out_ref[cut] = own_ref[cut] + expand(matrix, one * ROOT_HALF)


def final_kernel(at_ref, own_ref, keep_ref, b1_ref, b2_ref, b3_ref, b7_ref, f0, f1, f2, f3, total):
    y = at_ref[0]
    z = at_ref[1]
    odd = lax.rem(z, 2)
    four = (b2_ref[...].astype(F32) + b3_ref[:HALF].astype(F32)) * ROOT_HALF
    up = keep_ref[...] + b1_ref[:B].astype(F32) + expand(repeat_matrix(HALF, 1), four)
    up *= ROOT_HALF * 0.5
    matrix = repeat_matrix(SMALL, 3)
    for n in range(NY):
        cut = slice(n * PIECE, (n + 1) * PIECE)
        total[cut] = own_ref[cut] + expand(matrix, up[n * SMALL : (n + 1) * SMALL])
    facing = part_at((1 - odd) * (PLANE // B - 1), B)
    total[facing, :] += b1_ref[B:].astype(F32)
    other = part_at(odd * (PLANE // B - 1), B)
    total[other, :] += jnp.where(by_three(z), b3_ref[HALF:], b7_ref[B:]).astype(F32)
    for d, ref in enumerate((f0, f1, f2, f3)):
        ref[...] = total[part_at(later(y, d)), :].astype(BF)


VMEM = pl.BlockSpec(memory_space=pltpu.VMEM)
SMEM = pl.BlockSpec(memory_space=pltpu.SMEM)
ANY = pl.BlockSpec(memory_space=pl.ANY)
HBM = pl.BlockSpec(memory_space=pltpu.HBM)


TOKEN = ((8, 128), F32)


def call(kernel, ins, outs, scratch=(), flops=10**6, source=VMEM, target=VMEM, after=(), vmem=8, alias=None):
    size = sum(a.size * a.dtype.itemsize for a in ins)
    size += sum(math.prod(s) * jnp.dtype(t).itemsize for s, t in outs)
    count = len(ins)

    def body(*refs):
        kernel(*refs[:count], *refs[count + len(after) :])

    return pl.pallas_call(
        body,
        out_shape=[jax.ShapeDtypeStruct(s, t) for s, t in outs],
        in_specs=[SMEM] + [source] * (count - 1) + [ANY] * len(after),
        out_specs=[target if s != TOKEN else VMEM for s in outs[: len(outs) - bool(alias)]]
        + [ANY] * bool(alias),
        scratch_shapes=list(scratch),
        input_output_aliases=alias or {},
        compiler_params=pltpu.CompilerParams(vmem_limit_bytes=vmem * 2**20),
        cost_estimate=pl.CostEstimate(flops=flops, bytes_accessed=size, transcendentals=0),
    )(*ins, *after)


def around_y(pieces):
    got = {0: pieces[0]}
    for d in Y_ORDER:
        got[d] = lax.ppermute(pieces[d], "y", [(i, (i + d) % NY) for i in range(NY)])
    return [got[d] for d in range(NY)]


def across_y(array):
    return lax.all_to_all(array, "y", split_axis=0, concat_axis=0, tiled=True)


def over_z(array, d):
    return lax.ppermute(array, "z", [(i, i ^ d) for i in range(NZ)])


def per_device(queries, keys, values, cotangent):
    at = jnp.stack([lax.axis_index("y"), lax.axis_index("z")]).astype(jnp.int32)
    piece = ((PIECE, 2 * D), BF)
    plane = ((PLANE, 2 * D), BF)
    level = ((B, 2 * D), BF)
    half = ((HALF, 2 * D), BF)
    tail = ((HALF + B, 2 * D), BF)
    double = ((2 * B, 2 * D), BF)
    wide = ((B, 2 * D), F32)
    sems = [pltpu.SemaphoreType.DMA((NY, 2))]
    kv = call(pack_kernel, [at, keys, values], [piece] * NY, scratch=sems, source=HBM)
    kv = around_y(kv)
    (qc_own,) = call(stack_kernel, [at, queries, cotangent], [plane], scratch=sems, source=HBM)
    qc = across_y(qc_own)
    kv, m1, m2, m3, own_tail = call(
        pool_kernel,
        [at, *kv],
        [plane, double, half, tail, tail],
        flops=POOL,
        after=[qc_own] if EARLY_STACK else [],
    )
    from_1, from_2, from_3 = over_z(m1, 1), over_z(m2, 2), over_z(m3, 3)
    (top,) = call(quad_kernel, [at, own_tail, from_1, from_2, from_3], [double])
    from_7 = over_z(top, 7)
    keys_t, vals_t, raised, pgrads, stats = call(
        early_kernel,
        [at, kv, from_1, from_2, from_3, qc],
        [((D, COLS), BF)] * 2 + [((NY, PAIR, PIECE), F32)] * 2 + [((8, PLANE), F32)],
        scratch=[pltpu.VMEM((COLS, D), BF)] * 2,
        flops=10**9,
        vmem=20,
    )
    g_top, g_facing, g_other, edges, found, w5, s5, ew, es = call(
        late_kernel,
        [at, from_1, from_3, from_7, qc, stats],
        [double, level, level, ((2, B, 2 * D), BF), ((8, PLANE), F32)]
        + [((B, PLANE), BF)] * 2
        + [((2, B, PIECE), BF)] * 2,
        flops=10**8,
    )
    og, g4, g3, g_own, g_one, g_two = call(
        rest_kernel,
        [at, keys_t, vals_t, raised, pgrads, qc, from_7, edges, found, w5, s5, ew, es],
        [plane, wide, wide]
        + [((PLANE, 2 * D), F32), ((PLANE // 2, 2 * D), F32), ((PLANE // 4, 2 * D), F32)],
        scratch=[pltpu.VMEM((COLS, 2 * D), F32)],
        flops=2 * 10**9,
        vmem=20,
    )
    back_7 = over_z(g_top, 7)
    s1, s2, s3, keep = call(
        spread_kernel,
        [at, back_7, g4, g3, g_facing, g_other],
        [double, half, tail, wide],
    )
    own, og = call(
        local_kernel,
        [at, g_own, g_one, g_two],
        [((PLANE, 2 * D), F32), plane],
        after=[og, keep],
        alias={4: 1},
    )
    og = across_y(og)
    back_1, back_2, back_3 = over_z(s1, 1), over_z(s2, 2), over_z(s3, 3)
    whole = ((PIECE, NY * D), BF)
    attended, grad_queries, token = call(
        unstack_kernel, [at, og], [whole] * 2 + [TOKEN], scratch=sems, target=HBM
    )
    final = call(
        final_kernel,
        [at, own, keep, back_1, back_2, back_3, back_7],
        [piece] * NY,
        scratch=[pltpu.VMEM((PLANE, 2 * D), F32)],
        flops=FINAL,
    )
    final = around_y(final)
    grad_keys, grad_values = call(
        unpack_kernel, [at, *final], [whole] * 2, scratch=sems, target=HBM, after=[token]
    )
    return attended, grad_queries, grad_keys, grad_values


def solution(mesh):
    seq, head, rep = mesh.devices.shape
    split = Mesh(mesh.devices.reshape(NZ, NY, head, rep), ("z", "y", "head", "rep"))
    spec = P(("rep", "z", "y"), "head")
    return jax.shard_map(
        per_device, mesh=split, in_specs=(spec,) * 4, out_specs=(spec,) * 4, check_vma=False
    )
```

time: 82.5 us -> 70 us (0.85)
  starting transfers between devices: 50 us -> 36.9 us
  waiting for transfers between devices: 11.7 us -> 9.73 us
  local copies, waits for them, and re-layouts: 1.91 us -> 3.8 us
    ppermute x10 -> x8, starting transfers between devices: 30 us -> 16.7 us  [over_z(): return lax.ppermute(array, 'z', [(i, i ^ d) for i in range(NZ)])]
    all_to_all x0 -> x2, starting transfers between devices: none -> 8.14 us  [across_y(): return lax.all_to_all(array, 'y', split_axis=0, concat_axis=0, tiled=True)]
    ppermute x12 -> x6, starting transfers between devices: 20 us -> 12.1 us  [around_y(): lax.ppermute(pieces[d], 'y', [(i, (i + d) % NY) for i in range(NY)])]
    ppermute x12 -> x6, waiting for transfers between devices: 6.7 us -> 1.41 us  [around_y(): lax.ppermute(pieces[d], 'y', [(i, (i + d) % NY) for i in range(NY)])]
    ppermute x10 -> x8, waiting for transfers between devices: 5.05 us -> 7.61 us  [over_z(): return lax.ppermute(array, 'z', [(i, i ^ d) for i in range(NZ)])]
    unnamed x8, local copies, waits for them, and re-layouts: 1.91 us -> 3.8 us
  transfers between devices with their start and end apart: 22 -> 16, of which waited for: 7 -> 6; matrix products, arithmetic and copies ran while one was open for 0% -> 0% of each run, Pallas kernels for 8% -> 20%
where the time goes in v2:
time: 70 us; the launch traced here: 69.7 us
  starting transfers between devices  36.9 us (53%)
  Pallas kernels  18.2 us (26%)
  waiting for transfers between devices  9.73 us (14%)
  local copies, waits for them, and re-layouts  3.8 us (5%)
  between operations  0.94 us (1%)
    pallas_call x12, Pallas kernels, call(): pl.pallas_call(body, out_shape=[jax.ShapeDtypeStruct(s, t) for s, t in ou...  18.2 us
    ppermute x8, starting transfers between devices, over_z(): return lax.ppermute(array, 'z', [(i, i ^ d) for i in range(NZ)])  16.7 us
    ppermute x6, starting transfers between devices, around_y(): lax.ppermute(pieces[d], 'y', [(i, (i + d) % NY) for i in range(NY)])  12.1 us
    all_to_all x2, starting transfers between devices, across_y(): return lax.all_to_all(array, 'y', split_axis=0, concat_axis=0, tiled=True)  8.14 us
    ppermute x8, waiting for transfers between devices, over_z(): return lax.ppermute(array, 'z', [(i, i ^ d) for i in range(NZ)])  7.61 us
    unnamed x8, local copies, waits for them, and re-layouts  3.8 us
    ppermute x6, waiting for transfers between devices, around_y(): lax.ppermute(pieces[d], 'y', [(i, (i + d) % NY) for i in range(NY)])  1.41 us
  transfers between devices with their start and end apart: 16, of which 6 were waited for; matrix products, arithmetic and copies ran while one was open for 0% of the time, Pallas kernels for 20%

profile of v2, /device:TPU:6, one launch (start us, length us, event | category | flops | bytes accessed | tf_op | source)
XLA Modules:
  0.0 69.7 jit_solution(9314726723687295043)
XLA Ops:
  0.6 0.1 pad_add_fusion.refs_0_
  0.7 0.9 %copy-done = bf16[256,512]{1,0:T(8,128)(2,1)S(1)} copy-done((bf16[256,512]{1,0:T(8,128)(2,1)S(1)}, bf16[256,512]{1,0:T(8,128)(2,1)}, u32[]{:S(2)}) %copy-start) | copy-done | bytes 262168
  1.7 0.9 %copy-done.1 = bf16[256,512]{1,0:T(8,128)(2,1)S(1)} copy-done((bf16[256,512]{1,0:T(8,128)(2,1)S(1)}, bf16[256,512]{1,0:T(8,128)(2,1)}, u32[]{:S(2)}) %copy-start.1) | copy-done | bytes 262168
  2.6 0.7 %shard_map.75 = (bf16[256,256]{1,0:T(8,128)(2,1)S(1)}, bf16[256,256]{1,0:T(8,128)(2,1)S(1)}, bf16[256,256]{1,0:T(8,128)(2,1)S(1)}, bf16[256,256]{1,0:T(8,128)(2,1)S(1)}) custom-call(s32[2]{0:T(128)S(1)} %pad_add_fusion.refs_0_, bf16[256,512]{1,0:T(8,128)(2,1)S(1)} %copy-done, bf16[256,512]{1,0:T(8,128)(2,1)S(1)} %copy-done.1), custom_call_target="tpu_custom_call" | custom-call | flops 1000000 | bytes 1048584 | tf_op jit(solution)/shard_map/pallas_call | solution.py:400
  3.4 1.7 %collective-permute-start = (bf16[256,256]{1,0:T(8,128)(2,1)S(1)}, bf16[256,256]{1,0:T(8,128)(2,1)S(1)}, u32[]{:S(2)}, u32[]{:S(2)}) collective-permute-start(bf16[256,256]{1,0:T(8,128)(2,1)S(1)} %get-tuple-element.49), channel_id=1, source_target_pairs={{0,8},{8,16},{16,24},{24,0},{1,9},{9,17},{17,25},{25,1},{2,10},{10... | collective-permute-start | bytes 393224 | tf_op jit(solution)/shard_map/ppermute | solution.py:416
  5.0 2.9 %collective-permute-start.1 = (bf16[256,256]{1,0:T(8,128)(2,1)S(1)}, bf16[256,256]{1,0:T(8,128)(2,1)S(1)}, u32[]{:S(2)}, u32[]{:S(2)}) collective-permute-start(bf16[256,256]{1,0:T(8,128)(2,1)S(1)} %get-tuple-element.50), channel_id=1, source_target_pairs={{0,16},{8,24},{16,0},{24,8},{1,17},{9,25},{17,1},{25,9},{2,18},{10... | collective-permute-start | bytes 393224 | tf_op jit(solution)/shard_map/ppermute | solution.py:416
  7.9 1.3 %collective-permute-start.2 = (bf16[256,256]{1,0:T(8,128)(2,1)S(1)}, bf16[256,256]{1,0:T(8,128)(2,1)S(1)}, u32[]{:S(2)}, u32[]{:S(2)}) collective-permute-start(bf16[256,256]{1,0:T(8,128)(2,1)S(1)} %get-tuple-element.51), channel_id=1, source_target_pairs={{0,24},{8,0},{16,8},{24,16},{1,25},{9,1},{17,9},{25,17},{2,26},{10... | collective-permute-start | bytes 393224 | tf_op jit(solution)/shard_map/ppermute | solution.py:416
  9.3 0.9 %copy-done.2 = bf16[256,512]{1,0:T(8,128)(2,1)S(1)} copy-done((bf16[256,512]{1,0:T(8,128)(2,1)S(1)}, bf16[256,512]{1,0:T(8,128)(2,1)}, u32[]{:S(2)}) %copy-start.2) | copy-done | bytes 262168
  10.2 0.9 %copy-done.3 = bf16[256,512]{1,0:T(8,128)(2,1)S(1)} copy-done((bf16[256,512]{1,0:T(8,128)(2,1)S(1)}, bf16[256,512]{1,0:T(8,128)(2,1)}, u32[]{:S(2)}) %copy-start.3) | copy-done | bytes 262168
  11.2 1.5 %shard_map.76.refs_5_ = bf16[1024,256]{1,0:T(8,128)(2,1)} custom-call(s32[2]{0:T(128)S(1)} %pad_add_fusion.refs_0_, bf16[256,512]{1,0:T(8,128)(2,1)S(1)} %copy-done.2, bf16[256,512]{1,0:T(8,128)(2,1)S(1)} %copy-done.3), custom_call_target="tpu_custom_call" | custom-call | flops 1000000 | bytes 1048584 | tf_op jit(solution)/shard_map/pallas_call | solution.py:400
  12.7 3.5 %all-to-all-start = ((bf16[4,256,256]{2,1,0:T(8,128)(2,1)}), bf16[4,256,256]{2,1,0:T(8,128)(2,1)S(1)}, u32[]{:S(2)}, u32[]{:S(2)}) async-start(bf16[4,256,256]{2,1,0:T(8,128)(2,1)} %bitcast.2), calls=%async_computation | async-start | bytes 1048576 | tf_op jit(solution)/shard_map/all_to_all | solution.py:421
  16.2 0.0 collective-permute-done.refs_2_
  16.2 0.0 collective-permute-done.1.refs_3_
  16.2 0.0 collective-permute-done.2.refs_4_
  16.2 1.3 %shard_map.77 = (bf16[1024,256]{1,0:T(8,128)(2,1)S(1)}, bf16[256,256]{1,0:T(8,128)(2,1)S(1)}, bf16[64,256]{1,0:T(8,128)(2,1)S(1)}, bf16[192,256]{1,0:T(8,128)(2,1)S(1)}, bf16[192,256]{1,0:T(8,128)(2,1)S(1)}) custom-call(s32[2]{0:T(128)S(1)} %pad_add_fusion.refs_0_, bf16[256,256]{1,0:T(8,128)(2,1)S(1)} %get-tuple-element.48.refs_1_, ...), custom_call_target="tpu_custom_call" | custom-call | flops 5000000000 | bytes 1409032 | tf_op jit(solution)/shard_map/pallas_call | solution.py:400
  17.5 2.0 %collective-permute-start.3 = (bf16[256,256]{1,0:T(8,128)(2,1)S(1)}, bf16[256,256]{1,0:T(8,128)(2,1)S(1)}, u32[]{:S(2)}, u32[]{:S(2)}) collective-permute-start(bf16[256,256]{1,0:T(8,128)(2,1)S(1)} %get-tuple-element.53), channel_id=1, source_target_pairs={{0,32},{32,0},{64,96},{96,64},{128,160},{160,128},{192,224},{224,1... | collective-permute-start | bytes 393224 | tf_op jit(solution)/shard_map/ppermute | solution.py:425
  19.5 2.8 %collective-permute-start.5 = (bf16[192,256]{1,0:T(8,128)(2,1)S(1)}, bf16[192,256]{1,0:T(8,128)(2,1)S(1)}, u32[]{:S(2)}, u32[]{:S(2)}) collective-permute-start(bf16[192,256]{1,0:T(8,128)(2,1)S(1)} %get-tuple-element.55), channel_id=1, source_target_pairs={{0,96},{32,64},{64,32},{96,0},{128,224},{160,192},{192,160},{224,1... | collective-permute-start | bytes 294920 | tf_op jit(solution)/shard_map/ppermute | solution.py:425
  22.3 0.5 collective-permute-start.4
  22.8 5.4 %collective-permute-done.4.refs_3_ = bf16[64,256]{1,0:T(8,128)(2,1)S(1)} collective-permute-done((bf16[64,256]{1,0:T(8,128)(2,1)S(1)}, bf16[64,256]{1,0:T(8,128)(2,1)S(1)}, u32[]{:S(2)}, u32[]{:S(2)}) %collective-permute-start.4) | collective-permute-done | bytes 32800 | tf_op jit(solution)/shard_map/ppermute | solution.py:425
  28.2 0.0 collective-permute-done.5.refs_4_.refs_2_
  28.2 0.0 collective-permute-done.3.refs_2_.refs_1_
  28.2 0.8 %shard_map.79 = bf16[256,256]{1,0:T(8,128)(2,1)S(1)} custom-call(s32[2]{0:T(128)S(1)} %pad_add_fusion.refs_0_, bf16[192,256]{1,0:T(8,128)(2,1)S(1)} %get-tuple-element.60.refs_1_, bf16[256,256]{1,0:T(8,128)(2,1)S(1)} %collective-permute-done.3.refs_2_.refs_1_, bf16[64,256]{1,0:T(8,128)(2,1)S(1)} %collective-permute-done.4.refs_3_, ...), custom_call_target="tpu_custom_call" | custom-call | flops 1000000 | bytes 491528 | tf_op jit(solution)/shard_map/pallas_call | solution.py:400
  29.1 4.2 %collective-permute-start.6 = (bf16[256,256]{1,0:T(8,128)(2,1)S(1)}, bf16[256,256]{1,0:T(8,128)(2,1)S(1)}, u32[]{:S(2)}, u32[]{:S(2)}) collective-permute-start(bf16[256,256]{1,0:T(8,128)(2,1)S(1)} %shard_map.79), channel_id=1, source_target_pairs={{0,224},{32,192},{64,160},{96,128},{128,96},{160,64},{192,32},{224... | collective-permute-start | bytes 393224 | tf_op jit(solution)/shard_map/ppermute | solution.py:425
  33.2 0.0 all-to-all-done
  33.2 2.5 %shard_map.78 = (bf16[128,2048]{1,0:T(8,128)(2,1)S(1)}, bf16[128,2048]{1,0:T(8,128)(2,1)S(1)}, f32[4,1024,256]{2,1,0:T(8,128)S(1)}, f32[4,1024,256]{2,1,0:T(8,128)S(1)}, f32[8,1024]{1,0:T(8,128)S(1)}) custom-call(s32[2]{0:T(128)S(1)} %pad_add_fusion.refs_0_, bf16[1024,256]{1,0:T(8,128)(2,1)S(1)} %get-tuple-element.52.refs_1_, ...), custom_call_target="tpu_custom_call" | custom-call | flops 1000000000 | bytes 10780680 | tf_op jit(solution)/shard_map/pallas_call | solution.py:400
  35.8 1.5 %collective-permute-done.6.refs_3_.refs_6_ = bf16[256,256]{1,0:T(8,128)(2,1)S(1)} collective-permute-done((bf16[256,256]{1,0:T(8,128)(2,1)S(1)}, bf16[256,256]{1,0:T(8,128)(2,1)S(1)}, u32[]{:S(2)}, u32[]{:S(2)}) %collective-permute-start.6) | collective-permute-done | bytes 131104 | tf_op jit(solution)/shard_map/ppermute | solution.py:425
  37.3 1.5 %shard_map.80 = (bf16[256,256]{1,0:T(8,128)(2,1)S(1)}, bf16[128,256]{1,0:T(8,128)(2,1)S(1)}, bf16[128,256]{1,0:T(8,128)(2,1)S(1)}, bf16[2,128,256]{2,1,0:T(8,128...) custom-call(s32[2]{0:T(128)S(1)} %pad_add_fusion.refs_0_, ...), custom_call_target="tpu_custom_call" | custom-call | flops 100000000 | bytes 2129928 | tf_op jit(solution)/shard_map/pallas_call | solution.py:400
  38.7 3.6 %collective-permute-start.7 = (bf16[256,256]{1,0:T(8,128)(2,1)S(1)}, bf16[256,256]{1,0:T(8,128)(2,1)S(1)}, u32[]{:S(2)}, u32[]{:S(2)}) collective-permute-start(bf16[256,256]{1,0:T(8,128)(2,1)S(1)} %get-tuple-element.72), channel_id=1, source_target_pairs={{0,224},{32,192},{64,160},{96,128},{128,96},{160,64},{192,32},{224... | collective-permute-start | bytes 393224 | tf_op jit(solution)/shard_map/ppermute | solution.py:425
  42.4 3.7 %shard_map.81 = (bf16[1024,256]{1,0:T(8,128)(2,1)}, f32[128,256]{1,0:T(8,128)S(1)}, f32[128,256]{1,0:T(8,128)S(1)}, f32[1024,256]{1,0:T(8,128)S(1)}, f32[512,256]{1,0:T(8,128)S(1)}, /*index=5*/f32[256,256]{1,0:T(8,128)S(1)}) custom-call(s32[2]{0:T(128)S(1)} %pad_add_fusion.refs_0_, bf16[128,2048]{1,0:T(8,128)(2,1)S(1)} %get-tuple-element.56.refs_1_, ...), custom_call_target="tpu_custom_call" | custom-call | flops 2000000000 | bytes 13664264 | tf_op jit(solution)/shard_map/pallas_call | solution.py:400
  46.0 0.7 collective-permute-done.7.refs_1_.refs_6_
  46.7 0.7 %shard_map.82 = (bf16[256,256]{1,0:T(8,128)(2,1)S(1)}, bf16[64,256]{1,0:T(8,128)(2,1)S(1)}, bf16[192,256]{1,0:T(8,128)(2,1)S(1)}, f32[128,256]{1,0:T(8,128)S(1)}) custom-call(s32[2]{0:T(128)S(1)} %pad_add_fusion.refs_0_, bf16[256,256]{1,0:T(8,128)(2,1)S(1)} %collective-permute-done.7.refs_1_.refs_6_, f32[128,256]{1,0:T(8,128)S(1)} %get-tuple-element.73.refs_2_, ...), custom_call_target="tpu_custom_call" | custom-call | flops 1000000 | bytes 917512 | tf_op jit(solution)/shard_map/pallas_call | solution.py:400
  47.4 1.0 %collective-permute-start.8 = (bf16[256,256]{1,0:T(8,128)(2,1)S(1)}, bf16[256,256]{1,0:T(8,128)(2,1)S(1)}, u32[]{:S(2)}, u32[]{:S(2)}) collective-permute-start(bf16[256,256]{1,0:T(8,128)(2,1)S(1)} %get-tuple-element.82), channel_id=1, source_target_pairs={{0,32},{32,0},{64,96},{96,64},{128,160},{160,128},{192,224},{224,1... | collective-permute-start | bytes 393224 | tf_op jit(solution)/shard_map/ppermute | solution.py:425
  48.5 2.0 %collective-permute-start.10 = (bf16[192,256]{1,0:T(8,128)(2,1)S(1)}, bf16[192,256]{1,0:T(8,128)(2,1)S(1)}, u32[]{:S(2)}, u32[]{:S(2)}) collective-permute-start(bf16[192,256]{1,0:T(8,128)(2,1)S(1)} %get-tuple-element.84), channel_id=1, source_target_pairs={{0,96},{32,64},{64,32},{96,0},{128,224},{160,192},{192,160},{224,1... | collective-permute-start | bytes 294920 | tf_op jit(solution)/shard_map/ppermute | solution.py:425
  50.4 0.6 collective-permute-start.9
  51.0 1.4 %shard_map.83 = (f32[1024,256]{1,0:T(8,128)S(1)}, bf16[1024,256]{1,0:T(8,128)(2,1)}) custom-call(s32[2]{0:T(128)S(1)} %pad_add_fusion.refs_0_, f32[1024,256]{1,0:T(8,128)S(1)} %get-tuple-element.68.refs_1_, f32[512,256]{1,0:T(8,128)S(1)} %get-tuple-element.69.refs_2_, f32[256,256]{1,0:T(8,128)S(1)} %get-tuple-element.70.refs_3_, ...), custom_call_target="tpu_custom_call", output_to_operand_aliasing={{1}: (4, {})} | custom-call | flops 1000000 | bytes 3407880 | tf_op jit(solution)/shard_map/pallas_call | solution.py:400
  52.5 4.7 %all-to-all-start.1 = ((bf16[4,256,256]{2,1,0:T(8,128)(2,1)}), bf16[4,256,256]{2,1,0:T(8,128)(2,1)S(1)}, u32[]{:S(2)}, u32[]{:S(2)}) async-start(bf16[4,256,256]{2,1,0:T(8,128)(2,1)} %bitcast.4), calls=%async_computation.1 | async-start | bytes 1048576 | tf_op jit(solution)/shard_map/all_to_all | solution.py:421
  57.1 0.0 collective-permute-done.9.refs_4_
  57.1 0.0 collective-permute-done.10.refs_5_
  57.2 1.2 %shard_map.85 = (bf16[256,256]{1,0:T(8,128)(2,1)S(1)}, bf16[256,256]{1,0:T(8,128)(2,1)S(1)}, bf16[256,256]{1,0:T(8,128)(2,1)S(1)}, bf16[256,256]{1,0:T(8,128)(2,1)S(1)}) custom-call(s32[2]{0:T(128)S(1)} %pad_add_fusion.refs_0_, f32[1024,256]{1,0:T(8,128)S(1)} %get-tuple-element.81.refs_1_, f32[128,256]{1,0:T(8,128)S(1)} %get-tuple-element.77.refs_5_.refs_2_, ...), custom_call_target="tpu_custom_call" | custom-call | flops 5000000000 | bytes 2097160 | tf_op jit(solution)/shard_map/pallas_call | solution.py:400
  58.4 2.1 %collective-permute-start.11 = (bf16[256,256]{1,0:T(8,128)(2,1)S(1)}, bf16[256,256]{1,0:T(8,128)(2,1)S(1)}, u32[]{:S(2)}, u32[]{:S(2)}) collective-permute-start(bf16[256,256]{1,0:T(8,128)(2,1)S(1)} %get-tuple-element.86), channel_id=1, source_target_pairs={{0,8},{8,16},{16,24},{24,0},{1,9},{9,17},{17,25},{25,1},{2,10},{10... | collective-permute-start | bytes 393224 | tf_op jit(solution)/shard_map/ppermute | solution.py:416
  60.5 2.7 %collective-permute-start.12 = (bf16[256,256]{1,0:T(8,128)(2,1)S(1)}, bf16[256,256]{1,0:T(8,128)(2,1)S(1)}, u32[]{:S(2)}, u32[]{:S(2)}) collective-permute-start(bf16[256,256]{1,0:T(8,128)(2,1)S(1)} %get-tuple-element.87), channel_id=1, source_target_pairs={{0,16},{8,24},{16,0},{24,8},{1,17},{9,25},{17,1},{25,9},{2,18},{10... | collective-permute-start | bytes 393224 | tf_op jit(solution)/shard_map/ppermute | solution.py:416
  63.2 1.5 %collective-permute-start.13 = (bf16[256,256]{1,0:T(8,128)(2,1)S(1)}, bf16[256,256]{1,0:T(8,128)(2,1)S(1)}, u32[]{:S(2)}, u32[]{:S(2)}) collective-permute-start(bf16[256,256]{1,0:T(8,128)(2,1)S(1)} %get-tuple-element.88), channel_id=1, source_target_pairs={{0,24},{8,0},{16,8},{24,16},{1,25},{9,1},{17,9},{25,17},{2,26},{10... | collective-permute-start | bytes 393224 | tf_op jit(solution)/shard_map/ppermute | solution.py:416
  64.6 0.7 %all-to-all-done.1 = bf16[4,256,256]{2,1,0:T(8,128)(2,1)S(1)} async-done(((bf16[4,256,256]{2,1,0:T(8,128)(2,1)}), bf16[4,256,256]{2,1,0:T(8,128)(2,1)S(1)}, u32[]{:S(2)}, u32[]{:S(2)}) %all-to-all-start.1) | async-done | bytes 524320 | tf_op jit(solution)/shard_map/all_to_all | solution.py:421
  65.3 1.4 %shard_map.84 = (bf16[256,512]{1,0:T(8,128)(2,1)}, bf16[256,512]{1,0:T(8,128)(2,1)}, f32[8,128]{1,0:T(8,128)S(1)}) custom-call(s32[2]{0:T(128)S(1)} %pad_add_fusion.refs_0_, bf16[1024,256]{1,0:T(8,128)(2,1)S(1)} %bitcast.9), custom_call_target="tpu_custom_call" | custom-call | flops 1000000 | bytes 1052680 | tf_op jit(solution)/shard_map/pallas_call | solution.py:400
  66.7 0.0 collective-permute-done.11.refs_2_
  66.7 1.3 %collective-permute-done.12.refs_3_ = bf16[256,256]{1,0:T(8,128)(2,1)S(1)} collective-permute-done((bf16[256,256]{1,0:T(8,128)(2,1)S(1)}, bf16[256,256]{1,0:T(8,128)(2,1)S(1)}, u32[]{:S(2)}, u32[]{:S(2)}) %collective-permute-start.12) | collective-permute-done | bytes 131104 | tf_op jit(solution)/shard_map/ppermute | solution.py:416
  68.1 0.1 collective-permute-done.13.refs_4_
  68.1 1.4 %shard_map.86 = (bf16[256,512]{1,0:T(8,128)(2,1)}, bf16[256,512]{1,0:T(8,128)(2,1)}) custom-call(s32[2]{0:T(128)S(1)} %pad_add_fusion.refs_0_, bf16[256,256]{1,0:T(8,128)(2,1)S(1)} %get-tuple-element.85.refs_1_, bf16[256,256]{1,0:T(8,128)(2,1)S(1)} %collective-permute-done.11.refs_2_, bf16[256,256]{1,0:T(8,128)(2,1)S(1)} %collective-permute-done.12.refs_3_, ...), custom_call_target="tpu_custom_call" | custom-call | flops 1000000 | bytes 1048584 | tf_op jit(solution)/shard_map/pallas_call | solution.py:400
  (5 shorter events, 0.0 us)
Async XLA Ops:
  0.7 1.0 %copy-start = (bf16[256,512]{1,0:T(8,128)(2,1)S(1)}, bf16[256,512]{1,0:T(8,128)(2,1)}, u32[]{:S(2)}) copy-start(bf16[256,512]{1,0:T(8,128)(2,1)} %refs_1_.2) | copy-start | bytes 786436
  1.7 0.9 %copy-start.1 = (bf16[256,512]{1,0:T(8,128)(2,1)S(1)}, bf16[256,512]{1,0:T(8,128)(2,1)}, u32[]{:S(2)}) copy-start(bf16[256,512]{1,0:T(8,128)(2,1)} %refs_2_.2) | copy-start | bytes 786436
  3.4 12.8 %collective-permute-start = (bf16[256,256]{1,0:T(8,128)(2,1)S(1)}, bf16[256,256]{1,0:T(8,128)(2,1)S(1)}, u32[]{:S(2)}, u32[]{:S(2)}) collective-permute-start(bf16[256,256]{1,0:T(8,128)(2,1)S(1)} %get-tuple-element.49), channel_id=1, source_target_pairs={{0,8},{8,16},{16,24},{24,0},{1,9},{9,17},{17,25},{25,1},{2,10},{10... | collective-permute-start | bytes 393224 | tf_op jit(solution)/shard_map/ppermute | solution.py:416
  5.0 11.2 %collective-permute-start.1 = (bf16[256,256]{1,0:T(8,128)(2,1)S(1)}, bf16[256,256]{1,0:T(8,128)(2,1)S(1)}, u32[]{:S(2)}, u32[]{:S(2)}) collective-permute-start(bf16[256,256]{1,0:T(8,128)(2,1)S(1)} %get-tuple-element.50), channel_id=1, source_target_pairs={{0,16},{8,24},{16,0},{24,8},{1,17},{9,25},{17,1},{25,9},{2,18},{10... | collective-permute-start | bytes 393224 | tf_op jit(solution)/shard_map/ppermute | solution.py:416
  7.9 8.3 %collective-permute-start.2 = (bf16[256,256]{1,0:T(8,128)(2,1)S(1)}, bf16[256,256]{1,0:T(8,128)(2,1)S(1)}, u32[]{:S(2)}, u32[]{:S(2)}) collective-permute-start(bf16[256,256]{1,0:T(8,128)(2,1)S(1)} %get-tuple-element.51), channel_id=1, source_target_pairs={{0,24},{8,0},{16,8},{24,16},{1,25},{9,1},{17,9},{25,17},{2,26},{10... | collective-permute-start | bytes 393224 | tf_op jit(solution)/shard_map/ppermute | solution.py:416
  9.3 0.9 %copy-start.2 = (bf16[256,512]{1,0:T(8,128)(2,1)S(1)}, bf16[256,512]{1,0:T(8,128)(2,1)}, u32[]{:S(2)}) copy-start(bf16[256,512]{1,0:T(8,128)(2,1)} %refs_1_.3) | copy-start | bytes 786436
  10.2 0.9 %copy-start.3 = (bf16[256,512]{1,0:T(8,128)(2,1)S(1)}, bf16[256,512]{1,0:T(8,128)(2,1)}, u32[]{:S(2)}) copy-start(bf16[256,512]{1,0:T(8,128)(2,1)} %refs_2_.3) | copy-start | bytes 786436
  12.7 20.5 %all-to-all-start = ((bf16[4,256,256]{2,1,0:T(8,128)(2,1)}), bf16[4,256,256]{2,1,0:T(8,128)(2,1)S(1)}, u32[]{:S(2)}, u32[]{:S(2)}) async-start(bf16[4,256,256]{2,1,0:T(8,128)(2,1)} %bitcast.2), calls=%async_computation | async-start | bytes 1048576 | tf_op jit(solution)/shard_map/all_to_all | solution.py:421
  17.5 10.7 %collective-permute-start.3 = (bf16[256,256]{1,0:T(8,128)(2,1)S(1)}, bf16[256,256]{1,0:T(8,128)(2,1)S(1)}, u32[]{:S(2)}, u32[]{:S(2)}) collective-permute-start(bf16[256,256]{1,0:T(8,128)(2,1)S(1)} %get-tuple-element.53), channel_id=1, source_target_pairs={{0,32},{32,0},{64,96},{96,64},{128,160},{160,128},{192,224},{224,1... | collective-permute-start | bytes 393224 | tf_op jit(solution)/shard_map/ppermute | solution.py:425
  19.5 8.7 %collective-permute-start.5 = (bf16[192,256]{1,0:T(8,128)(2,1)S(1)}, bf16[192,256]{1,0:T(8,128)(2,1)S(1)}, u32[]{:S(2)}, u32[]{:S(2)}) collective-permute-start(bf16[192,256]{1,0:T(8,128)(2,1)S(1)} %get-tuple-element.55), channel_id=1, source_target_pairs={{0,96},{32,64},{64,32},{96,0},{128,224},{160,192},{192,160},{224,1... | collective-permute-start | bytes 294920 | tf_op jit(solution)/shard_map/ppermute | solution.py:425
  22.3 5.9 %collective-permute-start.4 = (bf16[64,256]{1,0:T(8,128)(2,1)S(1)}, bf16[64,256]{1,0:T(8,128)(2,1)S(1)}, u32[]{:S(2)}, u32[]{:S(2)}) collective-permute-start(bf16[64,256]{1,0:T(8,128)(2,1)S(1)} %get-tuple-element.54), channel_id=1, source_target_pairs={{0,64},{32,96},{64,0},{96,32},{128,192},{160,224},{192,128},{224,1... | collective-permute-start | bytes 98312 | tf_op jit(solution)/shard_map/ppermute | solution.py:425
  29.1 8.2 %collective-permute-start.6 = (bf16[256,256]{1,0:T(8,128)(2,1)S(1)}, bf16[256,256]{1,0:T(8,128)(2,1)S(1)}, u32[]{:S(2)}, u32[]{:S(2)}) collective-permute-start(bf16[256,256]{1,0:T(8,128)(2,1)S(1)} %shard_map.79), channel_id=1, source_target_pairs={{0,224},{32,192},{64,160},{96,128},{128,96},{160,64},{192,32},{224... | collective-permute-start | bytes 393224 | tf_op jit(solution)/shard_map/ppermute | solution.py:425
  38.7 8.0 %collective-permute-start.7 = (bf16[256,256]{1,0:T(8,128)(2,1)S(1)}, bf16[256,256]{1,0:T(8,128)(2,1)S(1)}, u32[]{:S(2)}, u32[]{:S(2)}) collective-permute-start(bf16[256,256]{1,0:T(8,128)(2,1)S(1)} %get-tuple-element.72), channel_id=1, source_target_pairs={{0,224},{32,192},{64,160},{96,128},{128,96},{160,64},{192,32},{224... | collective-permute-start | bytes 393224 | tf_op jit(solution)/shard_map/ppermute | solution.py:425
  47.4 9.7 %collective-permute-start.8 = (bf16[256,256]{1,0:T(8,128)(2,1)S(1)}, bf16[256,256]{1,0:T(8,128)(2,1)S(1)}, u32[]{:S(2)}, u32[]{:S(2)}) collective-permute-start(bf16[256,256]{1,0:T(8,128)(2,1)S(1)} %get-tuple-element.82), channel_id=1, source_target_pairs={{0,32},{32,0},{64,96},{96,64},{128,160},{160,128},{192,224},{224,1... | collective-permute-start | bytes 393224 | tf_op jit(solution)/shard_map/ppermute | solution.py:425
  48.5 8.7 %collective-permute-start.10 = (bf16[192,256]{1,0:T(8,128)(2,1)S(1)}, bf16[192,256]{1,0:T(8,128)(2,1)S(1)}, u32[]{:S(2)}, u32[]{:S(2)}) collective-permute-start(bf16[192,256]{1,0:T(8,128)(2,1)S(1)} %get-tuple-element.84), channel_id=1, source_target_pairs={{0,96},{32,64},{64,32},{96,0},{128,224},{160,192},{192,160},{224,1... | collective-permute-start | bytes 294920 | tf_op jit(solution)/shard_map/ppermute | solution.py:425
  50.4 6.7 %collective-permute-start.9 = (bf16[64,256]{1,0:T(8,128)(2,1)S(1)}, bf16[64,256]{1,0:T(8,128)(2,1)S(1)}, u32[]{:S(2)}, u32[]{:S(2)}) collective-permute-start(bf16[64,256]{1,0:T(8,128)(2,1)S(1)} %get-tuple-element.83), channel_id=1, source_target_pairs={{0,64},{32,96},{64,0},{96,32},{128,192},{160,224},{192,128},{224,1... | collective-permute-start | bytes 98312 | tf_op jit(solution)/shard_map/ppermute | solution.py:425
  52.5 12.9 %all-to-all-start.1 = ((bf16[4,256,256]{2,1,0:T(8,128)(2,1)}), bf16[4,256,256]{2,1,0:T(8,128)(2,1)S(1)}, u32[]{:S(2)}, u32[]{:S(2)}) async-start(bf16[4,256,256]{2,1,0:T(8,128)(2,1)} %bitcast.4), calls=%async_computation.1 | async-start | bytes 1048576 | tf_op jit(solution)/shard_map/all_to_all | solution.py:421
  58.4 8.3 %collective-permute-start.11 = (bf16[256,256]{1,0:T(8,128)(2,1)S(1)}, bf16[256,256]{1,0:T(8,128)(2,1)S(1)}, u32[]{:S(2)}, u32[]{:S(2)}) collective-permute-start(bf16[256,256]{1,0:T(8,128)(2,1)S(1)} %get-tuple-element.86), channel_id=1, source_target_pairs={{0,8},{8,16},{16,24},{24,0},{1,9},{9,17},{17,25},{25,1},{2,10},{10... | collective-permute-start | bytes 393224 | tf_op jit(solution)/shard_map/ppermute | solution.py:416
  60.5 7.6 %collective-permute-start.12 = (bf16[256,256]{1,0:T(8,128)(2,1)S(1)}, bf16[256,256]{1,0:T(8,128)(2,1)S(1)}, u32[]{:S(2)}, u32[]{:S(2)}) collective-permute-start(bf16[256,256]{1,0:T(8,128)(2,1)S(1)} %get-tuple-element.87), channel_id=1, source_target_pairs={{0,16},{8,24},{16,0},{24,8},{1,17},{9,25},{17,1},{25,9},{2,18},{10... | collective-permute-start | bytes 393224 | tf_op jit(solution)/shard_map/ppermute | solution.py:416
  63.2 5.0 %collective-permute-start.13 = (bf16[256,256]{1,0:T(8,128)(2,1)S(1)}, bf16[256,256]{1,0:T(8,128)(2,1)S(1)}, u32[]{:S(2)}, u32[]{:S(2)}) collective-permute-start(bf16[256,256]{1,0:T(8,128)(2,1)S(1)} %get-tuple-element.88), channel_id=1, source_target_pairs={{0,24},{8,0},{16,8},{24,16},{1,25},{9,1},{17,9},{25,17},{2,26},{10... | collective-permute-start | bytes 393224 | tf_op jit(solution)/shard_map/ppermute | solution.py:416

commit v3 on v2

--- a/solution.py
+++ b/solution.py
@@ -18,7 +18,6 @@
 PLANE = NY * PIECE
 SMALL = PIECE // 8
 Y_ORDER = (1, 2, 3)
-EARLY_OUT = False
 POOL = 5 * 10**9
 FINAL = 5*10**9
 EARLY_STACK = True
@@ -77,9 +76,9 @@
     return lax.rem(y - d + NY, NY)
 
 
-def pack_kernel(at_ref, left_hbm, right_hbm, *refs):
+def pack_kernel(left_hbm, right_hbm, *refs):
     outs, sems = refs[:NY], refs[-1]
-    y = at_ref[0]
+    y = lax.axis_index("y")
     copies = [
         pltpu.make_async_copy(
             src.at[:, head_at(later(y, d))], outs[d].at[:, n * D : (n + 1) * D], sems.at[d, n]
@@ -93,7 +92,7 @@
         copy.wait()
 
 
-def stack_kernel(at_ref, left_hbm, right_hbm, out_ref, sems):
+def stack_kernel(left_hbm, right_hbm, out_ref, sems):
     copies = [
         pltpu.make_async_copy(
             src.at[:, h * D : (h + 1) * D],
@@ -109,7 +108,7 @@
         copy.wait()
 
 
-def unstack_kernel(at_ref, in_ref, left_hbm, right_hbm, token_ref, sems):
+def unstack_kernel(in_ref, left_hbm, right_hbm, token_ref, sems):
     token_ref[...] = jnp.zeros_like(token_ref)
     copies = [
         pltpu.make_async_copy(
@@ -126,9 +125,9 @@
         copy.wait()
 
 
-def unpack_kernel(at_ref, *refs):
+def unpack_kernel(*refs):
     pieces, left_hbm, right_hbm, sems = refs[:NY], refs[NY], refs[NY + 1], refs[-1]
-    y = at_ref[0]
+    y = lax.axis_index("y")
     copies = [
         pltpu.make_async_copy(
             pieces[d].at[:, n * D : (n + 1) * D], dst.at[:, head_at(earlier(y, d))], sems.at[d, n]
@@ -142,9 +141,9 @@
         copy.wait()
 
 
-def pool_kernel(at_ref, k0, k1, k2, k3, kv_ref, m1_ref, m2_ref, m3_ref, tail_ref):
-    y = at_ref[0]
-    odd = lax.rem(at_ref[1], 2)
+def pool_kernel(k0, k1, k2, k3, kv_ref, m1_ref, m2_ref, m3_ref, tail_ref):
+    y = lax.axis_index("y")
+    odd = lax.rem(lax.axis_index("z"), 2)
     for d, ref in enumerate((k0, k1, k2, k3)):
         kv_ref[part_at(earlier(y, d)), :] = ref[...]
     matrix = pair_sum(B)
@@ -163,8 +162,8 @@
     tail_ref[HALF:] = other
 
 
-def quad_kernel(at_ref, tail_ref, three_1, four_2, four_3, top_ref):
-    z = at_ref[1]
+def quad_kernel(tail_ref, three_1, four_2, four_3, top_ref):
+    z = lax.axis_index("z")
     matrix = pair_sum(HALF)
     small = matrix[: B // 4, :HALF]
     fours = (tail_ref[:HALF], pool(matrix, three_1[:B]), four_2[...], four_3[:HALF])
@@ -193,7 +192,7 @@
 
 
 def early_kernel(
-    at_ref, kv, from_1, from_2, from_3, qc, keys_t, vals_t, raised, pgrads, stats, keys, vals
+    kv, from_1, from_2, from_3, qc, keys_t, vals_t, raised, pgrads, stats, keys, vals
 ):
     matrix = pair_sum(B)
     one = [pool(matrix, kv[n * PIECE : (n + 1) * PIECE]) for n in range(4)]
@@ -237,9 +236,9 @@
 
 
 def late_kernel(
-    at_ref, from_1, from_3, from_7, qc, stats, top_ref, g_facing, g_other, edges, found, w5, s5, ew, es
+    from_1, from_3, from_7, qc, stats, top_ref, g_facing, g_other, edges, found, w5, s5, ew, es
 ):
-    z = at_ref[1]
+    z = lax.axis_index("z")
     odd = lax.rem(z, 2)
     edges[1 - odd] = from_1[B:]
     edges[odd] = jnp.where(by_three(z), from_3[HALF:], from_7[B:])
@@ -297,7 +296,7 @@
 
 
 def rest_kernel(
-    at_ref, keys_t, vals_t, raised, pgrads, qc, from_7, edges, found, w5, s5, ew, es,
+    keys_t, vals_t, raised, pgrads, qc, from_7, edges, found, w5, s5, ew, es,
     og, g4, g3, g_own, g_one, g_two, grads,
 ):
     grads[...] = jnp.zeros_like(grads)
@@ -333,9 +332,9 @@
 
 
 def spread_kernel(
-    at_ref, back_ref, g4_ref, g3_ref, facing_ref, other_ref, s1_ref, s2_ref, s3_ref, keep_ref
+    back_ref, g4_ref, g3_ref, facing_ref, other_ref, s1_ref, s2_ref, s3_ref, keep_ref
 ):
-    z = at_ref[1]
+    z = lax.axis_index("z")
     twice = repeat_matrix(B // 4, 1)
     fourfold = repeat_matrix(B // 4, 2)
 
@@ -350,7 +349,7 @@
     keep_ref[...] = dot(fourfold, rows(0)) * 0.5
 
 
-def local_kernel(at_ref, own_ref, one_ref, two_ref, out_ref, *_):
+def local_kernel(own_ref, one_ref, two_ref, out_ref, *_):
     matrix = repeat_matrix(B, 1)
     for n in range(2):
         two = expand(matrix, two_ref[n * B : (n + 1) * B] * ROOT_HALF)
@@ -361,9 +360,9 @@
             out_ref[cut] = own_ref[cut] + expand(matrix, one * ROOT_HALF)
 
 
-def final_kernel(at_ref, own_ref, keep_ref, b1_ref, b2_ref, b3_ref, b7_ref, f0, f1, f2, f3, total):
-    y = at_ref[0]
-    z = at_ref[1]
+def final_kernel(own_ref, keep_ref, b1_ref, b2_ref, b3_ref, b7_ref, f0, f1, f2, f3, total):
+    y = lax.axis_index("y")
+    z = lax.axis_index("z")
     odd = lax.rem(z, 2)
     four = (b2_ref[...].astype(F32) + b3_ref[:HALF].astype(F32)) * ROOT_HALF
     up = keep_ref[...] + b1_ref[:B].astype(F32) + expand(repeat_matrix(HALF, 1), four)
@@ -381,7 +380,6 @@
 
 
 VMEM = pl.BlockSpec(memory_space=pltpu.VMEM)
-SMEM = pl.BlockSpec(memory_space=pltpu.SMEM)
 ANY = pl.BlockSpec(memory_space=pl.ANY)
 HBM = pl.BlockSpec(memory_space=pltpu.HBM)
 
@@ -400,7 +398,7 @@
     return pl.pallas_call(
         body,
         out_shape=[jax.ShapeDtypeStruct(s, t) for s, t in outs],
-        in_specs=[SMEM] + [source] * (count - 1) + [ANY] * len(after),
+        in_specs=[source] * count + [ANY] * len(after),
         out_specs=[target if s != TOKEN else VMEM for s in outs[: len(outs) - bool(alias)]]
         + [ANY] * bool(alias),
         scratch_shapes=list(scratch),
@@ -426,7 +424,6 @@
 
 
 def per_device(queries, keys, values, cotangent):
-    at = jnp.stack([lax.axis_index("y"), lax.axis_index("z")]).astype(jnp.int32)
     piece = ((PIECE, 2 * D), BF)
     plane = ((PLANE, 2 * D), BF)
     level = ((B, 2 * D), BF)
@@ -435,23 +432,23 @@
     double = ((2 * B, 2 * D), BF)
     wide = ((B, 2 * D), F32)
     sems = [pltpu.SemaphoreType.DMA((NY, 2))]
-    kv = call(pack_kernel, [at, keys, values], [piece] * NY, scratch=sems, source=HBM)
+    kv = call(pack_kernel, [keys, values], [piece] * NY, scratch=sems, source=HBM, flops=5 * 10**9)
     kv = around_y(kv)
-    (qc_own,) = call(stack_kernel, [at, queries, cotangent], [plane], scratch=sems, source=HBM)
+    (qc_own,) = call(stack_kernel, [queries, cotangent], [plane], scratch=sems, source=HBM)
     qc = across_y(qc_own)
     kv, m1, m2, m3, own_tail = call(
         pool_kernel,
-        [at, *kv],
+        [*kv],
         [plane, double, half, tail, tail],
         flops=POOL,
         after=[qc_own] if EARLY_STACK else [],
     )
     from_1, from_2, from_3 = over_z(m1, 1), over_z(m2, 2), over_z(m3, 3)
-    (top,) = call(quad_kernel, [at, own_tail, from_1, from_2, from_3], [double])
+    (top,) = call(quad_kernel, [own_tail, from_1, from_2, from_3], [double])
     from_7 = over_z(top, 7)
     keys_t, vals_t, raised, pgrads, stats = call(
         early_kernel,
-        [at, kv, from_1, from_2, from_3, qc],
+        [kv, from_1, from_2, from_3, qc],
         [((D, COLS), BF)] * 2 + [((NY, PAIR, PIECE), F32)] * 2 + [((8, PLANE), F32)],
         scratch=[pltpu.VMEM((COLS, D), BF)] * 2,
         flops=10**9,
@@ -459,7 +456,7 @@
     )
     g_top, g_facing, g_other, edges, found, w5, s5, ew, es = call(
         late_kernel,
-        [at, from_1, from_3, from_7, qc, stats],
+        [from_1, from_3, from_7, qc, stats],
         [double, level, level, ((2, B, 2 * D), BF), ((8, PLANE), F32)]
         + [((B, PLANE), BF)] * 2
         + [((2, B, PIECE), BF)] * 2,
@@ -467,7 +464,7 @@
     )
     og, g4, g3, g_own, g_one, g_two = call(
         rest_kernel,
-        [at, keys_t, vals_t, raised, pgrads, qc, from_7, edges, found, w5, s5, ew, es],
+        [keys_t, vals_t, raised, pgrads, qc, from_7, edges, found, w5, s5, ew, es],
         [plane, wide, wide]
         + [((PLANE, 2 * D), F32), ((PLANE // 2, 2 * D), F32), ((PLANE // 4, 2 * D), F32)],
         scratch=[pltpu.VMEM((COLS, 2 * D), F32)],
@@ -477,32 +474,32 @@
     back_7 = over_z(g_top, 7)
     s1, s2, s3, keep = call(
         spread_kernel,
-        [at, back_7, g4, g3, g_facing, g_other],
+        [back_7, g4, g3, g_facing, g_other],
         [double, half, tail, wide],
     )
     own, og = call(
         local_kernel,
-        [at, g_own, g_one, g_two],
+        [g_own, g_one, g_two],
         [((PLANE, 2 * D), F32), plane],
         after=[og, keep],
-        alias={4: 1},
+        alias={3: 1},
     )
     og = across_y(og)
     back_1, back_2, back_3 = over_z(s1, 1), over_z(s2, 2), over_z(s3, 3)
     whole = ((PIECE, NY * D), BF)
     attended, grad_queries, token = call(
-        unstack_kernel, [at, og], [whole] * 2 + [TOKEN], scratch=sems, target=HBM
+        unstack_kernel, [og], [whole] * 2 + [TOKEN], scratch=sems, target=HBM
     )
     final = call(
         final_kernel,
-        [at, own, keep, back_1, back_2, back_3, back_7],
+        [own, keep, back_1, back_2, back_3, back_7],
         [piece] * NY,
         scratch=[pltpu.VMEM((PLANE, 2 * D), F32)],
         flops=FINAL,
     )
     final = around_y(final)
     grad_keys, grad_values = call(
-        unpack_kernel, [at, *final], [whole] * 2, scratch=sems, target=HBM, after=[token]
+        unpack_kernel, [*final], [whole] * 2, scratch=sems, target=HBM, after=[token]
     )
     return attended, grad_queries, grad_keys, grad_values
 

time: 70 us -> 63.6 us (0.909)
  Pallas kernels: 18.2 us -> 11.5 us
  waiting for transfers between devices: 9.73 us -> 12 us
  local copies, waits for them, and re-layouts: 3.8 us -> 1.94 us
    pallas_call x12, Pallas kernels: 18.2 us -> 11.5 us  [call(): pl.pallas_call(body, out_shape=[jax.ShapeDtypeStruct(s, t) for s, t in ou...]
    unnamed x8, local copies, waits for them, and re-layouts: 3.8 us -> 1.94 us
    ppermute x8, waiting for transfers between devices: 7.61 us -> 8.67 us  [over_z(): return lax.ppermute(array, 'z', [(i, i ^ d) for i in range(NZ)])]
  transfers between devices with their start and end apart: 16 -> 16, of which waited for: 6 -> 7; matrix products, arithmetic and copies ran while one was open for 0% -> 0% of each run, Pallas kernels for 20% -> 15%
where the time goes in v3:
time: 63.6 us; the launch traced here: 63.4 us
  starting transfers between devices  37 us (58%)
  waiting for transfers between devices  12 us (19%)
  Pallas kernels  11.5 us (18%)
  local copies, waits for them, and re-layouts  1.94 us (3%)
  between operations  0.92 us (1%)
    ppermute x8, starting transfers between devices, over_z(): return lax.ppermute(array, 'z', [(i, i ^ d) for i in range(NZ)])  17 us
    ppermute x6, starting transfers between devices, around_y(): lax.ppermute(pieces[d], 'y', [(i, (i + d) % NY) for i in range(NY)])  12.1 us
    pallas_call x12, Pallas kernels, call(): pl.pallas_call(body, out_shape=[jax.ShapeDtypeStruct(s, t) for s, t in ou...  11.5 us
    ppermute x8, waiting for transfers between devices, over_z(): return lax.ppermute(array, 'z', [(i, i ^ d) for i in range(NZ)])  8.67 us
    all_to_all x2, starting transfers between devices, across_y(): return lax.all_to_all(array, 'y', split_axis=0, concat_axis=0, tiled=True)  7.83 us
    ppermute x6, waiting for transfers between devices, around_y(): lax.ppermute(pieces[d], 'y', [(i, (i + d) % NY) for i in range(NY)])  2.07 us
    unnamed x8, local copies, waits for them, and re-layouts  1.94 us
  transfers between devices with their start and end apart: 16, of which 7 were waited for; matrix products, arithmetic and copies ran while one was open for 0% of the time, Pallas kernels for 15%

profile of v3, /device:TPU:6, one launch (start us, length us, event | category | flops | bytes accessed | tf_op | source)
XLA Modules:
  0.0 63.4 jit_solution(7587671351534223388)
XLA Ops:
  0.6 0.0 copy-start.1
  0.6 0.0 copy-start.2
  0.7 1.0 %copy-done.2 = bf16[256,512]{1,0:T(8,128)(2,1)S(1)} copy-done((bf16[256,512]{1,0:T(8,128)(2,1)S(1)}, bf16[256,512]{1,0:T(8,128)(2,1)}, u32[]{:S(2)}) %copy-start.2) | copy-done | bytes 262168
  1.6 0.9 %copy-done.3 = bf16[256,512]{1,0:T(8,128)(2,1)S(1)} copy-done((bf16[256,512]{1,0:T(8,128)(2,1)S(1)}, bf16[256,512]{1,0:T(8,128)(2,1)}, u32[]{:S(2)}) %copy-start.3) | copy-done | bytes 262168
  2.6 0.2 shard_map.75
  2.8 1.7 %collective-permute-start = (bf16[256,256]{1,0:T(8,128)(2,1)S(1)}, bf16[256,256]{1,0:T(8,128)(2,1)S(1)}, u32[]{:S(2)}, u32[]{:S(2)}) collective-permute-start(bf16[256,256]{1,0:T(8,128)(2,1)S(1)} %get-tuple-element.49), channel_id=1, source_target_pairs={{0,8},{8,16},{16,24},{24,0},{1,9},{9,17},{17,25},{25,1},{2,10},{10... | collective-permute-start | bytes 393224 | tf_op jit(solution)/shard_map/ppermute | solution.py:414
  4.4 2.9 %collective-permute-start.1 = (bf16[256,256]{1,0:T(8,128)(2,1)S(1)}, bf16[256,256]{1,0:T(8,128)(2,1)S(1)}, u32[]{:S(2)}, u32[]{:S(2)}) collective-permute-start(bf16[256,256]{1,0:T(8,128)(2,1)S(1)} %get-tuple-element.50), channel_id=1, source_target_pairs={{0,16},{8,24},{16,0},{24,8},{1,17},{9,25},{17,1},{25,9},{2,18},{10... | collective-permute-start | bytes 393224 | tf_op jit(solution)/shard_map/ppermute | solution.py:414
  7.3 1.3 %collective-permute-start.2 = (bf16[256,256]{1,0:T(8,128)(2,1)S(1)}, bf16[256,256]{1,0:T(8,128)(2,1)S(1)}, u32[]{:S(2)}, u32[]{:S(2)}) collective-permute-start(bf16[256,256]{1,0:T(8,128)(2,1)S(1)} %get-tuple-element.51), channel_id=1, source_target_pairs={{0,24},{8,0},{16,8},{24,16},{1,25},{9,1},{17,9},{25,17},{2,26},{10... | collective-permute-start | bytes 393224 | tf_op jit(solution)/shard_map/ppermute | solution.py:414
  8.7 1.0 %shard_map.76.refs_4_ = bf16[1024,256]{1,0:T(8,128)(2,1)} custom-call(bf16[256,512]{1,0:T(8,128)(2,1)S(1)} %copy-done, bf16[256,512]{1,0:T(8,128)(2,1)S(1)} %copy-done.1), custom_call_target="tpu_custom_call" | custom-call | flops 1000000 | bytes 1048576 | tf_op jit(solution)/shard_map/pallas_call | solution.py:398
  9.7 3.5 %all-to-all-start = ((bf16[4,256,256]{2,1,0:T(8,128)(2,1)}), bf16[4,256,256]{2,1,0:T(8,128)(2,1)S(1)}, u32[]{:S(2)}, u32[]{:S(2)}) async-start(bf16[4,256,256]{2,1,0:T(8,128)(2,1)} %bitcast), calls=%async_computation | async-start | bytes 1048576 | tf_op jit(solution)/shard_map/all_to_all | solution.py:419
  13.2 0.0 collective-permute-done.refs_1_
  13.2 0.2 collective-permute-done.1.refs_2_
  13.4 0.0 collective-permute-done.2.refs_3_
  13.4 0.7 %shard_map.77 = (bf16[1024,256]{1,0:T(8,128)(2,1)S(1)}, bf16[256,256]{1,0:T(8,128)(2,1)S(1)}, bf16[64,256]{1,0:T(8,128)(2,1)S(1)}, bf16[192,256]{1,0:T(8,128)(2,1)S(1)}, bf16[192,256]{1,0:T(8,128)(2,1)S(1)}) custom-call(bf16[256,256]{1,0:T(8,128)(2,1)S(1)} %get-tuple-element.48.refs_0_, bf16[256,256]{1,0:T(8,128)(2,1)S(1)} %collective-permute-done.refs_1_, ...), custom_call_target="tpu_custom_call" | custom-call | flops 5000000000 | bytes 1409024 | tf_op jit(solution)/shard_map/pallas_call | solution.py:398
  14.1 2.0 %collective-permute-start.3 = (bf16[256,256]{1,0:T(8,128)(2,1)S(1)}, bf16[256,256]{1,0:T(8,128)(2,1)S(1)}, u32[]{:S(2)}, u32[]{:S(2)}) collective-permute-start(bf16[256,256]{1,0:T(8,128)(2,1)S(1)} %get-tuple-element.53), channel_id=1, source_target_pairs={{0,32},{32,0},{64,96},{96,64},{128,160},{160,128},{192,224},{224,1... | collective-permute-start | bytes 393224 | tf_op jit(solution)/shard_map/ppermute | solution.py:423
  16.1 2.8 %collective-permute-start.5 = (bf16[192,256]{1,0:T(8,128)(2,1)S(1)}, bf16[192,256]{1,0:T(8,128)(2,1)S(1)}, u32[]{:S(2)}, u32[]{:S(2)}) collective-permute-start(bf16[192,256]{1,0:T(8,128)(2,1)S(1)} %get-tuple-element.55), channel_id=1, source_target_pairs={{0,96},{32,64},{64,32},{96,0},{128,224},{160,192},{192,160},{224,1... | collective-permute-start | bytes 294920 | tf_op jit(solution)/shard_map/ppermute | solution.py:423
  18.9 0.5 collective-permute-start.4
  19.4 5.4 %collective-permute-done.4.refs_2_ = bf16[64,256]{1,0:T(8,128)(2,1)S(1)} collective-permute-done((bf16[64,256]{1,0:T(8,128)(2,1)S(1)}, bf16[64,256]{1,0:T(8,128)(2,1)S(1)}, u32[]{:S(2)}, u32[]{:S(2)}) %collective-permute-start.4) | collective-permute-done | bytes 32800 | tf_op jit(solution)/shard_map/ppermute | solution.py:423
  24.8 0.0 collective-permute-done.5.refs_3_.refs_1_
  24.8 0.0 collective-permute-done.3.refs_1_.refs_0_
  24.8 0.3 shard_map.79
  25.1 4.2 %collective-permute-start.6 = (bf16[256,256]{1,0:T(8,128)(2,1)S(1)}, bf16[256,256]{1,0:T(8,128)(2,1)S(1)}, u32[]{:S(2)}, u32[]{:S(2)}) collective-permute-start(bf16[256,256]{1,0:T(8,128)(2,1)S(1)} %shard_map.79), channel_id=1, source_target_pairs={{0,224},{32,192},{64,160},{96,128},{128,96},{160,64},{192,32},{224... | collective-permute-start | bytes 393224 | tf_op jit(solution)/shard_map/ppermute | solution.py:423
  29.3 0.0 all-to-all-done
  29.3 1.9 %shard_map.78 = (bf16[128,2048]{1,0:T(8,128)(2,1)S(1)}, bf16[128,2048]{1,0:T(8,128)(2,1)S(1)}, f32[4,1024,256]{2,1,0:T(8,128)S(1)}, f32[4,1024,256]{2,1,0:T(8,128)S(1)}, f32[8,1024]{1,0:T(8,128)S(1)}) custom-call(bf16[1024,256]{1,0:T(8,128)(2,1)S(1)} %get-tuple-element.52.refs_0_, bf16[256,256]{1,0:T(8,128)(2,1)S(1)} %collective-permute-done.3.refs_1_.refs_0_, ...), custom_call_target="tpu_custom_call" | custom-call | flops 1000000000 | bytes 10780672 | tf_op jit(solution)/shard_map/pallas_call | solution.py:398
  31.3 2.3 %collective-permute-done.6.refs_2_.refs_5_ = bf16[256,256]{1,0:T(8,128)(2,1)S(1)} collective-permute-done((bf16[256,256]{1,0:T(8,128)(2,1)S(1)}, bf16[256,256]{1,0:T(8,128)(2,1)S(1)}, u32[]{:S(2)}, u32[]{:S(2)}) %collective-permute-start.6) | collective-permute-done | bytes 131104 | tf_op jit(solution)/shard_map/ppermute | solution.py:423
  33.6 0.9 %shard_map.80 = (bf16[256,256]{1,0:T(8,128)(2,1)S(1)}, bf16[128,256]{1,0:T(8,128)(2,1)S(1)}, bf16[128,256]{1,0:T(8,128)(2,1)S(1)}, bf16[2,128,256]{2,1,0:T(8,128...) custom-call(bf16[256,256]{1,0:T(8,128)(2,1)S(1)} %collective-permute, ...), custom_call_target="tpu_custom_call" | custom-call | flops 100000000 | bytes 2129920 | tf_op jit(solution)/shard_map/pallas_call | solution.py:398
  34.5 3.9 %collective-permute-start.7 = (bf16[256,256]{1,0:T(8,128)(2,1)S(1)}, bf16[256,256]{1,0:T(8,128)(2,1)S(1)}, u32[]{:S(2)}, u32[]{:S(2)}) collective-permute-start(bf16[256,256]{1,0:T(8,128)(2,1)S(1)} %get-tuple-element.72), channel_id=1, source_target_pairs={{0,224},{32,192},{64,160},{96,128},{128,96},{160,64},{192,32},{224... | collective-permute-start | bytes 393224 | tf_op jit(solution)/shard_map/ppermute | solution.py:423
  38.4 3.0 %shard_map.81 = (bf16[1024,256]{1,0:T(8,128)(2,1)}, f32[128,256]{1,0:T(8,128)S(1)}, f32[128,256]{1,0:T(8,128)S(1)}, f32[1024,256]{1,0:T(8,128)S(1)}, f32[512,256]{1,0:T(8,128)S(1)}, /*index=5*/f32[256,256]{1,0:T(8,128)S(1)}) custom-call(bf16[128,2048]{1,0:T(8,128)(2,1)S(1)} %get-tuple-element.56.refs_0_, bf16[128,2048]{1,0:T(8,128)(2,1)S(1)} %get-tuple-element.57.refs_1_, ...), custom_call_target="tpu_custom_call" | custom-call | flops 2000000000 | bytes 13664256 | tf_op jit(solution)/shard_map/pallas_call | solution.py:398
  41.4 1.0 %collective-permute-done.7.refs_0_.refs_5_ = bf16[256,256]{1,0:T(8,128)(2,1)S(1)} collective-permute-done((bf16[256,256]{1,0:T(8,128)(2,1)S(1)}, bf16[256,256]{1,0:T(8,128)(2,1)S(1)}, u32[]{:S(2)}, u32[]{:S(2)}) %collective-permute-start.7) | collective-permute-done | bytes 131104 | tf_op jit(solution)/shard_map/ppermute | solution.py:423
  42.4 0.2 shard_map.82
  42.6 0.4 collective-permute-start.8
  43.0 2.6 %collective-permute-start.10 = (bf16[192,256]{1,0:T(8,128)(2,1)S(1)}, bf16[192,256]{1,0:T(8,128)(2,1)S(1)}, u32[]{:S(2)}, u32[]{:S(2)}) collective-permute-start(bf16[192,256]{1,0:T(8,128)(2,1)S(1)} %get-tuple-element.84), channel_id=1, source_target_pairs={{0,96},{32,64},{64,32},{96,0},{128,224},{160,192},{192,160},{224,1... | collective-permute-start | bytes 294920 | tf_op jit(solution)/shard_map/ppermute | solution.py:423
  45.6 0.6 collective-permute-start.9
  46.1 0.9 %shard_map.83 = (f32[1024,256]{1,0:T(8,128)S(1)}, bf16[1024,256]{1,0:T(8,128)(2,1)}) custom-call(f32[1024,256]{1,0:T(8,128)S(1)} %get-tuple-element.68.refs_0_, f32[512,256]{1,0:T(8,128)S(1)} %get-tuple-element.69.refs_1_, f32[256,256]{1,0:T(8,128)S(1)} %get-tuple-element.70.refs_2_, ...), custom_call_target="tpu_custom_call", output_to_operand_aliasing={{1}: (3, {})} | custom-call | flops 1000000 | bytes 3407872 | tf_op jit(solution)/shard_map/pallas_call | solution.py:398
  47.1 4.3 %all-to-all-start.1 = ((bf16[4,256,256]{2,1,0:T(8,128)(2,1)}), bf16[4,256,256]{2,1,0:T(8,128)(2,1)S(1)}, u32[]{:S(2)}, u32[]{:S(2)}) async-start(bf16[4,256,256]{2,1,0:T(8,128)(2,1)} %bitcast.2), calls=%async_computation.1 | async-start | bytes 1048576 | tf_op jit(solution)/shard_map/all_to_all | solution.py:419
  51.4 0.0 collective-permute-done.9.refs_3_
  51.4 0.0 collective-permute-done.10.refs_4_
  51.4 0.0 collective-permute-done.8.refs_2_
  51.4 0.7 %shard_map.85 = (bf16[256,256]{1,0:T(8,128)(2,1)S(1)}, bf16[256,256]{1,0:T(8,128)(2,1)S(1)}, bf16[256,256]{1,0:T(8,128)(2,1)S(1)}, bf16[256,256]{1,0:T(8,128)(2,1)S(1)}) custom-call(f32[1024,256]{1,0:T(8,128)S(1)} %get-tuple-element.81.refs_0_, f32[128,256]{1,0:T(8,128)S(1)} %get-tuple-element.77.refs_4_.refs_1_, ...), custom_call_target="tpu_custom_call" | custom-call | flops 5000000000 | bytes 2097152 | tf_op jit(solution)/shard_map/pallas_call | solution.py:398
  52.1 2.1 %collective-permute-start.11 = (bf16[256,256]{1,0:T(8,128)(2,1)S(1)}, bf16[256,256]{1,0:T(8,128)(2,1)S(1)}, u32[]{:S(2)}, u32[]{:S(2)}) collective-permute-start(bf16[256,256]{1,0:T(8,128)(2,1)S(1)} %get-tuple-element.86), channel_id=1, source_target_pairs={{0,8},{8,16},{16,24},{24,0},{1,9},{9,17},{17,25},{25,1},{2,10},{10... | collective-permute-start | bytes 393224 | tf_op jit(solution)/shard_map/ppermute | solution.py:414
  54.2 2.7 %collective-permute-start.12 = (bf16[256,256]{1,0:T(8,128)(2,1)S(1)}, bf16[256,256]{1,0:T(8,128)(2,1)S(1)}, u32[]{:S(2)}, u32[]{:S(2)}) collective-permute-start(bf16[256,256]{1,0:T(8,128)(2,1)S(1)} %get-tuple-element.87), channel_id=1, source_target_pairs={{0,16},{8,24},{16,0},{24,8},{1,17},{9,25},{17,1},{25,9},{2,18},{10... | collective-permute-start | bytes 393224 | tf_op jit(solution)/shard_map/ppermute | solution.py:414
  56.9 1.5 %collective-permute-start.13 = (bf16[256,256]{1,0:T(8,128)(2,1)S(1)}, bf16[256,256]{1,0:T(8,128)(2,1)S(1)}, u32[]{:S(2)}, u32[]{:S(2)}) collective-permute-start(bf16[256,256]{1,0:T(8,128)(2,1)S(1)} %get-tuple-element.88), channel_id=1, source_target_pairs={{0,24},{8,0},{16,8},{24,16},{1,25},{9,1},{17,9},{25,17},{2,26},{10... | collective-permute-start | bytes 393224 | tf_op jit(solution)/shard_map/ppermute | solution.py:414
  58.4 1.2 %all-to-all-done.1 = bf16[4,256,256]{2,1,0:T(8,128)(2,1)S(1)} async-done(((bf16[4,256,256]{2,1,0:T(8,128)(2,1)}), bf16[4,256,256]{2,1,0:T(8,128)(2,1)S(1)}, u32[]{:S(2)}, u32[]{:S(2)}) %all-to-all-start.1) | async-done | bytes 524320 | tf_op jit(solution)/shard_map/all_to_all | solution.py:419
  59.6 0.8 %shard_map.84 = (bf16[256,512]{1,0:T(8,128)(2,1)}, bf16[256,512]{1,0:T(8,128)(2,1)}, f32[8,128]{1,0:T(8,128)S(1)}) custom-call(bf16[1024,256]{1,0:T(8,128)(2,1)S(1)} %bitcast.7), custom_call_target="tpu_custom_call" | custom-call | flops 1000000 | bytes 1052672 | tf_op jit(solution)/shard_map/pallas_call | solution.py:398
  60.5 0.1 collective-permute-done.11.refs_1_
  60.6 1.7 %collective-permute-done.12.refs_2_ = bf16[256,256]{1,0:T(8,128)(2,1)S(1)} collective-permute-done((bf16[256,256]{1,0:T(8,128)(2,1)S(1)}, bf16[256,256]{1,0:T(8,128)(2,1)S(1)}, u32[]{:S(2)}, u32[]{:S(2)}) %collective-permute-start.12) | collective-permute-done | bytes 131104 | tf_op jit(solution)/shard_map/ppermute | solution.py:414
  62.4 0.0 collective-permute-done.13.refs_3_
  62.4 0.8 %shard_map.86 = (bf16[256,512]{1,0:T(8,128)(2,1)}, bf16[256,512]{1,0:T(8,128)(2,1)}) custom-call(bf16[256,256]{1,0:T(8,128)(2,1)S(1)} %get-tuple-element.85.refs_0_, bf16[256,256]{1,0:T(8,128)(2,1)S(1)} %collective-permute-done.11.refs_1_, bf16[256,256]{1,0:T(8,128)(2,1)S(1)} %collective-permute-done.12.refs_2_, ...), custom_call_target="tpu_custom_call" | custom-call | flops 1000000 | bytes 1048576 | tf_op jit(solution)/shard_map/pallas_call | solution.py:398
  (4 shorter events, 0.0 us)
Async XLA Ops:
  0.6 8.1 %copy-start.1 = (bf16[256,512]{1,0:T(8,128)(2,1)S(1)}, bf16[256,512]{1,0:T(8,128)(2,1)}, u32[]{:S(2)}) copy-start(bf16[256,512]{1,0:T(8,128)(2,1)} %refs_1_.3) | copy-start | bytes 786436
  0.6 1.0 %copy-start.2 = (bf16[256,512]{1,0:T(8,128)(2,1)S(1)}, bf16[256,512]{1,0:T(8,128)(2,1)}, u32[]{:S(2)}) copy-start(bf16[256,512]{1,0:T(8,128)(2,1)} %refs_0_.2) | copy-start | bytes 786436
  1.6 0.9 %copy-start.3 = (bf16[256,512]{1,0:T(8,128)(2,1)S(1)}, bf16[256,512]{1,0:T(8,128)(2,1)}, u32[]{:S(2)}) copy-start(bf16[256,512]{1,0:T(8,128)(2,1)} %refs_1_.2) | copy-start | bytes 786436
  2.6 6.1 %copy-start = (bf16[256,512]{1,0:T(8,128)(2,1)S(1)}, bf16[256,512]{1,0:T(8,128)(2,1)}, u32[]{:S(2)}) copy-start(bf16[256,512]{1,0:T(8,128)(2,1)} %refs_0_.3) | copy-start | bytes 786436
  2.8 10.4 %collective-permute-start = (bf16[256,256]{1,0:T(8,128)(2,1)S(1)}, bf16[256,256]{1,0:T(8,128)(2,1)S(1)}, u32[]{:S(2)}, u32[]{:S(2)}) collective-permute-start(bf16[256,256]{1,0:T(8,128)(2,1)S(1)} %get-tuple-element.49), channel_id=1, source_target_pairs={{0,8},{8,16},{16,24},{24,0},{1,9},{9,17},{17,25},{25,1},{2,10},{10... | collective-permute-start | bytes 393224 | tf_op jit(solution)/shard_map/ppermute | solution.py:414
  4.4 8.9 %collective-permute-start.1 = (bf16[256,256]{1,0:T(8,128)(2,1)S(1)}, bf16[256,256]{1,0:T(8,128)(2,1)S(1)}, u32[]{:S(2)}, u32[]{:S(2)}) collective-permute-start(bf16[256,256]{1,0:T(8,128)(2,1)S(1)} %get-tuple-element.50), channel_id=1, source_target_pairs={{0,16},{8,24},{16,0},{24,8},{1,17},{9,25},{17,1},{25,9},{2,18},{10... | collective-permute-start | bytes 393224 | tf_op jit(solution)/shard_map/ppermute | solution.py:414
  7.3 6.0 %collective-permute-start.2 = (bf16[256,256]{1,0:T(8,128)(2,1)S(1)}, bf16[256,256]{1,0:T(8,128)(2,1)S(1)}, u32[]{:S(2)}, u32[]{:S(2)}) collective-permute-start(bf16[256,256]{1,0:T(8,128)(2,1)S(1)} %get-tuple-element.51), channel_id=1, source_target_pairs={{0,24},{8,0},{16,8},{24,16},{1,25},{9,1},{17,9},{25,17},{2,26},{10... | collective-permute-start | bytes 393224 | tf_op jit(solution)/shard_map/ppermute | solution.py:414
  9.7 19.6 %all-to-all-start = ((bf16[4,256,256]{2,1,0:T(8,128)(2,1)}), bf16[4,256,256]{2,1,0:T(8,128)(2,1)S(1)}, u32[]{:S(2)}, u32[]{:S(2)}) async-start(bf16[4,256,256]{2,1,0:T(8,128)(2,1)} %bitcast), calls=%async_computation | async-start | bytes 1048576 | tf_op jit(solution)/shard_map/all_to_all | solution.py:419
  14.1 10.7 %collective-permute-start.3 = (bf16[256,256]{1,0:T(8,128)(2,1)S(1)}, bf16[256,256]{1,0:T(8,128)(2,1)S(1)}, u32[]{:S(2)}, u32[]{:S(2)}) collective-permute-start(bf16[256,256]{1,0:T(8,128)(2,1)S(1)} %get-tuple-element.53), channel_id=1, source_target_pairs={{0,32},{32,0},{64,96},{96,64},{128,160},{160,128},{192,224},{224,1... | collective-permute-start | bytes 393224 | tf_op jit(solution)/shard_map/ppermute | solution.py:423
  16.1 8.7 %collective-permute-start.5 = (bf16[192,256]{1,0:T(8,128)(2,1)S(1)}, bf16[192,256]{1,0:T(8,128)(2,1)S(1)}, u32[]{:S(2)}, u32[]{:S(2)}) collective-permute-start(bf16[192,256]{1,0:T(8,128)(2,1)S(1)} %get-tuple-element.55), channel_id=1, source_target_pairs={{0,96},{32,64},{64,32},{96,0},{128,224},{160,192},{192,160},{224,1... | collective-permute-start | bytes 294920 | tf_op jit(solution)/shard_map/ppermute | solution.py:423
  18.9 5.9 %collective-permute-start.4 = (bf16[64,256]{1,0:T(8,128)(2,1)S(1)}, bf16[64,256]{1,0:T(8,128)(2,1)S(1)}, u32[]{:S(2)}, u32[]{:S(2)}) collective-permute-start(bf16[64,256]{1,0:T(8,128)(2,1)S(1)} %get-tuple-element.54), channel_id=1, source_target_pairs={{0,64},{32,96},{64,0},{96,32},{128,192},{160,224},{192,128},{224,1... | collective-permute-start | bytes 98312 | tf_op jit(solution)/shard_map/ppermute | solution.py:423
  25.1 8.5 %collective-permute-start.6 = (bf16[256,256]{1,0:T(8,128)(2,1)S(1)}, bf16[256,256]{1,0:T(8,128)(2,1)S(1)}, u32[]{:S(2)}, u32[]{:S(2)}) collective-permute-start(bf16[256,256]{1,0:T(8,128)(2,1)S(1)} %shard_map.79), channel_id=1, source_target_pairs={{0,224},{32,192},{64,160},{96,128},{128,96},{160,64},{192,32},{224... | collective-permute-start | bytes 393224 | tf_op jit(solution)/shard_map/ppermute | solution.py:423
  34.5 7.9 %collective-permute-start.7 = (bf16[256,256]{1,0:T(8,128)(2,1)S(1)}, bf16[256,256]{1,0:T(8,128)(2,1)S(1)}, u32[]{:S(2)}, u32[]{:S(2)}) collective-permute-start(bf16[256,256]{1,0:T(8,128)(2,1)S(1)} %get-tuple-element.72), channel_id=1, source_target_pairs={{0,224},{32,192},{64,160},{96,128},{128,96},{160,64},{192,32},{224... | collective-permute-start | bytes 393224 | tf_op jit(solution)/shard_map/ppermute | solution.py:423
  42.6 8.9 %collective-permute-start.8 = (bf16[256,256]{1,0:T(8,128)(2,1)S(1)}, bf16[256,256]{1,0:T(8,128)(2,1)S(1)}, u32[]{:S(2)}, u32[]{:S(2)}) collective-permute-start(bf16[256,256]{1,0:T(8,128)(2,1)S(1)} %get-tuple-element.82), channel_id=1, source_target_pairs={{0,32},{32,0},{64,96},{96,64},{128,160},{160,128},{192,224},{224,1... | collective-permute-start | bytes 393224 | tf_op jit(solution)/shard_map/ppermute | solution.py:423
  43.0 8.5 %collective-permute-start.10 = (bf16[192,256]{1,0:T(8,128)(2,1)S(1)}, bf16[192,256]{1,0:T(8,128)(2,1)S(1)}, u32[]{:S(2)}, u32[]{:S(2)}) collective-permute-start(bf16[192,256]{1,0:T(8,128)(2,1)S(1)} %get-tuple-element.84), channel_id=1, source_target_pairs={{0,96},{32,64},{64,32},{96,0},{128,224},{160,192},{192,160},{224,1... | collective-permute-start | bytes 294920 | tf_op jit(solution)/shard_map/ppermute | solution.py:423
  45.6 5.9 %collective-permute-start.9 = (bf16[64,256]{1,0:T(8,128)(2,1)S(1)}, bf16[64,256]{1,0:T(8,128)(2,1)S(1)}, u32[]{:S(2)}, u32[]{:S(2)}) collective-permute-start(bf16[64,256]{1,0:T(8,128)(2,1)S(1)} %get-tuple-element.83), channel_id=1, source_target_pairs={{0,64},{32,96},{64,0},{96,32},{128,192},{160,224},{192,128},{224,1... | collective-permute-start | bytes 98312 | tf_op jit(solution)/shard_map/ppermute | solution.py:423
  47.1 12.5 %all-to-all-start.1 = ((bf16[4,256,256]{2,1,0:T(8,128)(2,1)}), bf16[4,256,256]{2,1,0:T(8,128)(2,1)S(1)}, u32[]{:S(2)}, u32[]{:S(2)}) async-start(bf16[4,256,256]{2,1,0:T(8,128)(2,1)} %bitcast.2), calls=%async_computation.1 | async-start | bytes 1048576 | tf_op jit(solution)/shard_map/all_to_all | solution.py:419
  52.1 8.5 %collective-permute-start.11 = (bf16[256,256]{1,0:T(8,128)(2,1)S(1)}, bf16[256,256]{1,0:T(8,128)(2,1)S(1)}, u32[]{:S(2)}, u32[]{:S(2)}) collective-permute-start(bf16[256,256]{1,0:T(8,128)(2,1)S(1)} %get-tuple-element.86), channel_id=1, source_target_pairs={{0,8},{8,16},{16,24},{24,0},{1,9},{9,17},{17,25},{25,1},{2,10},{10... | collective-permute-start | bytes 393224 | tf_op jit(solution)/shard_map/ppermute | solution.py:414
  54.2 8.1 %collective-permute-start.12 = (bf16[256,256]{1,0:T(8,128)(2,1)S(1)}, bf16[256,256]{1,0:T(8,128)(2,1)S(1)}, u32[]{:S(2)}, u32[]{:S(2)}) collective-permute-start(bf16[256,256]{1,0:T(8,128)(2,1)S(1)} %get-tuple-element.87), channel_id=1, source_target_pairs={{0,16},{8,24},{16,0},{24,8},{1,17},{9,25},{17,1},{25,9},{2,18},{10... | collective-permute-start | bytes 393224 | tf_op jit(solution)/shard_map/ppermute | solution.py:414
  56.9 5.5 %collective-permute-start.13 = (bf16[256,256]{1,0:T(8,128)(2,1)S(1)}, bf16[256,256]{1,0:T(8,128)(2,1)S(1)}, u32[]{:S(2)}, u32[]{:S(2)}) collective-permute-start(bf16[256,256]{1,0:T(8,128)(2,1)S(1)} %get-tuple-element.88), channel_id=1, source_target_pairs={{0,24},{8,0},{16,8},{24,16},{1,25},{9,1},{17,9},{25,17},{2,26},{10... | collective-permute-start | bytes 393224 | tf_op jit(solution)/shard_map/ppermute | solution.py:414

commit v4 on v3

--- a/solution.py
+++ b/solution.py
@@ -19,6 +19,7 @@
 SMALL = PIECE // 8
 Y_ORDER = (1, 2, 3)
 POOL = 5 * 10**9
+FIRST = 5 * 10**9
 FINAL = 5*10**9
 EARLY_STACK = True
 ROOT_HALF = 0.7071067811865476
@@ -74,6 +75,10 @@
 
 def earlier(y, d):
     return lax.rem(y - d + NY, NY)
+
+
+def first_kernel(token_ref):
+    token_ref[...] = jnp.zeros_like(token_ref)
 
 
 def pack_kernel(left_hbm, right_hbm, *refs):
@@ -432,7 +437,10 @@
     double = ((2 * B, 2 * D), BF)
     wide = ((B, 2 * D), F32)
     sems = [pltpu.SemaphoreType.DMA((NY, 2))]
-    kv = call(pack_kernel, [keys, values], [piece] * NY, scratch=sems, source=HBM, flops=5 * 10**9)
+    (token,) = call(first_kernel, [], [TOKEN], flops=FIRST)
+    kv = call(
+        pack_kernel, [keys, values], [piece] * NY, scratch=sems, source=HBM, flops=5 * 10**9, after=[token]
+    )
     kv = around_y(kv)
     (qc_own,) = call(stack_kernel, [queries, cotangent], [plane], scratch=sems, source=HBM)
     qc = across_y(qc_own)

time: 63.6 us -> 62.7 us (0.986)
  local copies, waits for them, and re-layouts: 1.94 us -> 1.01 us
    unnamed x8, local copies, waits for them, and re-layouts: 1.94 us -> 1.01 us
    pallas_call x12 -> x13, Pallas kernels: 11.5 us -> 11.5 us  [call(): pl.pallas_call(body, out_shape=[jax.ShapeDtypeStruct(s, t) for s, t in ou...]
where the time goes in v4:
time: 62.7 us; the launch traced here: 62.4 us
  starting transfers between devices  37 us (59%)
  waiting for transfers between devices  12 us (19%)
  Pallas kernels  11.5 us (18%)
  local copies, waits for them, and re-layouts  1.01 us (2%)
  between operations  0.93 us (1%)
    ppermute x8, starting transfers between devices, over_z(): return lax.ppermute(array, 'z', [(i, i ^ d) for i in range(NZ)])  17 us
    ppermute x6, starting transfers between devices, around_y(): lax.ppermute(pieces[d], 'y', [(i, (i + d) % NY) for i in range(NY)])  12.1 us
    pallas_call x13, Pallas kernels, call(): pl.pallas_call(body, out_shape=[jax.ShapeDtypeStruct(s, t) for s, t in ou...  11.5 us
    ppermute x8, waiting for transfers between devices, over_z(): return lax.ppermute(array, 'z', [(i, i ^ d) for i in range(NZ)])  8.67 us
    all_to_all x2, starting transfers between devices, across_y(): return lax.all_to_all(array, 'y', split_axis=0, concat_axis=0, tiled=True)  7.84 us
    ppermute x6, waiting for transfers between devices, around_y(): lax.ppermute(pieces[d], 'y', [(i, (i + d) % NY) for i in range(NY)])  2.07 us
  transfers between devices with their start and end apart: 16, of which 7 were waited for; matrix products, arithmetic and copies ran while one was open for 0% of the time, Pallas kernels for 15%

profile of v4, /device:TPU:6, one launch (start us, length us, event | category | flops | bytes accessed | tf_op | source)
XLA Modules:
  0.0 62.4 jit_solution(17954961613830313917)
XLA Ops:
  0.6 0.0 copy-start.3
  0.7 0.9 %copy-done.3 = bf16[256,512]{1,0:T(8,128)(2,1)S(1)} copy-done((bf16[256,512]{1,0:T(8,128)(2,1)S(1)}, bf16[256,512]{1,0:T(8,128)(2,1)}, u32[]{:S(2)}) %copy-start.3) | copy-done | bytes 262168
  1.6 0.1 copy-done.2
  1.7 0.2 shard_map.76
  1.9 1.7 %collective-permute-start = (bf16[256,256]{1,0:T(8,128)(2,1)S(1)}, bf16[256,256]{1,0:T(8,128)(2,1)S(1)}, u32[]{:S(2)}, u32[]{:S(2)}) collective-permute-start(bf16[256,256]{1,0:T(8,128)(2,1)S(1)} %get-tuple-element.49), channel_id=1, source_target_pairs={{0,8},{8,16},{16,24},{24,0},{1,9},{9,17},{17,25},{25,1},{2,10},{10... | collective-permute-start | bytes 393224 | tf_op jit(solution)/shard_map/ppermute | solution.py:419
  3.5 2.9 %collective-permute-start.1 = (bf16[256,256]{1,0:T(8,128)(2,1)S(1)}, bf16[256,256]{1,0:T(8,128)(2,1)S(1)}, u32[]{:S(2)}, u32[]{:S(2)}) collective-permute-start(bf16[256,256]{1,0:T(8,128)(2,1)S(1)} %get-tuple-element.50), channel_id=1, source_target_pairs={{0,16},{8,24},{16,0},{24,8},{1,17},{9,25},{17,1},{25,9},{2,18},{10... | collective-permute-start | bytes 393224 | tf_op jit(solution)/shard_map/ppermute | solution.py:419
  6.4 1.3 %collective-permute-start.2 = (bf16[256,256]{1,0:T(8,128)(2,1)S(1)}, bf16[256,256]{1,0:T(8,128)(2,1)S(1)}, u32[]{:S(2)}, u32[]{:S(2)}) collective-permute-start(bf16[256,256]{1,0:T(8,128)(2,1)S(1)} %get-tuple-element.51), channel_id=1, source_target_pairs={{0,24},{8,0},{16,8},{24,16},{1,25},{9,1},{17,9},{25,17},{2,26},{10... | collective-permute-start | bytes 393224 | tf_op jit(solution)/shard_map/ppermute | solution.py:419
  7.8 0.0 copy-done
  7.8 1.0 %shard_map.77.refs_4_ = bf16[1024,256]{1,0:T(8,128)(2,1)} custom-call(bf16[256,512]{1,0:T(8,128)(2,1)S(1)} %copy-done, bf16[256,512]{1,0:T(8,128)(2,1)S(1)} %copy-done.1), custom_call_target="tpu_custom_call" | custom-call | flops 1000000 | bytes 1048576 | tf_op jit(solution)/shard_map/pallas_call | solution.py:403
  8.8 3.5 %all-to-all-start = ((bf16[4,256,256]{2,1,0:T(8,128)(2,1)}), bf16[4,256,256]{2,1,0:T(8,128)(2,1)S(1)}, u32[]{:S(2)}, u32[]{:S(2)}) async-start(bf16[4,256,256]{2,1,0:T(8,128)(2,1)} %bitcast), calls=%async_computation | async-start | bytes 1048576 | tf_op jit(solution)/shard_map/all_to_all | solution.py:424
  12.2 0.0 collective-permute-done.refs_1_
  12.3 0.2 collective-permute-done.1.refs_2_
  12.4 0.0 collective-permute-done.2.refs_3_
  12.4 0.7 %shard_map.78 = (bf16[1024,256]{1,0:T(8,128)(2,1)S(1)}, bf16[256,256]{1,0:T(8,128)(2,1)S(1)}, bf16[64,256]{1,0:T(8,128)(2,1)S(1)}, bf16[192,256]{1,0:T(8,128)(2,1)S(1)}, bf16[192,256]{1,0:T(8,128)(2,1)S(1)}) custom-call(bf16[256,256]{1,0:T(8,128)(2,1)S(1)} %get-tuple-element.48.refs_0_, bf16[256,256]{1,0:T(8,128)(2,1)S(1)} %collective-permute-done.refs_1_, ...), custom_call_target="tpu_custom_call" | custom-call | flops 5000000000 | bytes 1409024 | tf_op jit(solution)/shard_map/pallas_call | solution.py:403
  13.2 2.0 %collective-permute-start.3 = (bf16[256,256]{1,0:T(8,128)(2,1)S(1)}, bf16[256,256]{1,0:T(8,128)(2,1)S(1)}, u32[]{:S(2)}, u32[]{:S(2)}) collective-permute-start(bf16[256,256]{1,0:T(8,128)(2,1)S(1)} %get-tuple-element.53), channel_id=1, source_target_pairs={{0,32},{32,0},{64,96},{96,64},{128,160},{160,128},{192,224},{224,1... | collective-permute-start | bytes 393224 | tf_op jit(solution)/shard_map/ppermute | solution.py:428
  15.2 2.8 %collective-permute-start.5 = (bf16[192,256]{1,0:T(8,128)(2,1)S(1)}, bf16[192,256]{1,0:T(8,128)(2,1)S(1)}, u32[]{:S(2)}, u32[]{:S(2)}) collective-permute-start(bf16[192,256]{1,0:T(8,128)(2,1)S(1)} %get-tuple-element.55), channel_id=1, source_target_pairs={{0,96},{32,64},{64,32},{96,0},{128,224},{160,192},{192,160},{224,1... | collective-permute-start | bytes 294920 | tf_op jit(solution)/shard_map/ppermute | solution.py:428
  18.0 0.5 collective-permute-start.4
  18.4 5.4 %collective-permute-done.4.refs_2_ = bf16[64,256]{1,0:T(8,128)(2,1)S(1)} collective-permute-done((bf16[64,256]{1,0:T(8,128)(2,1)S(1)}, bf16[64,256]{1,0:T(8,128)(2,1)S(1)}, u32[]{:S(2)}, u32[]{:S(2)}) %collective-permute-start.4) | collective-permute-done | bytes 32800 | tf_op jit(solution)/shard_map/ppermute | solution.py:428
  23.9 0.0 collective-permute-done.5.refs_3_.refs_1_
  23.9 0.0 collective-permute-done.3.refs_1_.refs_0_
  23.9 0.3 shard_map.80
  24.2 4.2 %collective-permute-start.6 = (bf16[256,256]{1,0:T(8,128)(2,1)S(1)}, bf16[256,256]{1,0:T(8,128)(2,1)S(1)}, u32[]{:S(2)}, u32[]{:S(2)}) collective-permute-start(bf16[256,256]{1,0:T(8,128)(2,1)S(1)} %shard_map.80), channel_id=1, source_target_pairs={{0,224},{32,192},{64,160},{96,128},{128,96},{160,64},{192,32},{224... | collective-permute-start | bytes 393224 | tf_op jit(solution)/shard_map/ppermute | solution.py:428
  28.4 0.0 all-to-all-done
  28.4 1.9 %shard_map.79 = (bf16[128,2048]{1,0:T(8,128)(2,1)S(1)}, bf16[128,2048]{1,0:T(8,128)(2,1)S(1)}, f32[4,1024,256]{2,1,0:T(8,128)S(1)}, f32[4,1024,256]{2,1,0:T(8,128)S(1)}, f32[8,1024]{1,0:T(8,128)S(1)}) custom-call(bf16[1024,256]{1,0:T(8,128)(2,1)S(1)} %get-tuple-element.52.refs_0_, bf16[256,256]{1,0:T(8,128)(2,1)S(1)} %collective-permute-done.3.refs_1_.refs_0_, ...), custom_call_target="tpu_custom_call" | custom-call | flops 1000000000 | bytes 10780672 | tf_op jit(solution)/shard_map/pallas_call | solution.py:403
  30.4 2.3 %collective-permute-done.6.refs_2_.refs_5_ = bf16[256,256]{1,0:T(8,128)(2,1)S(1)} collective-permute-done((bf16[256,256]{1,0:T(8,128)(2,1)S(1)}, bf16[256,256]{1,0:T(8,128)(2,1)S(1)}, u32[]{:S(2)}, u32[]{:S(2)}) %collective-permute-start.6) | collective-permute-done | bytes 131104 | tf_op jit(solution)/shard_map/ppermute | solution.py:428
  32.6 0.9 %shard_map.81 = (bf16[256,256]{1,0:T(8,128)(2,1)S(1)}, bf16[128,256]{1,0:T(8,128)(2,1)S(1)}, bf16[128,256]{1,0:T(8,128)(2,1)S(1)}, bf16[2,128,256]{2,1,0:T(8,128...) custom-call(bf16[256,256]{1,0:T(8,128)(2,1)S(1)} %collective-permute, ...), custom_call_target="tpu_custom_call" | custom-call | flops 100000000 | bytes 2129920 | tf_op jit(solution)/shard_map/pallas_call | solution.py:403
  33.5 3.9 %collective-permute-start.7 = (bf16[256,256]{1,0:T(8,128)(2,1)S(1)}, bf16[256,256]{1,0:T(8,128)(2,1)S(1)}, u32[]{:S(2)}, u32[]{:S(2)}) collective-permute-start(bf16[256,256]{1,0:T(8,128)(2,1)S(1)} %get-tuple-element.72), channel_id=1, source_target_pairs={{0,224},{32,192},{64,160},{96,128},{128,96},{160,64},{192,32},{224... | collective-permute-start | bytes 393224 | tf_op jit(solution)/shard_map/ppermute | solution.py:428
  37.5 3.0 %shard_map.82 = (bf16[1024,256]{1,0:T(8,128)(2,1)}, f32[128,256]{1,0:T(8,128)S(1)}, f32[128,256]{1,0:T(8,128)S(1)}, f32[1024,256]{1,0:T(8,128)S(1)}, f32[512,256]{1,0:T(8,128)S(1)}, /*index=5*/f32[256,256]{1,0:T(8,128)S(1)}) custom-call(bf16[128,2048]{1,0:T(8,128)(2,1)S(1)} %get-tuple-element.56.refs_0_, bf16[128,2048]{1,0:T(8,128)(2,1)S(1)} %get-tuple-element.57.refs_1_, ...), custom_call_target="tpu_custom_call" | custom-call | flops 2000000000 | bytes 13664256 | tf_op jit(solution)/shard_map/pallas_call | solution.py:403
  40.5 1.0 %collective-permute-done.7.refs_0_.refs_5_ = bf16[256,256]{1,0:T(8,128)(2,1)S(1)} collective-permute-done((bf16[256,256]{1,0:T(8,128)(2,1)S(1)}, bf16[256,256]{1,0:T(8,128)(2,1)S(1)}, u32[]{:S(2)}, u32[]{:S(2)}) %collective-permute-start.7) | collective-permute-done | bytes 131104 | tf_op jit(solution)/shard_map/ppermute | solution.py:428
  41.5 0.2 shard_map.83
  41.6 0.4 collective-permute-start.8
  42.0 2.6 %collective-permute-start.10 = (bf16[192,256]{1,0:T(8,128)(2,1)S(1)}, bf16[192,256]{1,0:T(8,128)(2,1)S(1)}, u32[]{:S(2)}, u32[]{:S(2)}) collective-permute-start(bf16[192,256]{1,0:T(8,128)(2,1)S(1)} %get-tuple-element.84), channel_id=1, source_target_pairs={{0,96},{32,64},{64,32},{96,0},{128,224},{160,192},{192,160},{224,1... | collective-permute-start | bytes 294920 | tf_op jit(solution)/shard_map/ppermute | solution.py:428
  44.6 0.6 collective-permute-start.9
  45.2 0.9 %shard_map.84 = (f32[1024,256]{1,0:T(8,128)S(1)}, bf16[1024,256]{1,0:T(8,128)(2,1)}) custom-call(f32[1024,256]{1,0:T(8,128)S(1)} %get-tuple-element.68.refs_0_, f32[512,256]{1,0:T(8,128)S(1)} %get-tuple-element.69.refs_1_, f32[256,256]{1,0:T(8,128)S(1)} %get-tuple-element.70.refs_2_, ...), custom_call_target="tpu_custom_call", output_to_operand_aliasing={{1}: (3, {})} | custom-call | flops 1000000 | bytes 3407872 | tf_op jit(solution)/shard_map/pallas_call | solution.py:403
  46.1 4.4 %all-to-all-start.1 = ((bf16[4,256,256]{2,1,0:T(8,128)(2,1)}), bf16[4,256,256]{2,1,0:T(8,128)(2,1)S(1)}, u32[]{:S(2)}, u32[]{:S(2)}) async-start(bf16[4,256,256]{2,1,0:T(8,128)(2,1)} %bitcast.2), calls=%async_computation.1 | async-start | bytes 1048576 | tf_op jit(solution)/shard_map/all_to_all | solution.py:424
  50.5 0.0 collective-permute-done.9.refs_3_
  50.5 0.0 collective-permute-done.10.refs_4_
  50.5 0.0 collective-permute-done.8.refs_2_
  50.5 0.7 %shard_map.86 = (bf16[256,256]{1,0:T(8,128)(2,1)S(1)}, bf16[256,256]{1,0:T(8,128)(2,1)S(1)}, bf16[256,256]{1,0:T(8,128)(2,1)S(1)}, bf16[256,256]{1,0:T(8,128)(2,1)S(1)}) custom-call(f32[1024,256]{1,0:T(8,128)S(1)} %get-tuple-element.81.refs_0_, f32[128,256]{1,0:T(8,128)S(1)} %get-tuple-element.77.refs_4_.refs_1_, ...), custom_call_target="tpu_custom_call" | custom-call | flops 5000000000 | bytes 2097152 | tf_op jit(solution)/shard_map/pallas_call | solution.py:403
  51.2 2.1 %collective-permute-start.11 = (bf16[256,256]{1,0:T(8,128)(2,1)S(1)}, bf16[256,256]{1,0:T(8,128)(2,1)S(1)}, u32[]{:S(2)}, u32[]{:S(2)}) collective-permute-start(bf16[256,256]{1,0:T(8,128)(2,1)S(1)} %get-tuple-element.86), channel_id=1, source_target_pairs={{0,8},{8,16},{16,24},{24,0},{1,9},{9,17},{17,25},{25,1},{2,10},{10... | collective-permute-start | bytes 393224 | tf_op jit(solution)/shard_map/ppermute | solution.py:419
  53.3 2.7 %collective-permute-start.12 = (bf16[256,256]{1,0:T(8,128)(2,1)S(1)}, bf16[256,256]{1,0:T(8,128)(2,1)S(1)}, u32[]{:S(2)}, u32[]{:S(2)}) collective-permute-start(bf16[256,256]{1,0:T(8,128)(2,1)S(1)} %get-tuple-element.87), channel_id=1, source_target_pairs={{0,16},{8,24},{16,0},{24,8},{1,17},{9,25},{17,1},{25,9},{2,18},{10... | collective-permute-start | bytes 393224 | tf_op jit(solution)/shard_map/ppermute | solution.py:419
  56.0 1.5 %collective-permute-start.13 = (bf16[256,256]{1,0:T(8,128)(2,1)S(1)}, bf16[256,256]{1,0:T(8,128)(2,1)S(1)}, u32[]{:S(2)}, u32[]{:S(2)}) collective-permute-start(bf16[256,256]{1,0:T(8,128)(2,1)S(1)} %get-tuple-element.88), channel_id=1, source_target_pairs={{0,24},{8,0},{16,8},{24,16},{1,25},{9,1},{17,9},{25,17},{2,26},{10... | collective-permute-start | bytes 393224 | tf_op jit(solution)/shard_map/ppermute | solution.py:419
  57.4 1.2 %all-to-all-done.1 = bf16[4,256,256]{2,1,0:T(8,128)(2,1)S(1)} async-done(((bf16[4,256,256]{2,1,0:T(8,128)(2,1)}), bf16[4,256,256]{2,1,0:T(8,128)(2,1)S(1)}, u32[]{:S(2)}, u32[]{:S(2)}) %all-to-all-start.1) | async-done | bytes 524320 | tf_op jit(solution)/shard_map/all_to_all | solution.py:424
  58.7 0.8 %shard_map.85 = (bf16[256,512]{1,0:T(8,128)(2,1)}, bf16[256,512]{1,0:T(8,128)(2,1)}, f32[8,128]{1,0:T(8,128)S(1)}) custom-call(bf16[1024,256]{1,0:T(8,128)(2,1)S(1)} %bitcast.7), custom_call_target="tpu_custom_call" | custom-call | flops 1000000 | bytes 1052672 | tf_op jit(solution)/shard_map/pallas_call | solution.py:403
  59.5 0.1 collective-permute-done.11.refs_1_
  59.7 1.7 %collective-permute-done.12.refs_2_ = bf16[256,256]{1,0:T(8,128)(2,1)S(1)} collective-permute-done((bf16[256,256]{1,0:T(8,128)(2,1)S(1)}, bf16[256,256]{1,0:T(8,128)(2,1)S(1)}, u32[]{:S(2)}, u32[]{:S(2)}) %collective-permute-start.12) | collective-permute-done | bytes 131104 | tf_op jit(solution)/shard_map/ppermute | solution.py:419
  61.4 0.0 collective-permute-done.13.refs_3_
  61.4 0.8 %shard_map.87 = (bf16[256,512]{1,0:T(8,128)(2,1)}, bf16[256,512]{1,0:T(8,128)(2,1)}) custom-call(bf16[256,256]{1,0:T(8,128)(2,1)S(1)} %get-tuple-element.85.refs_0_, bf16[256,256]{1,0:T(8,128)(2,1)S(1)} %collective-permute-done.11.refs_1_, bf16[256,256]{1,0:T(8,128)(2,1)S(1)} %collective-permute-done.12.refs_2_, ...), custom_call_target="tpu_custom_call" | custom-call | flops 1000000 | bytes 1048576 | tf_op jit(solution)/shard_map/pallas_call | solution.py:403
  (5 shorter events, 0.0 us)
Async XLA Ops:
  0.6 1.0 %copy-start.3 = (bf16[256,512]{1,0:T(8,128)(2,1)S(1)}, bf16[256,512]{1,0:T(8,128)(2,1)}, u32[]{:S(2)}) copy-start(bf16[256,512]{1,0:T(8,128)(2,1)} %refs_1_.2) | copy-start | bytes 786436
  0.6 1.0 %copy-start.2 = (bf16[256,512]{1,0:T(8,128)(2,1)S(1)}, bf16[256,512]{1,0:T(8,128)(2,1)}, u32[]{:S(2)}) copy-start(bf16[256,512]{1,0:T(8,128)(2,1)} %refs_0_.2) | copy-start | bytes 786436
  1.7 6.1 %copy-start = (bf16[256,512]{1,0:T(8,128)(2,1)S(1)}, bf16[256,512]{1,0:T(8,128)(2,1)}, u32[]{:S(2)}) copy-start(bf16[256,512]{1,0:T(8,128)(2,1)} %refs_0_.3) | copy-start | bytes 786436
  1.7 6.1 %copy-start.1 = (bf16[256,512]{1,0:T(8,128)(2,1)S(1)}, bf16[256,512]{1,0:T(8,128)(2,1)}, u32[]{:S(2)}) copy-start(bf16[256,512]{1,0:T(8,128)(2,1)} %refs_1_.3) | copy-start | bytes 786436
  1.9 10.4 %collective-permute-start = (bf16[256,256]{1,0:T(8,128)(2,1)S(1)}, bf16[256,256]{1,0:T(8,128)(2,1)S(1)}, u32[]{:S(2)}, u32[]{:S(2)}) collective-permute-start(bf16[256,256]{1,0:T(8,128)(2,1)S(1)} %get-tuple-element.49), channel_id=1, source_target_pairs={{0,8},{8,16},{16,24},{24,0},{1,9},{9,17},{17,25},{25,1},{2,10},{10... | collective-permute-start | bytes 393224 | tf_op jit(solution)/shard_map/ppermute | solution.py:419
  3.5 8.9 %collective-permute-start.1 = (bf16[256,256]{1,0:T(8,128)(2,1)S(1)}, bf16[256,256]{1,0:T(8,128)(2,1)S(1)}, u32[]{:S(2)}, u32[]{:S(2)}) collective-permute-start(bf16[256,256]{1,0:T(8,128)(2,1)S(1)} %get-tuple-element.50), channel_id=1, source_target_pairs={{0,16},{8,24},{16,0},{24,8},{1,17},{9,25},{17,1},{25,9},{2,18},{10... | collective-permute-start | bytes 393224 | tf_op jit(solution)/shard_map/ppermute | solution.py:419
  6.4 6.0 %collective-permute-start.2 = (bf16[256,256]{1,0:T(8,128)(2,1)S(1)}, bf16[256,256]{1,0:T(8,128)(2,1)S(1)}, u32[]{:S(2)}, u32[]{:S(2)}) collective-permute-start(bf16[256,256]{1,0:T(8,128)(2,1)S(1)} %get-tuple-element.51), channel_id=1, source_target_pairs={{0,24},{8,0},{16,8},{24,16},{1,25},{9,1},{17,9},{25,17},{2,26},{10... | collective-permute-start | bytes 393224 | tf_op jit(solution)/shard_map/ppermute | solution.py:419
  8.8 19.6 %all-to-all-start = ((bf16[4,256,256]{2,1,0:T(8,128)(2,1)}), bf16[4,256,256]{2,1,0:T(8,128)(2,1)S(1)}, u32[]{:S(2)}, u32[]{:S(2)}) async-start(bf16[4,256,256]{2,1,0:T(8,128)(2,1)} %bitcast), calls=%async_computation | async-start | bytes 1048576 | tf_op jit(solution)/shard_map/all_to_all | solution.py:424
  13.2 10.7 %collective-permute-start.3 = (bf16[256,256]{1,0:T(8,128)(2,1)S(1)}, bf16[256,256]{1,0:T(8,128)(2,1)S(1)}, u32[]{:S(2)}, u32[]{:S(2)}) collective-permute-start(bf16[256,256]{1,0:T(8,128)(2,1)S(1)} %get-tuple-element.53), channel_id=1, source_target_pairs={{0,32},{32,0},{64,96},{96,64},{128,160},{160,128},{192,224},{224,1... | collective-permute-start | bytes 393224 | tf_op jit(solution)/shard_map/ppermute | solution.py:428
  15.2 8.7 %collective-permute-start.5 = (bf16[192,256]{1,0:T(8,128)(2,1)S(1)}, bf16[192,256]{1,0:T(8,128)(2,1)S(1)}, u32[]{:S(2)}, u32[]{:S(2)}) collective-permute-start(bf16[192,256]{1,0:T(8,128)(2,1)S(1)} %get-tuple-element.55), channel_id=1, source_target_pairs={{0,96},{32,64},{64,32},{96,0},{128,224},{160,192},{192,160},{224,1... | collective-permute-start | bytes 294920 | tf_op jit(solution)/shard_map/ppermute | solution.py:428
  18.0 5.9 %collective-permute-start.4 = (bf16[64,256]{1,0:T(8,128)(2,1)S(1)}, bf16[64,256]{1,0:T(8,128)(2,1)S(1)}, u32[]{:S(2)}, u32[]{:S(2)}) collective-permute-start(bf16[64,256]{1,0:T(8,128)(2,1)S(1)} %get-tuple-element.54), channel_id=1, source_target_pairs={{0,64},{32,96},{64,0},{96,32},{128,192},{160,224},{192,128},{224,1... | collective-permute-start | bytes 98312 | tf_op jit(solution)/shard_map/ppermute | solution.py:428
  24.2 8.5 %collective-permute-start.6 = (bf16[256,256]{1,0:T(8,128)(2,1)S(1)}, bf16[256,256]{1,0:T(8,128)(2,1)S(1)}, u32[]{:S(2)}, u32[]{:S(2)}) collective-permute-start(bf16[256,256]{1,0:T(8,128)(2,1)S(1)} %shard_map.80), channel_id=1, source_target_pairs={{0,224},{32,192},{64,160},{96,128},{128,96},{160,64},{192,32},{224... | collective-permute-start | bytes 393224 | tf_op jit(solution)/shard_map/ppermute | solution.py:428
  33.5 7.9 %collective-permute-start.7 = (bf16[256,256]{1,0:T(8,128)(2,1)S(1)}, bf16[256,256]{1,0:T(8,128)(2,1)S(1)}, u32[]{:S(2)}, u32[]{:S(2)}) collective-permute-start(bf16[256,256]{1,0:T(8,128)(2,1)S(1)} %get-tuple-element.72), channel_id=1, source_target_pairs={{0,224},{32,192},{64,160},{96,128},{128,96},{160,64},{192,32},{224... | collective-permute-start | bytes 393224 | tf_op jit(solution)/shard_map/ppermute | solution.py:428
  41.6 8.9 %collective-permute-start.8 = (bf16[256,256]{1,0:T(8,128)(2,1)S(1)}, bf16[256,256]{1,0:T(8,128)(2,1)S(1)}, u32[]{:S(2)}, u32[]{:S(2)}) collective-permute-start(bf16[256,256]{1,0:T(8,128)(2,1)S(1)} %get-tuple-element.82), channel_id=1, source_target_pairs={{0,32},{32,0},{64,96},{96,64},{128,160},{160,128},{192,224},{224,1... | collective-permute-start | bytes 393224 | tf_op jit(solution)/shard_map/ppermute | solution.py:428
  42.0 8.5 %collective-permute-start.10 = (bf16[192,256]{1,0:T(8,128)(2,1)S(1)}, bf16[192,256]{1,0:T(8,128)(2,1)S(1)}, u32[]{:S(2)}, u32[]{:S(2)}) collective-permute-start(bf16[192,256]{1,0:T(8,128)(2,1)S(1)} %get-tuple-element.84), channel_id=1, source_target_pairs={{0,96},{32,64},{64,32},{96,0},{128,224},{160,192},{192,160},{224,1... | collective-permute-start | bytes 294920 | tf_op jit(solution)/shard_map/ppermute | solution.py:428
  44.6 5.9 %collective-permute-start.9 = (bf16[64,256]{1,0:T(8,128)(2,1)S(1)}, bf16[64,256]{1,0:T(8,128)(2,1)S(1)}, u32[]{:S(2)}, u32[]{:S(2)}) collective-permute-start(bf16[64,256]{1,0:T(8,128)(2,1)S(1)} %get-tuple-element.83), channel_id=1, source_target_pairs={{0,64},{32,96},{64,0},{96,32},{128,192},{160,224},{192,128},{224,1... | collective-permute-start | bytes 98312 | tf_op jit(solution)/shard_map/ppermute | solution.py:428
  46.1 12.6 %all-to-all-start.1 = ((bf16[4,256,256]{2,1,0:T(8,128)(2,1)}), bf16[4,256,256]{2,1,0:T(8,128)(2,1)S(1)}, u32[]{:S(2)}, u32[]{:S(2)}) async-start(bf16[4,256,256]{2,1,0:T(8,128)(2,1)} %bitcast.2), calls=%async_computation.1 | async-start | bytes 1048576 | tf_op jit(solution)/shard_map/all_to_all | solution.py:424
  51.2 8.5 %collective-permute-start.11 = (bf16[256,256]{1,0:T(8,128)(2,1)S(1)}, bf16[256,256]{1,0:T(8,128)(2,1)S(1)}, u32[]{:S(2)}, u32[]{:S(2)}) collective-permute-start(bf16[256,256]{1,0:T(8,128)(2,1)S(1)} %get-tuple-element.86), channel_id=1, source_target_pairs={{0,8},{8,16},{16,24},{24,0},{1,9},{9,17},{17,25},{25,1},{2,10},{10... | collective-permute-start | bytes 393224 | tf_op jit(solution)/shard_map/ppermute | solution.py:419
  53.3 8.1 %collective-permute-start.12 = (bf16[256,256]{1,0:T(8,128)(2,1)S(1)}, bf16[256,256]{1,0:T(8,128)(2,1)S(1)}, u32[]{:S(2)}, u32[]{:S(2)}) collective-permute-start(bf16[256,256]{1,0:T(8,128)(2,1)S(1)} %get-tuple-element.87), channel_id=1, source_target_pairs={{0,16},{8,24},{16,0},{24,8},{1,17},{9,25},{17,1},{25,9},{2,18},{10... | collective-permute-start | bytes 393224 | tf_op jit(solution)/shard_map/ppermute | solution.py:419
  56.0 5.5 %collective-permute-start.13 = (bf16[256,256]{1,0:T(8,128)(2,1)S(1)}, bf16[256,256]{1,0:T(8,128)(2,1)S(1)}, u32[]{:S(2)}, u32[]{:S(2)}) collective-permute-start(bf16[256,256]{1,0:T(8,128)(2,1)S(1)} %get-tuple-element.88), channel_id=1, source_target_pairs={{0,24},{8,0},{16,8},{24,16},{1,25},{9,1},{17,9},{25,17},{2,26},{10... | collective-permute-start | bytes 393224 | tf_op jit(solution)/shard_map/ppermute | solution.py:419

commit v5 on v4

--- a/solution.py
+++ b/solution.py
@@ -17,6 +17,8 @@
 PIECE = 2 * B
 PLANE = NY * PIECE
 SMALL = PIECE // 8
+TOP = [(z, (6, 7, 4, 5, 2, 3, 0, 1)[z]) for z in range(NZ)]
+SIDE = [(z, (z - 1 if z % 2 == 0 else z + 1) % NZ) for z in range(NZ)]
 Y_ORDER = (1, 2, 3)
 POOL = 5 * 10**9
 FIRST = 5 * 10**9
@@ -146,7 +148,7 @@
         copy.wait()
 
 
-def pool_kernel(k0, k1, k2, k3, kv_ref, m1_ref, m2_ref, m3_ref, tail_ref):
+def pool_kernel(k0, k1, k2, k3, kv_ref, m1_ref, four_ref, side_ref):
     y = lax.axis_index("y")
     odd = lax.rem(lax.axis_index("z"), 2)
     for d, ref in enumerate((k0, k1, k2, k3)):
@@ -160,21 +162,17 @@
     other = kv_ref[part_at(odd * (PLANE // B - 1), B), :]
     m1_ref[:B] = three
     m1_ref[B:] = facing
-    m2_ref[...] = four
-    m3_ref[:HALF] = four
-    m3_ref[HALF:] = other
-    tail_ref[:HALF] = four
-    tail_ref[HALF:] = other
-
-
-def quad_kernel(tail_ref, three_1, four_2, four_3, top_ref):
+    four_ref[...] = four
+    side_ref[...] = other
+
+
+def quad_kernel(own_four, three_1, four_2, four_3, top_ref):
     z = lax.axis_index("z")
     matrix = pair_sum(HALF)
     small = matrix[: B // 4, :HALF]
-    fours = (tail_ref[:HALF], pool(matrix, three_1[:B]), four_2[...], four_3[:HALF])
+    fours = (own_four[...], pool(matrix, three_1[:B]), four_2[...], four_3[...])
     for d, four in enumerate(fours):
         top_ref[part_at((z ^ d) & 3, SMALL), :] = pool(small, four)
-    top_ref[B:] = tail_ref[HALF:]
 
 
 def by_three(z):
@@ -203,7 +201,7 @@
     one = [pool(matrix, kv[n * PIECE : (n + 1) * PIECE]) for n in range(4)]
     two = [pool(matrix, jnp.concatenate(one[n : n + 2], axis=0)) for n in (0, 2)]
     at = 0
-    for part in (kv[...], *one, *two, from_1[:B], from_2[...], from_3[:HALF]):
+    for part in (kv[...], *one, *two, from_1[:B], from_2[...], from_3[...]):
         rows = part.shape[0]
         keys[at : at + rows, :] = part[:, :D]
         vals[at : at + rows, :] = part[:, D:]
@@ -241,12 +239,12 @@
 
 
 def late_kernel(
-    from_1, from_3, from_7, qc, stats, top_ref, g_facing, g_other, edges, found, w5, s5, ew, es
+    from_1, from_side, from_7, qc, stats, top_ref, g_facing, g_other, edges, found, w5, s5, ew, es
 ):
     z = lax.axis_index("z")
     odd = lax.rem(z, 2)
     edges[1 - odd] = from_1[B:]
-    edges[odd] = jnp.where(by_three(z), from_3[HALF:], from_7[B:])
+    edges[odd] = from_side[...]
     first = lax.broadcasted_iota(jnp.int32, (B, PIECE), 1) < B
     for i in range(NY):
         lanes = slice(i * PIECE, (i + 1) * PIECE)
@@ -444,16 +442,17 @@
     kv = around_y(kv)
     (qc_own,) = call(stack_kernel, [queries, cotangent], [plane], scratch=sems, source=HBM)
     qc = across_y(qc_own)
-    kv, m1, m2, m3, own_tail = call(
+    kv, m1, four, side = call(
         pool_kernel,
         [*kv],
-        [plane, double, half, tail, tail],
+        [plane, double, half, level],
         flops=POOL,
-        after=[qc_own] if EARLY_STACK else [],
-    )
-    from_1, from_2, from_3 = over_z(m1, 1), over_z(m2, 2), over_z(m3, 3)
-    (top,) = call(quad_kernel, [own_tail, from_1, from_2, from_3], [double])
-    from_7 = over_z(top, 7)
+        after=[qc_own],
+    )
+    from_1, from_2, from_3 = over_z(m1, 1), over_z(four, 2), over_z(four, 3)
+    from_side = lax.ppermute(side, "z", SIDE)
+    (top,) = call(quad_kernel, [four, from_1, from_2, from_3], [level])
+    from_7 = lax.ppermute(top, "z", TOP)
     keys_t, vals_t, raised, pgrads, stats = call(
         early_kernel,
         [kv, from_1, from_2, from_3, qc],
@@ -464,7 +463,7 @@
     )
     g_top, g_facing, g_other, edges, found, w5, s5, ew, es = call(
         late_kernel,
-        [from_1, from_3, from_7, qc, stats],
+        [from_1, from_side, from_7, qc, stats],
         [double, level, level, ((2, B, 2 * D), BF), ((8, PLANE), F32)]
         + [((B, PLANE), BF)] * 2
         + [((2, B, PIECE), BF)] * 2,

time: 62.7 us -> 61.3 us (0.978)
  waiting for transfers between devices: 12 us -> 5.24 us
  starting transfers between devices: 37 us -> 41.7 us
    ppermute x0 -> x2, starting transfers between devices: none -> 7.82 us  [the longest x1 4.16 us: per_device(): from_side = lax.ppermute(side, 'z', SIDE)]
    ppermute x8 -> x7, waiting for transfers between devices: 8.67 us -> 1 us  [over_z(): return lax.ppermute(array, 'z', [(i, i ^ d) for i in range(NZ)])]
    ppermute x8 -> x7, starting transfers between devices: 17 us -> 13.7 us  [over_z(): return lax.ppermute(array, 'z', [(i, i ^ d) for i in range(NZ)])]
    ppermute x0 -> x2, waiting for transfers between devices: none -> 0.93 us  [the longest x1 0.93 us: per_device(): from_7 = lax.ppermute(top, 'z', TOP)]
  transfers between devices with their start and end apart: 16 -> 17, of which waited for: 7 -> 7; matrix products, arithmetic and copies ran while one was open for 0% -> 0% of each run, Pallas kernels for 15% -> 16%
where the time goes in v5:
time: 61.3 us; the launch traced here: 60.4 us
  starting transfers between devices  41.7 us (68%)
  Pallas kernels  11.5 us (19%)
  waiting for transfers between devices  5.24 us (9%)
  local copies, waits for them, and re-layouts  1.01 us (2%)
  between operations  0.94 us (2%)
    ppermute x7, starting transfers between devices, over_z(): return lax.ppermute(array, 'z', [(i, i ^ d) for i in range(NZ)])  13.7 us
    ppermute x6, starting transfers between devices, around_y(): lax.ppermute(pieces[d], 'y', [(i, (i + d) % NY) for i in range(NY)])  12.1 us
    pallas_call x13, Pallas kernels, call(): pl.pallas_call(body, out_shape=[jax.ShapeDtypeStruct(s, t) for s, t in ou...  11.5 us
    all_to_all x2, starting transfers between devices, across_y(): return lax.all_to_all(array, 'y', split_axis=0, concat_axis=0, tiled=True)  8.02 us
    ppermute x1, starting transfers between devices, per_device(): from_side = lax.ppermute(side, 'z', SIDE)  4.16 us
    ppermute x1, starting transfers between devices, per_device(): from_7 = lax.ppermute(top, 'z', TOP)  3.66 us
    ppermute x6, waiting for transfers between devices, around_y(): lax.ppermute(pieces[d], 'y', [(i, (i + d) % NY) for i in range(NY)])  2.07 us
    all_to_all x2, waiting for transfers between devices, across_y(): return lax.all_to_all(array, 'y', split_axis=0, concat_axis=0, tiled=True)  1.24 us
  transfers between devices with their start and end apart: 17, of which 7 were waited for; matrix products, arithmetic and copies ran while one was open for 0% of the time, Pallas kernels for 16%

profile of v5, /device:TPU:6, one launch (start us, length us, event | category | flops | bytes accessed | tf_op | source)
XLA Modules:
  0.0 60.4 jit_solution(2571125723308578267)
XLA Ops:
  0.7 0.9 %copy-done.3 = bf16[256,512]{1,0:T(8,128)(2,1)S(1)} copy-done((bf16[256,512]{1,0:T(8,128)(2,1)S(1)}, bf16[256,512]{1,0:T(8,128)(2,1)}, u32[]{:S(2)}) %copy-start.3) | copy-done | bytes 262168
  1.6 0.1 copy-done.2
  1.7 0.2 shard_map.76
  1.9 1.7 %collective-permute-start = (bf16[256,256]{1,0:T(8,128)(2,1)S(1)}, bf16[256,256]{1,0:T(8,128)(2,1)S(1)}, u32[]{:S(2)}, u32[]{:S(2)}) collective-permute-start(bf16[256,256]{1,0:T(8,128)(2,1)S(1)} %get-tuple-element.48), channel_id=1, source_target_pairs={{0,8},{8,16},{16,24},{24,0},{1,9},{9,17},{17,25},{25,1},{2,10},{10... | collective-permute-start | bytes 393224 | tf_op jit(solution)/shard_map/ppermute | solution.py:417
  3.5 2.9 %collective-permute-start.1 = (bf16[256,256]{1,0:T(8,128)(2,1)S(1)}, bf16[256,256]{1,0:T(8,128)(2,1)S(1)}, u32[]{:S(2)}, u32[]{:S(2)}) collective-permute-start(bf16[256,256]{1,0:T(8,128)(2,1)S(1)} %get-tuple-element.49), channel_id=1, source_target_pairs={{0,16},{8,24},{16,0},{24,8},{1,17},{9,25},{17,1},{25,9},{2,18},{10... | collective-permute-start | bytes 393224 | tf_op jit(solution)/shard_map/ppermute | solution.py:417
  6.4 1.3 %collective-permute-start.2 = (bf16[256,256]{1,0:T(8,128)(2,1)S(1)}, bf16[256,256]{1,0:T(8,128)(2,1)S(1)}, u32[]{:S(2)}, u32[]{:S(2)}) collective-permute-start(bf16[256,256]{1,0:T(8,128)(2,1)S(1)} %get-tuple-element.50), channel_id=1, source_target_pairs={{0,24},{8,0},{16,8},{24,16},{1,25},{9,1},{17,9},{25,17},{2,26},{10... | collective-permute-start | bytes 393224 | tf_op jit(solution)/shard_map/ppermute | solution.py:417
  7.8 1.0 %shard_map.77.refs_4_ = bf16[1024,256]{1,0:T(8,128)(2,1)} custom-call(bf16[256,512]{1,0:T(8,128)(2,1)S(1)} %copy-done, bf16[256,512]{1,0:T(8,128)(2,1)S(1)} %copy-done.1), custom_call_target="tpu_custom_call" | custom-call | flops 1000000 | bytes 1048576 | tf_op jit(solution)/shard_map/pallas_call | solution.py:401
  8.8 3.5 %all-to-all-start = ((bf16[4,256,256]{2,1,0:T(8,128)(2,1)}), bf16[4,256,256]{2,1,0:T(8,128)(2,1)S(1)}, u32[]{:S(2)}, u32[]{:S(2)}) async-start(bf16[4,256,256]{2,1,0:T(8,128)(2,1)} %bitcast), calls=%async_computation | async-start | bytes 1048576 | tf_op jit(solution)/shard_map/all_to_all | solution.py:422
  12.2 0.0 collective-permute-done.refs_1_
  12.3 0.2 collective-permute-done.1.refs_2_
  12.4 0.0 collective-permute-done.2.refs_3_
  12.4 0.7 %shard_map.78 = (bf16[1024,256]{1,0:T(8,128)(2,1)S(1)}, bf16[256,256]{1,0:T(8,128)(2,1)S(1)}, bf16[64,256]{1,0:T(8,128)(2,1)S(1)}, bf16[128,256]{1,0:T(8,128)(2,1)S(1)}) custom-call(bf16[256,256]{1,0:T(8,128)(2,1)S(1)} %get-tuple-element.47.refs_0_, bf16[256,256]{1,0:T(8,128)(2,1)S(1)} %collective-permute-done.refs_1_, ...), custom_call_target="tpu_custom_call" | custom-call | flops 5000000000 | bytes 1277952 | tf_op jit(solution)/shard_map/pallas_call | solution.py:401
  13.2 2.0 %collective-permute-start.3 = (bf16[256,256]{1,0:T(8,128)(2,1)S(1)}, bf16[256,256]{1,0:T(8,128)(2,1)S(1)}, u32[]{:S(2)}, u32[]{:S(2)}) collective-permute-start(bf16[256,256]{1,0:T(8,128)(2,1)S(1)} %get-tuple-element.52), channel_id=1, source_target_pairs={{0,32},{32,0},{64,96},{96,64},{128,160},{160,128},{192,224},{224,1... | collective-permute-start | bytes 393224 | tf_op jit(solution)/shard_map/ppermute | solution.py:426
  15.2 2.8 %collective-permute-start.5 = (bf16[64,256]{1,0:T(8,128)(2,1)S(1)}, bf16[64,256]{1,0:T(8,128)(2,1)S(1)}, u32[]{:S(2)}, u32[]{:S(2)}) collective-permute-start(bf16[64,256]{1,0:T(8,128)(2,1)S(1)} %get-tuple-element.53.refs_0_), channel_id=1, source_target_pairs={{0,96},{32,64},{64,32},{96,0},{128,224},{160,192},{192,160},{224,1... | collective-permute-start | bytes 98312 | tf_op jit(solution)/shard_map/ppermute | solution.py:426
  18.0 0.5 collective-permute-start.4
  18.4 4.2 %collective-permute-start.7 = (bf16[128,256]{1,0:T(8,128)(2,1)S(1)}, bf16[128,256]{1,0:T(8,128)(2,1)S(1)}, u32[]{:S(2)}, u32[]{:S(2)}) collective-permute-start(bf16[128,256]{1,0:T(8,128)(2,1)S(1)} %get-tuple-element.58), channel_id=1, source_target_pairs={{0,224},{32,64},{64,32},{96,128},{128,96},{160,192},{192,160},{224... | collective-permute-start | bytes 196616 | tf_op jit(solution)/shard_map/ppermute | solution.py:453
  22.6 0.0 collective-permute-done.5.refs_3_
  22.6 0.2 collective-permute-done.4.refs_2_
  22.8 0.0 collective-permute-done.3.refs_1_.refs_0_
  22.8 0.3 shard_map.80
  23.1 3.7 %collective-permute-start.6 = (bf16[128,256]{1,0:T(8,128)(2,1)S(1)}, bf16[128,256]{1,0:T(8,128)(2,1)S(1)}, u32[]{:S(2)}, u32[]{:S(2)}) collective-permute-start(bf16[128,256]{1,0:T(8,128)(2,1)S(1)} %shard_map.80), channel_id=1, source_target_pairs={{0,192},{32,224},{64,128},{96,160},{128,64},{160,96},{192,0},{224,... | collective-permute-start | bytes 196616 | tf_op jit(solution)/shard_map/ppermute | solution.py:455
  26.8 0.0 all-to-all-done
  26.8 2.0 %shard_map.79 = (bf16[128,2048]{1,0:T(8,128)(2,1)S(1)}, bf16[128,2048]{1,0:T(8,128)(2,1)S(1)}, f32[4,1024,256]{2,1,0:T(8,128)S(1)}, f32[4,1024,256]{2,1,0:T(8,128)S(1)}, f32[8,1024]{1,0:T(8,128)S(1)}) custom-call(bf16[1024,256]{1,0:T(8,128)(2,1)S(1)} %get-tuple-element.51.refs_0_, bf16[256,256]{1,0:T(8,128)(2,1)S(1)} %collective-permute-done.3.refs_1_.refs_0_, ...), custom_call_target="tpu_custom_call" | custom-call | flops 1000000000 | bytes 10715136 | tf_op jit(solution)/shard_map/pallas_call | solution.py:401
  28.7 0.0 collective-permute-done.7.refs_1_
  28.7 0.9 %collective-permute-done.6.refs_2_.refs_5_ = bf16[128,256]{1,0:T(8,128)(2,1)S(1)} collective-permute-done((bf16[128,256]{1,0:T(8,128)(2,1)S(1)}, bf16[128,256]{1,0:T(8,128)(2,1)S(1)}, u32[]{:S(2)}, u32[]{:S(2)}) %collective-permute-start.6) | collective-permute-done | bytes 65568 | tf_op jit(solution)/shard_map/ppermute | solution.py:455
  29.7 0.9 %shard_map.81 = (bf16[256,256]{1,0:T(8,128)(2,1)S(1)}, bf16[128,256]{1,0:T(8,128)(2,1)S(1)}, bf16[128,256]{1,0:T(8,128)(2,1)S(1)}, bf16[2,128,256]{2,1,0:T(8,128...) custom-call(bf16[256,256]{1,0:T(8,128)(2,1)S(1)} %collective-permute, ...), custom_call_target="tpu_custom_call" | custom-call | flops 100000000 | bytes 2031616 | tf_op jit(solution)/shard_map/pallas_call | solution.py:401
  30.6 4.0 %collective-permute-start.8 = (bf16[256,256]{1,0:T(8,128)(2,1)S(1)}, bf16[256,256]{1,0:T(8,128)(2,1)S(1)}, u32[]{:S(2)}, u32[]{:S(2)}) collective-permute-start(bf16[256,256]{1,0:T(8,128)(2,1)S(1)} %get-tuple-element.70), channel_id=1, source_target_pairs={{0,224},{32,192},{64,160},{96,128},{128,96},{160,64},{192,32},{224... | collective-permute-start | bytes 393224 | tf_op jit(solution)/shard_map/ppermute | solution.py:426
  34.6 3.0 %shard_map.82 = (bf16[1024,256]{1,0:T(8,128)(2,1)}, f32[128,256]{1,0:T(8,128)S(1)}, f32[128,256]{1,0:T(8,128)S(1)}, f32[1024,256]{1,0:T(8,128)S(1)}, f32[512,256]{1,0:T(8,128)S(1)}, /*index=5*/f32[256,256]{1,0:T(8,128)S(1)}) custom-call(bf16[128,2048]{1,0:T(8,128)(2,1)S(1)} %get-tuple-element.54.refs_0_, bf16[128,2048]{1,0:T(8,128)(2,1)S(1)} %get-tuple-element.55.refs_1_, ...), custom_call_target="tpu_custom_call" | custom-call | flops 2000000000 | bytes 13598720 | tf_op jit(solution)/shard_map/pallas_call | solution.py:401
  37.6 0.8 %collective-permute-done.8.refs_0_.refs_5_ = bf16[256,256]{1,0:T(8,128)(2,1)S(1)} collective-permute-done((bf16[256,256]{1,0:T(8,128)(2,1)S(1)}, bf16[256,256]{1,0:T(8,128)(2,1)S(1)}, u32[]{:S(2)}, u32[]{:S(2)}) %collective-permute-start.8) | collective-permute-done | bytes 131104 | tf_op jit(solution)/shard_map/ppermute | solution.py:426
  38.4 0.2 shard_map.83
  38.6 2.4 %collective-permute-start.9 = (bf16[256,256]{1,0:T(8,128)(2,1)S(1)}, bf16[256,256]{1,0:T(8,128)(2,1)S(1)}, u32[]{:S(2)}, u32[]{:S(2)}) collective-permute-start(bf16[256,256]{1,0:T(8,128)(2,1)S(1)} %get-tuple-element.80), channel_id=1, source_target_pairs={{0,32},{32,0},{64,96},{96,64},{128,160},{160,128},{192,224},{224,1... | collective-permute-start | bytes 393224 | tf_op jit(solution)/shard_map/ppermute | solution.py:426
  41.0 2.0 %collective-permute-start.11 = (bf16[192,256]{1,0:T(8,128)(2,1)S(1)}, bf16[192,256]{1,0:T(8,128)(2,1)S(1)}, u32[]{:S(2)}, u32[]{:S(2)}) collective-permute-start(bf16[192,256]{1,0:T(8,128)(2,1)S(1)} %get-tuple-element.82), channel_id=1, source_target_pairs={{0,96},{32,64},{64,32},{96,0},{128,224},{160,192},{192,160},{224,1... | collective-permute-start | bytes 294920 | tf_op jit(solution)/shard_map/ppermute | solution.py:426
  43.0 0.0 collective-permute-start.10
  43.0 0.9 %shard_map.84 = (f32[1024,256]{1,0:T(8,128)S(1)}, bf16[1024,256]{1,0:T(8,128)(2,1)}) custom-call(f32[1024,256]{1,0:T(8,128)S(1)} %get-tuple-element.66.refs_0_, f32[512,256]{1,0:T(8,128)S(1)} %get-tuple-element.67.refs_1_, f32[256,256]{1,0:T(8,128)S(1)} %get-tuple-element.68.refs_2_, ...), custom_call_target="tpu_custom_call", output_to_operand_aliasing={{1}: (3, {})} | custom-call | flops 1000000 | bytes 3407872 | tf_op jit(solution)/shard_map/pallas_call | solution.py:401
  43.9 4.5 %all-to-all-start.1 = ((bf16[4,256,256]{2,1,0:T(8,128)(2,1)}), bf16[4,256,256]{2,1,0:T(8,128)(2,1)S(1)}, u32[]{:S(2)}, u32[]{:S(2)}) async-start(bf16[4,256,256]{2,1,0:T(8,128)(2,1)} %bitcast.2), calls=%async_computation.1 | async-start | bytes 1048576 | tf_op jit(solution)/shard_map/all_to_all | solution.py:422
  48.5 0.0 collective-permute-done.10.refs_3_
  48.5 0.0 collective-permute-done.11.refs_4_
  48.5 0.0 collective-permute-done.9.refs_2_
  48.5 0.7 %shard_map.86 = (bf16[256,256]{1,0:T(8,128)(2,1)S(1)}, bf16[256,256]{1,0:T(8,128)(2,1)S(1)}, bf16[256,256]{1,0:T(8,128)(2,1)S(1)}, bf16[256,256]{1,0:T(8,128)(2,1)S(1)}) custom-call(f32[1024,256]{1,0:T(8,128)S(1)} %get-tuple-element.79.refs_0_, f32[128,256]{1,0:T(8,128)S(1)} %get-tuple-element.75.refs_4_.refs_1_, ...), custom_call_target="tpu_custom_call" | custom-call | flops 5000000000 | bytes 2097152 | tf_op jit(solution)/shard_map/pallas_call | solution.py:401
  49.2 2.1 %collective-permute-start.12 = (bf16[256,256]{1,0:T(8,128)(2,1)S(1)}, bf16[256,256]{1,0:T(8,128)(2,1)S(1)}, u32[]{:S(2)}, u32[]{:S(2)}) collective-permute-start(bf16[256,256]{1,0:T(8,128)(2,1)S(1)} %get-tuple-element.84), channel_id=1, source_target_pairs={{0,8},{8,16},{16,24},{24,0},{1,9},{9,17},{17,25},{25,1},{2,10},{10... | collective-permute-start | bytes 393224 | tf_op jit(solution)/shard_map/ppermute | solution.py:417
  51.3 2.7 %collective-permute-start.13 = (bf16[256,256]{1,0:T(8,128)(2,1)S(1)}, bf16[256,256]{1,0:T(8,128)(2,1)S(1)}, u32[]{:S(2)}, u32[]{:S(2)}) collective-permute-start(bf16[256,256]{1,0:T(8,128)(2,1)S(1)} %get-tuple-element.85), channel_id=1, source_target_pairs={{0,16},{8,24},{16,0},{24,8},{1,17},{9,25},{17,1},{25,9},{2,18},{10... | collective-permute-start | bytes 393224 | tf_op jit(solution)/shard_map/ppermute | solution.py:417
  54.0 1.5 %collective-permute-start.14 = (bf16[256,256]{1,0:T(8,128)(2,1)S(1)}, bf16[256,256]{1,0:T(8,128)(2,1)S(1)}, u32[]{:S(2)}, u32[]{:S(2)}) collective-permute-start(bf16[256,256]{1,0:T(8,128)(2,1)S(1)} %get-tuple-element.86), channel_id=1, source_target_pairs={{0,24},{8,0},{16,8},{24,16},{1,25},{9,1},{17,9},{25,17},{2,26},{10... | collective-permute-start | bytes 393224 | tf_op jit(solution)/shard_map/ppermute | solution.py:417
  55.4 1.2 %all-to-all-done.1 = bf16[4,256,256]{2,1,0:T(8,128)(2,1)S(1)} async-done(((bf16[4,256,256]{2,1,0:T(8,128)(2,1)}), bf16[4,256,256]{2,1,0:T(8,128)(2,1)S(1)}, u32[]{:S(2)}, u32[]{:S(2)}) %all-to-all-start.1) | async-done | bytes 524320 | tf_op jit(solution)/shard_map/all_to_all | solution.py:422
  56.7 0.8 %shard_map.85 = (bf16[256,512]{1,0:T(8,128)(2,1)}, bf16[256,512]{1,0:T(8,128)(2,1)}, f32[8,128]{1,0:T(8,128)S(1)}) custom-call(bf16[1024,256]{1,0:T(8,128)(2,1)S(1)} %bitcast.7), custom_call_target="tpu_custom_call" | custom-call | flops 1000000 | bytes 1052672 | tf_op jit(solution)/shard_map/pallas_call | solution.py:401
  57.5 0.1 collective-permute-done.12.refs_1_
  57.7 1.7 %collective-permute-done.13.refs_2_ = bf16[256,256]{1,0:T(8,128)(2,1)S(1)} collective-permute-done((bf16[256,256]{1,0:T(8,128)(2,1)S(1)}, bf16[256,256]{1,0:T(8,128)(2,1)S(1)}, u32[]{:S(2)}, u32[]{:S(2)}) %collective-permute-start.13) | collective-permute-done | bytes 131104 | tf_op jit(solution)/shard_map/ppermute | solution.py:417
  59.4 0.0 collective-permute-done.14.refs_3_
  59.4 0.8 %shard_map.87 = (bf16[256,512]{1,0:T(8,128)(2,1)}, bf16[256,512]{1,0:T(8,128)(2,1)}) custom-call(bf16[256,256]{1,0:T(8,128)(2,1)S(1)} %get-tuple-element.83.refs_0_, bf16[256,256]{1,0:T(8,128)(2,1)S(1)} %collective-permute-done.12.refs_1_, bf16[256,256]{1,0:T(8,128)(2,1)S(1)} %collective-permute-done.13.refs_2_, ...), custom_call_target="tpu_custom_call" | custom-call | flops 1000000 | bytes 1048576 | tf_op jit(solution)/shard_map/pallas_call | solution.py:401
  (7 shorter events, 0.0 us)
Async XLA Ops:
  0.6 1.0 %copy-start.3 = (bf16[256,512]{1,0:T(8,128)(2,1)S(1)}, bf16[256,512]{1,0:T(8,128)(2,1)}, u32[]{:S(2)}) copy-start(bf16[256,512]{1,0:T(8,128)(2,1)} %refs_1_.2) | copy-start | bytes 786436
  0.6 1.0 %copy-start.2 = (bf16[256,512]{1,0:T(8,128)(2,1)S(1)}, bf16[256,512]{1,0:T(8,128)(2,1)}, u32[]{:S(2)}) copy-start(bf16[256,512]{1,0:T(8,128)(2,1)} %refs_0_.2) | copy-start | bytes 786436
  1.7 6.1 %copy-start = (bf16[256,512]{1,0:T(8,128)(2,1)S(1)}, bf16[256,512]{1,0:T(8,128)(2,1)}, u32[]{:S(2)}) copy-start(bf16[256,512]{1,0:T(8,128)(2,1)} %refs_0_.3) | copy-start | bytes 786436
  1.7 6.1 %copy-start.1 = (bf16[256,512]{1,0:T(8,128)(2,1)S(1)}, bf16[256,512]{1,0:T(8,128)(2,1)}, u32[]{:S(2)}) copy-start(bf16[256,512]{1,0:T(8,128)(2,1)} %refs_1_.3) | copy-start | bytes 786436
  1.9 10.4 %collective-permute-start = (bf16[256,256]{1,0:T(8,128)(2,1)S(1)}, bf16[256,256]{1,0:T(8,128)(2,1)S(1)}, u32[]{:S(2)}, u32[]{:S(2)}) collective-permute-start(bf16[256,256]{1,0:T(8,128)(2,1)S(1)} %get-tuple-element.48), channel_id=1, source_target_pairs={{0,8},{8,16},{16,24},{24,0},{1,9},{9,17},{17,25},{25,1},{2,10},{10... | collective-permute-start | bytes 393224 | tf_op jit(solution)/shard_map/ppermute | solution.py:417
  3.5 8.9 %collective-permute-start.1 = (bf16[256,256]{1,0:T(8,128)(2,1)S(1)}, bf16[256,256]{1,0:T(8,128)(2,1)S(1)}, u32[]{:S(2)}, u32[]{:S(2)}) collective-permute-start(bf16[256,256]{1,0:T(8,128)(2,1)S(1)} %get-tuple-element.49), channel_id=1, source_target_pairs={{0,16},{8,24},{16,0},{24,8},{1,17},{9,25},{17,1},{25,9},{2,18},{10... | collective-permute-start | bytes 393224 | tf_op jit(solution)/shard_map/ppermute | solution.py:417
  6.4 6.0 %collective-permute-start.2 = (bf16[256,256]{1,0:T(8,128)(2,1)S(1)}, bf16[256,256]{1,0:T(8,128)(2,1)S(1)}, u32[]{:S(2)}, u32[]{:S(2)}) collective-permute-start(bf16[256,256]{1,0:T(8,128)(2,1)S(1)} %get-tuple-element.50), channel_id=1, source_target_pairs={{0,24},{8,0},{16,8},{24,16},{1,25},{9,1},{17,9},{25,17},{2,26},{10... | collective-permute-start | bytes 393224 | tf_op jit(solution)/shard_map/ppermute | solution.py:417
  8.8 18.0 %all-to-all-start = ((bf16[4,256,256]{2,1,0:T(8,128)(2,1)}), bf16[4,256,256]{2,1,0:T(8,128)(2,1)S(1)}, u32[]{:S(2)}, u32[]{:S(2)}) async-start(bf16[4,256,256]{2,1,0:T(8,128)(2,1)} %bitcast), calls=%async_computation | async-start | bytes 1048576 | tf_op jit(solution)/shard_map/all_to_all | solution.py:422
  13.2 9.6 %collective-permute-start.3 = (bf16[256,256]{1,0:T(8,128)(2,1)S(1)}, bf16[256,256]{1,0:T(8,128)(2,1)S(1)}, u32[]{:S(2)}, u32[]{:S(2)}) collective-permute-start(bf16[256,256]{1,0:T(8,128)(2,1)S(1)} %get-tuple-element.52), channel_id=1, source_target_pairs={{0,32},{32,0},{64,96},{96,64},{128,160},{160,128},{192,224},{224,1... | collective-permute-start | bytes 393224 | tf_op jit(solution)/shard_map/ppermute | solution.py:426
  15.2 7.4 %collective-permute-start.5 = (bf16[64,256]{1,0:T(8,128)(2,1)S(1)}, bf16[64,256]{1,0:T(8,128)(2,1)S(1)}, u32[]{:S(2)}, u32[]{:S(2)}) collective-permute-start(bf16[64,256]{1,0:T(8,128)(2,1)S(1)} %get-tuple-element.53.refs_0_), channel_id=1, source_target_pairs={{0,96},{32,64},{64,32},{96,0},{128,224},{160,192},{192,160},{224,1... | collective-permute-start | bytes 98312 | tf_op jit(solution)/shard_map/ppermute | solution.py:426
  18.0 4.8 %collective-permute-start.4 = (bf16[64,256]{1,0:T(8,128)(2,1)S(1)}, bf16[64,256]{1,0:T(8,128)(2,1)S(1)}, u32[]{:S(2)}, u32[]{:S(2)}) collective-permute-start(bf16[64,256]{1,0:T(8,128)(2,1)S(1)} %get-tuple-element.53.refs_0_), channel_id=1, source_target_pairs={{0,64},{32,96},{64,0},{96,32},{128,192},{160,224},{192,128},{224,1... | collective-permute-start | bytes 98312 | tf_op jit(solution)/shard_map/ppermute | solution.py:426
  18.4 10.3 %collective-permute-start.7 = (bf16[128,256]{1,0:T(8,128)(2,1)S(1)}, bf16[128,256]{1,0:T(8,128)(2,1)S(1)}, u32[]{:S(2)}, u32[]{:S(2)}) collective-permute-start(bf16[128,256]{1,0:T(8,128)(2,1)S(1)} %get-tuple-element.58), channel_id=1, source_target_pairs={{0,224},{32,64},{64,32},{96,128},{128,96},{160,192},{192,160},{224... | collective-permute-start | bytes 196616 | tf_op jit(solution)/shard_map/ppermute | solution.py:453
  23.1 6.6 %collective-permute-start.6 = (bf16[128,256]{1,0:T(8,128)(2,1)S(1)}, bf16[128,256]{1,0:T(8,128)(2,1)S(1)}, u32[]{:S(2)}, u32[]{:S(2)}) collective-permute-start(bf16[128,256]{1,0:T(8,128)(2,1)S(1)} %shard_map.80), channel_id=1, source_target_pairs={{0,192},{32,224},{64,128},{96,160},{128,64},{160,96},{192,0},{224,... | collective-permute-start | bytes 196616 | tf_op jit(solution)/shard_map/ppermute | solution.py:455
  30.6 7.8 %collective-permute-start.8 = (bf16[256,256]{1,0:T(8,128)(2,1)S(1)}, bf16[256,256]{1,0:T(8,128)(2,1)S(1)}, u32[]{:S(2)}, u32[]{:S(2)}) collective-permute-start(bf16[256,256]{1,0:T(8,128)(2,1)S(1)} %get-tuple-element.70), channel_id=1, source_target_pairs={{0,224},{32,192},{64,160},{96,128},{128,96},{160,64},{192,32},{224... | collective-permute-start | bytes 393224 | tf_op jit(solution)/shard_map/ppermute | solution.py:426
  38.6 9.9 %collective-permute-start.9 = (bf16[256,256]{1,0:T(8,128)(2,1)S(1)}, bf16[256,256]{1,0:T(8,128)(2,1)S(1)}, u32[]{:S(2)}, u32[]{:S(2)}) collective-permute-start(bf16[256,256]{1,0:T(8,128)(2,1)S(1)} %get-tuple-element.80), channel_id=1, source_target_pairs={{0,32},{32,0},{64,96},{96,64},{128,160},{160,128},{192,224},{224,1... | collective-permute-start | bytes 393224 | tf_op jit(solution)/shard_map/ppermute | solution.py:426
  41.0 7.5 %collective-permute-start.11 = (bf16[192,256]{1,0:T(8,128)(2,1)S(1)}, bf16[192,256]{1,0:T(8,128)(2,1)S(1)}, u32[]{:S(2)}, u32[]{:S(2)}) collective-permute-start(bf16[192,256]{1,0:T(8,128)(2,1)S(1)} %get-tuple-element.82), channel_id=1, source_target_pairs={{0,96},{32,64},{64,32},{96,0},{128,224},{160,192},{192,160},{224,1... | collective-permute-start | bytes 294920 | tf_op jit(solution)/shard_map/ppermute | solution.py:426
  43.0 5.5 %collective-permute-start.10 = (bf16[64,256]{1,0:T(8,128)(2,1)S(1)}, bf16[64,256]{1,0:T(8,128)(2,1)S(1)}, u32[]{:S(2)}, u32[]{:S(2)}) collective-permute-start(bf16[64,256]{1,0:T(8,128)(2,1)S(1)} %get-tuple-element.81), channel_id=1, source_target_pairs={{0,64},{32,96},{64,0},{96,32},{128,192},{160,224},{192,128},{224,1... | collective-permute-start | bytes 98312 | tf_op jit(solution)/shard_map/ppermute | solution.py:426
  43.9 12.7 %all-to-all-start.1 = ((bf16[4,256,256]{2,1,0:T(8,128)(2,1)}), bf16[4,256,256]{2,1,0:T(8,128)(2,1)S(1)}, u32[]{:S(2)}, u32[]{:S(2)}) async-start(bf16[4,256,256]{2,1,0:T(8,128)(2,1)} %bitcast.2), calls=%async_computation.1 | async-start | bytes 1048576 | tf_op jit(solution)/shard_map/all_to_all | solution.py:422
  49.2 8.5 %collective-permute-start.12 = (bf16[256,256]{1,0:T(8,128)(2,1)S(1)}, bf16[256,256]{1,0:T(8,128)(2,1)S(1)}, u32[]{:S(2)}, u32[]{:S(2)}) collective-permute-start(bf16[256,256]{1,0:T(8,128)(2,1)S(1)} %get-tuple-element.84), channel_id=1, source_target_pairs={{0,8},{8,16},{16,24},{24,0},{1,9},{9,17},{17,25},{25,1},{2,10},{10... | collective-permute-start | bytes 393224 | tf_op jit(solution)/shard_map/ppermute | solution.py:417
  51.3 8.1 %collective-permute-start.13 = (bf16[256,256]{1,0:T(8,128)(2,1)S(1)}, bf16[256,256]{1,0:T(8,128)(2,1)S(1)}, u32[]{:S(2)}, u32[]{:S(2)}) collective-permute-start(bf16[256,256]{1,0:T(8,128)(2,1)S(1)} %get-tuple-element.85), channel_id=1, source_target_pairs={{0,16},{8,24},{16,0},{24,8},{1,17},{9,25},{17,1},{25,9},{2,18},{10... | collective-permute-start | bytes 393224 | tf_op jit(solution)/shard_map/ppermute | solution.py:417
  54.0 5.5 %collective-permute-start.14 = (bf16[256,256]{1,0:T(8,128)(2,1)S(1)}, bf16[256,256]{1,0:T(8,128)(2,1)S(1)}, u32[]{:S(2)}, u32[]{:S(2)}) collective-permute-start(bf16[256,256]{1,0:T(8,128)(2,1)S(1)} %get-tuple-element.86), channel_id=1, source_target_pairs={{0,24},{8,0},{16,8},{24,16},{1,25},{9,1},{17,9},{25,17},{2,26},{10... | collective-permute-start | bytes 393224 | tf_op jit(solution)/shard_map/ppermute | solution.py:417

commit v6 on v5

--- a/solution.py
+++ b/solution.py
@@ -335,7 +335,7 @@
 
 
 def spread_kernel(
-    back_ref, g4_ref, g3_ref, facing_ref, other_ref, s1_ref, s2_ref, s3_ref, keep_ref
+    back_ref, g4_ref, g3_ref, facing_ref, other_ref, s1_ref, s2_ref, s3_ref, keep_ref, *_
 ):
     z = lax.axis_index("z")
     twice = repeat_matrix(B // 4, 1)
@@ -352,7 +352,7 @@
     keep_ref[...] = dot(fourfold, rows(0)) * 0.5
 
 
-def local_kernel(own_ref, one_ref, two_ref, out_ref, *_):
+def local_kernel(own_ref, one_ref, two_ref, out_ref):
     matrix = repeat_matrix(B, 1)
     for n in range(2):
         two = expand(matrix, two_ref[n * B : (n + 1) * B] * ROOT_HALF)
@@ -479,18 +479,15 @@
         vmem=20,
     )
     back_7 = over_z(g_top, 7)
-    s1, s2, s3, keep = call(
+    (own,) = call(local_kernel, [g_own, g_one, g_two], [((PLANE, 2 * D), F32)])
+    s1, s2, s3, keep, og = call(
         spread_kernel,
         [back_7, g4, g3, g_facing, g_other],
-        [double, half, tail, wide],
-    )
-    own, og = call(
-        local_kernel,
-        [g_own, g_one, g_two],
-        [((PLANE, 2 * D), F32), plane],
-        after=[og, keep],
-        alias={3: 1},
-    )
+        [double, half, tail, wide, plane],
+        after=[og, own],
+        alias={5: 4},
+    )
+    back_1, back_2, back_3 = over_z(s1, 1), over_z(s2, 2), over_z(s3, 3)
     og = across_y(og)
     back_1, back_2, back_3 = over_z(s1, 1), over_z(s2, 2), over_z(s3, 3)
     whole = ((PIECE, NY * D), BF)

time: 61.3 us -> 60.5 us (0.987)
  waiting for transfers between devices: 5.24 us -> 4.57 us
where the time goes in v6:
time: 60.5 us; the launch traced here: 59.7 us
  starting transfers between devices  41.6 us (69%)
  Pallas kernels  11.5 us (19%)
  waiting for transfers between devices  4.57 us (8%)
  local copies, waits for them, and re-layouts  1.01 us (2%)
  between operations  0.94 us (2%)
    ppermute x7, starting transfers between devices, over_z(): return lax.ppermute(array, 'z', [(i, i ^ d) for i in range(NZ)])  13.7 us
    ppermute x6, starting transfers between devices, around_y(): lax.ppermute(pieces[d], 'y', [(i, (i + d) % NY) for i in range(NY)])  12 us
    pallas_call x13, Pallas kernels, call(): pl.pallas_call(body, out_shape=[jax.ShapeDtypeStruct(s, t) for s, t in ou...  11.5 us
    all_to_all x2, starting transfers between devices, across_y(): return lax.all_to_all(array, 'y', split_axis=0, concat_axis=0, tiled=True)  8.02 us
    ppermute x1, starting transfers between devices, per_device(): from_side = lax.ppermute(side, 'z', SIDE)  4.16 us
    ppermute x1, starting transfers between devices, per_device(): from_7 = lax.ppermute(top, 'z', TOP)  3.66 us
    ppermute x6, waiting for transfers between devices, around_y(): lax.ppermute(pieces[d], 'y', [(i, (i + d) % NY) for i in range(NY)])  2.07 us
  transfers between devices with their start and end apart: 17, of which 7 were waited for; matrix products, arithmetic and copies ran while one was open for 0% of the time, Pallas kernels for 16%

profile of v6, /device:TPU:6, one launch (start us, length us, event | category | flops | bytes accessed | tf_op | source)
XLA Modules:
  0.0 59.7 jit_solution(5208657541330307797)
XLA Ops:
  0.7 0.9 %copy-done.3 = bf16[256,512]{1,0:T(8,128)(2,1)S(1)} copy-done((bf16[256,512]{1,0:T(8,128)(2,1)S(1)}, bf16[256,512]{1,0:T(8,128)(2,1)}, u32[]{:S(2)}) %copy-start.3) | copy-done | bytes 262168
  1.6 0.1 copy-done.2
  1.7 0.2 shard_map.76
  1.9 1.7 %collective-permute-start = (bf16[256,256]{1,0:T(8,128)(2,1)S(1)}, bf16[256,256]{1,0:T(8,128)(2,1)S(1)}, u32[]{:S(2)}, u32[]{:S(2)}) collective-permute-start(bf16[256,256]{1,0:T(8,128)(2,1)S(1)} %get-tuple-element.47), channel_id=1, source_target_pairs={{0,8},{8,16},{16,24},{24,0},{1,9},{9,17},{17,25},{25,1},{2,10},{10... | collective-permute-start | bytes 393224 | tf_op jit(solution)/shard_map/ppermute | solution.py:417
  3.5 2.9 %collective-permute-start.1 = (bf16[256,256]{1,0:T(8,128)(2,1)S(1)}, bf16[256,256]{1,0:T(8,128)(2,1)S(1)}, u32[]{:S(2)}, u32[]{:S(2)}) collective-permute-start(bf16[256,256]{1,0:T(8,128)(2,1)S(1)} %get-tuple-element.48), channel_id=1, source_target_pairs={{0,16},{8,24},{16,0},{24,8},{1,17},{9,25},{17,1},{25,9},{2,18},{10... | collective-permute-start | bytes 393224 | tf_op jit(solution)/shard_map/ppermute | solution.py:417
  6.4 1.3 %collective-permute-start.2 = (bf16[256,256]{1,0:T(8,128)(2,1)S(1)}, bf16[256,256]{1,0:T(8,128)(2,1)S(1)}, u32[]{:S(2)}, u32[]{:S(2)}) collective-permute-start(bf16[256,256]{1,0:T(8,128)(2,1)S(1)} %get-tuple-element.49), channel_id=1, source_target_pairs={{0,24},{8,0},{16,8},{24,16},{1,25},{9,1},{17,9},{25,17},{2,26},{10... | collective-permute-start | bytes 393224 | tf_op jit(solution)/shard_map/ppermute | solution.py:417
  7.8 1.0 %shard_map.77.refs_4_ = bf16[1024,256]{1,0:T(8,128)(2,1)} custom-call(bf16[256,512]{1,0:T(8,128)(2,1)S(1)} %copy-done, bf16[256,512]{1,0:T(8,128)(2,1)S(1)} %copy-done.1), custom_call_target="tpu_custom_call" | custom-call | flops 1000000 | bytes 1048576 | tf_op jit(solution)/shard_map/pallas_call | solution.py:401
  8.8 3.5 %all-to-all-start = ((bf16[4,256,256]{2,1,0:T(8,128)(2,1)}), bf16[4,256,256]{2,1,0:T(8,128)(2,1)S(1)}, u32[]{:S(2)}, u32[]{:S(2)}) async-start(bf16[4,256,256]{2,1,0:T(8,128)(2,1)} %bitcast), calls=%async_computation | async-start | bytes 1048576 | tf_op jit(solution)/shard_map/all_to_all | solution.py:422
  12.2 0.0 collective-permute-done.refs_1_
  12.3 0.2 collective-permute-done.1.refs_2_
  12.4 0.0 collective-permute-done.2.refs_3_
  12.4 0.7 %shard_map.78 = (bf16[1024,256]{1,0:T(8,128)(2,1)S(1)}, bf16[256,256]{1,0:T(8,128)(2,1)S(1)}, bf16[64,256]{1,0:T(8,128)(2,1)S(1)}, bf16[128,256]{1,0:T(8,128)(2,1)S(1)}) custom-call(bf16[256,256]{1,0:T(8,128)(2,1)S(1)} %get-tuple-element.46.refs_0_, bf16[256,256]{1,0:T(8,128)(2,1)S(1)} %collective-permute-done.refs_1_, ...), custom_call_target="tpu_custom_call" | custom-call | flops 5000000000 | bytes 1277952 | tf_op jit(solution)/shard_map/pallas_call | solution.py:401
  13.2 2.0 %collective-permute-start.3 = (bf16[256,256]{1,0:T(8,128)(2,1)S(1)}, bf16[256,256]{1,0:T(8,128)(2,1)S(1)}, u32[]{:S(2)}, u32[]{:S(2)}) collective-permute-start(bf16[256,256]{1,0:T(8,128)(2,1)S(1)} %get-tuple-element.50), channel_id=1, source_target_pairs={{0,32},{32,0},{64,96},{96,64},{128,160},{160,128},{192,224},{224,1... | collective-permute-start | bytes 393224 | tf_op jit(solution)/shard_map/ppermute | solution.py:426
  15.2 2.8 %collective-permute-start.6 = (bf16[64,256]{1,0:T(8,128)(2,1)S(1)}, bf16[64,256]{1,0:T(8,128)(2,1)S(1)}, u32[]{:S(2)}, u32[]{:S(2)}) collective-permute-start(bf16[64,256]{1,0:T(8,128)(2,1)S(1)} %get-tuple-element.52.refs_0_), channel_id=1, source_target_pairs={{0,96},{32,64},{64,32},{96,0},{128,224},{160,192},{192,160},{224,1... | collective-permute-start | bytes 98312 | tf_op jit(solution)/shard_map/ppermute | solution.py:426
  18.0 0.5 collective-permute-start.5
  18.4 4.2 %collective-permute-start.4 = (bf16[128,256]{1,0:T(8,128)(2,1)S(1)}, bf16[128,256]{1,0:T(8,128)(2,1)S(1)}, u32[]{:S(2)}, u32[]{:S(2)}) collective-permute-start(bf16[128,256]{1,0:T(8,128)(2,1)S(1)} %get-tuple-element.51), channel_id=1, source_target_pairs={{0,224},{32,64},{64,32},{96,128},{128,96},{160,192},{192,160},{224... | collective-permute-start | bytes 196616 | tf_op jit(solution)/shard_map/ppermute | solution.py:453
  22.6 0.0 collective-permute-done.6.refs_3_
  22.6 0.2 collective-permute-done.5.refs_2_
  22.8 0.0 collective-permute-done.3.refs_1_.refs_0_
  22.8 0.3 shard_map.79
  23.1 3.7 %collective-permute-start.7 = (bf16[128,256]{1,0:T(8,128)(2,1)S(1)}, bf16[128,256]{1,0:T(8,128)(2,1)S(1)}, u32[]{:S(2)}, u32[]{:S(2)}) collective-permute-start(bf16[128,256]{1,0:T(8,128)(2,1)S(1)} %shard_map.79), channel_id=1, source_target_pairs={{0,192},{32,224},{64,128},{96,160},{128,64},{160,96},{192,0},{224,... | collective-permute-start | bytes 196616 | tf_op jit(solution)/shard_map/ppermute | solution.py:455
  26.8 0.0 all-to-all-done
  26.8 2.0 %shard_map.80 = (bf16[128,2048]{1,0:T(8,128)(2,1)S(1)}, bf16[128,2048]{1,0:T(8,128)(2,1)S(1)}, f32[4,1024,256]{2,1,0:T(8,128)S(1)}, f32[4,1024,256]{2,1,0:T(8,128)S(1)}, f32[8,1024]{1,0:T(8,128)S(1)}) custom-call(bf16[1024,256]{1,0:T(8,128)(2,1)S(1)} %get-tuple-element.53.refs_0_, bf16[256,256]{1,0:T(8,128)(2,1)S(1)} %collective-permute-done.3.refs_1_.refs_0_, ...), custom_call_target="tpu_custom_call" | custom-call | flops 1000000000 | bytes 10715136 | tf_op jit(solution)/shard_map/pallas_call | solution.py:401
  28.7 0.0 collective-permute-done.4.refs_1_
  28.7 0.9 %collective-permute-done.7.refs_2_.refs_5_ = bf16[128,256]{1,0:T(8,128)(2,1)S(1)} collective-permute-done((bf16[128,256]{1,0:T(8,128)(2,1)S(1)}, bf16[128,256]{1,0:T(8,128)(2,1)S(1)}, u32[]{:S(2)}, u32[]{:S(2)}) %collective-permute-start.7) | collective-permute-done | bytes 65568 | tf_op jit(solution)/shard_map/ppermute | solution.py:455
  29.7 0.9 %shard_map.81 = (bf16[256,256]{1,0:T(8,128)(2,1)S(1)}, bf16[128,256]{1,0:T(8,128)(2,1)S(1)}, bf16[128,256]{1,0:T(8,128)(2,1)S(1)}, bf16[2,128,256]{2,1,0:T(8,128...) custom-call(bf16[256,256]{1,0:T(8,128)(2,1)S(1)} %collective-permute, ...), custom_call_target="tpu_custom_call" | custom-call | flops 100000000 | bytes 2031616 | tf_op jit(solution)/shard_map/pallas_call | solution.py:401
  30.6 4.0 %collective-permute-start.8 = (bf16[256,256]{1,0:T(8,128)(2,1)S(1)}, bf16[256,256]{1,0:T(8,128)(2,1)S(1)}, u32[]{:S(2)}, u32[]{:S(2)}) collective-permute-start(bf16[256,256]{1,0:T(8,128)(2,1)S(1)} %get-tuple-element.55), channel_id=1, source_target_pairs={{0,224},{32,192},{64,160},{96,128},{128,96},{160,64},{192,32},{224... | collective-permute-start | bytes 393224 | tf_op jit(solution)/shard_map/ppermute | solution.py:426
  34.6 3.0 %shard_map.82 = (bf16[1024,256]{1,0:T(8,128)(2,1)}, f32[128,256]{1,0:T(8,128)S(1)}, f32[128,256]{1,0:T(8,128)S(1)}, f32[1024,256]{1,0:T(8,128)S(1)}, f32[512,256]{1,0:T(8,128)S(1)}, /*index=5*/f32[256,256]{1,0:T(8,128)S(1)}) custom-call(bf16[128,2048]{1,0:T(8,128)(2,1)S(1)} %get-tuple-element.56.refs_0_, bf16[128,2048]{1,0:T(8,128)(2,1)S(1)} %get-tuple-element.57.refs_1_, ...), custom_call_target="tpu_custom_call" | custom-call | flops 2000000000 | bytes 13598720 | tf_op jit(solution)/shard_map/pallas_call | solution.py:401
  37.6 0.9 %shard_map.83.refs_6_.refs_0_ = f32[1024,256]{1,0:T(8,128)S(1)} custom-call(f32[1024,256]{1,0:T(8,128)S(1)} %get-tuple-element.71.refs_0_, f32[512,256]{1,0:T(8,128)S(1)} %get-tuple-element.72.refs_1_, f32[256,256]{1,0:T(8,128)S(1)} %get-tuple-element.73.refs_2_), custom_call_target="tpu_custom_call" | custom-call | flops 1000000 | bytes 2883584 | tf_op jit(solution)/shard_map/pallas_call | solution.py:401
  38.5 0.0 collective-permute-done.8.refs_0_.refs_5_
  38.5 0.2 shard_map.84
  38.7 2.4 %collective-permute-start.9 = (bf16[256,256]{1,0:T(8,128)(2,1)S(1)}, bf16[256,256]{1,0:T(8,128)(2,1)S(1)}, u32[]{:S(2)}, u32[]{:S(2)}) collective-permute-start(bf16[256,256]{1,0:T(8,128)(2,1)S(1)} %get-tuple-element.78), channel_id=1, source_target_pairs={{0,32},{32,0},{64,96},{96,64},{128,160},{160,128},{192,224},{224,1... | collective-permute-start | bytes 393224 | tf_op jit(solution)/shard_map/ppermute | solution.py:426
  41.2 2.0 %collective-permute-start.11 = (bf16[192,256]{1,0:T(8,128)(2,1)S(1)}, bf16[192,256]{1,0:T(8,128)(2,1)S(1)}, u32[]{:S(2)}, u32[]{:S(2)}) collective-permute-start(bf16[192,256]{1,0:T(8,128)(2,1)S(1)} %get-tuple-element.80), channel_id=1, source_target_pairs={{0,96},{32,64},{64,32},{96,0},{128,224},{160,192},{192,160},{224,1... | collective-permute-start | bytes 294920 | tf_op jit(solution)/shard_map/ppermute | solution.py:426
  43.2 0.0 collective-permute-start.10
  43.2 4.5 %all-to-all-start.1 = ((bf16[4,256,256]{2,1,0:T(8,128)(2,1)}), bf16[4,256,256]{2,1,0:T(8,128)(2,1)S(1)}, u32[]{:S(2)}, u32[]{:S(2)}) async-start(bf16[4,256,256]{2,1,0:T(8,128)(2,1)} %bitcast.2), calls=%async_computation.1 | async-start | bytes 1048576 | tf_op jit(solution)/shard_map/all_to_all | solution.py:422
  47.7 0.6 collective-permute-done.10.refs_3_
  48.3 0.0 collective-permute-done.11.refs_4_
  48.3 0.0 collective-permute-done.9.refs_2_
  48.3 0.7 %shard_map.86 = (bf16[256,256]{1,0:T(8,128)(2,1)S(1)}, bf16[256,256]{1,0:T(8,128)(2,1)S(1)}, bf16[256,256]{1,0:T(8,128)(2,1)S(1)}, bf16[256,256]{1,0:T(8,128)(2,1)S(1)}) custom-call(f32[1024,256]{1,0:T(8,128)S(1)} %shard_map.83.refs_6_.refs_0_, f32[128,256]{1,0:T(8,128)S(1)} %get-tuple-element.77.refs_1_, ...), custom_call_target="tpu_custom_call" | custom-call | flops 5000000000 | bytes 2097152 | tf_op jit(solution)/shard_map/pallas_call | solution.py:401
  49.0 2.0 %collective-permute-start.12 = (bf16[256,256]{1,0:T(8,128)(2,1)S(1)}, bf16[256,256]{1,0:T(8,128)(2,1)S(1)}, u32[]{:S(2)}, u32[]{:S(2)}) collective-permute-start(bf16[256,256]{1,0:T(8,128)(2,1)S(1)} %get-tuple-element.82), channel_id=1, source_target_pairs={{0,8},{8,16},{16,24},{24,0},{1,9},{9,17},{17,25},{25,1},{2,10},{10... | collective-permute-start | bytes 393224 | tf_op jit(solution)/shard_map/ppermute | solution.py:417
  51.0 2.7 %collective-permute-start.13 = (bf16[256,256]{1,0:T(8,128)(2,1)S(1)}, bf16[256,256]{1,0:T(8,128)(2,1)S(1)}, u32[]{:S(2)}, u32[]{:S(2)}) collective-permute-start(bf16[256,256]{1,0:T(8,128)(2,1)S(1)} %get-tuple-element.83), channel_id=1, source_target_pairs={{0,16},{8,24},{16,0},{24,8},{1,17},{9,25},{17,1},{25,9},{2,18},{10... | collective-permute-start | bytes 393224 | tf_op jit(solution)/shard_map/ppermute | solution.py:417
  53.7 1.5 %collective-permute-start.14 = (bf16[256,256]{1,0:T(8,128)(2,1)S(1)}, bf16[256,256]{1,0:T(8,128)(2,1)S(1)}, u32[]{:S(2)}, u32[]{:S(2)}) collective-permute-start(bf16[256,256]{1,0:T(8,128)(2,1)S(1)} %get-tuple-element.84), channel_id=1, source_target_pairs={{0,24},{8,0},{16,8},{24,16},{1,25},{9,1},{17,9},{25,17},{2,26},{10... | collective-permute-start | bytes 393224 | tf_op jit(solution)/shard_map/ppermute | solution.py:417
  55.1 0.8 %all-to-all-done.1 = bf16[4,256,256]{2,1,0:T(8,128)(2,1)S(1)} async-done(((bf16[4,256,256]{2,1,0:T(8,128)(2,1)}), bf16[4,256,256]{2,1,0:T(8,128)(2,1)S(1)}, u32[]{:S(2)}, u32[]{:S(2)}) %all-to-all-start.1) | async-done | bytes 524320 | tf_op jit(solution)/shard_map/all_to_all | solution.py:422
  55.9 0.8 %shard_map.85 = (bf16[256,512]{1,0:T(8,128)(2,1)}, bf16[256,512]{1,0:T(8,128)(2,1)}, f32[8,128]{1,0:T(8,128)S(1)}) custom-call(bf16[1024,256]{1,0:T(8,128)(2,1)S(1)} %bitcast.7), custom_call_target="tpu_custom_call" | custom-call | flops 1000000 | bytes 1052672 | tf_op jit(solution)/shard_map/pallas_call | solution.py:401
  56.8 0.1 collective-permute-done.12.refs_1_
  56.9 1.7 %collective-permute-done.13.refs_2_ = bf16[256,256]{1,0:T(8,128)(2,1)S(1)} collective-permute-done((bf16[256,256]{1,0:T(8,128)(2,1)S(1)}, bf16[256,256]{1,0:T(8,128)(2,1)S(1)}, u32[]{:S(2)}, u32[]{:S(2)}) %collective-permute-start.13) | collective-permute-done | bytes 131104 | tf_op jit(solution)/shard_map/ppermute | solution.py:417
  58.7 0.0 collective-permute-done.14.refs_3_
  58.7 0.8 %shard_map.87 = (bf16[256,512]{1,0:T(8,128)(2,1)}, bf16[256,512]{1,0:T(8,128)(2,1)}) custom-call(bf16[256,256]{1,0:T(8,128)(2,1)S(1)} %get-tuple-element.81.refs_0_, bf16[256,256]{1,0:T(8,128)(2,1)S(1)} %collective-permute-done.12.refs_1_, bf16[256,256]{1,0:T(8,128)(2,1)S(1)} %collective-permute-done.13.refs_2_, ...), custom_call_target="tpu_custom_call" | custom-call | flops 1000000 | bytes 1048576 | tf_op jit(solution)/shard_map/pallas_call | solution.py:401
  (7 shorter events, 0.0 us)
Async XLA Ops:
  0.6 1.0 %copy-start.3 = (bf16[256,512]{1,0:T(8,128)(2,1)S(1)}, bf16[256,512]{1,0:T(8,128)(2,1)}, u32[]{:S(2)}) copy-start(bf16[256,512]{1,0:T(8,128)(2,1)} %refs_1_.2) | copy-start | bytes 786436
  0.6 1.0 %copy-start.2 = (bf16[256,512]{1,0:T(8,128)(2,1)S(1)}, bf16[256,512]{1,0:T(8,128)(2,1)}, u32[]{:S(2)}) copy-start(bf16[256,512]{1,0:T(8,128)(2,1)} %refs_0_.2) | copy-start | bytes 786436
  1.7 6.1 %copy-start = (bf16[256,512]{1,0:T(8,128)(2,1)S(1)}, bf16[256,512]{1,0:T(8,128)(2,1)}, u32[]{:S(2)}) copy-start(bf16[256,512]{1,0:T(8,128)(2,1)} %refs_0_.3) | copy-start | bytes 786436
  1.7 6.1 %copy-start.1 = (bf16[256,512]{1,0:T(8,128)(2,1)S(1)}, bf16[256,512]{1,0:T(8,128)(2,1)}, u32[]{:S(2)}) copy-start(bf16[256,512]{1,0:T(8,128)(2,1)} %refs_1_.3) | copy-start | bytes 786436
  1.9 10.4 %collective-permute-start = (bf16[256,256]{1,0:T(8,128)(2,1)S(1)}, bf16[256,256]{1,0:T(8,128)(2,1)S(1)}, u32[]{:S(2)}, u32[]{:S(2)}) collective-permute-start(bf16[256,256]{1,0:T(8,128)(2,1)S(1)} %get-tuple-element.47), channel_id=1, source_target_pairs={{0,8},{8,16},{16,24},{24,0},{1,9},{9,17},{17,25},{25,1},{2,10},{10... | collective-permute-start | bytes 393224 | tf_op jit(solution)/shard_map/ppermute | solution.py:417
  3.5 8.9 %collective-permute-start.1 = (bf16[256,256]{1,0:T(8,128)(2,1)S(1)}, bf16[256,256]{1,0:T(8,128)(2,1)S(1)}, u32[]{:S(2)}, u32[]{:S(2)}) collective-permute-start(bf16[256,256]{1,0:T(8,128)(2,1)S(1)} %get-tuple-element.48), channel_id=1, source_target_pairs={{0,16},{8,24},{16,0},{24,8},{1,17},{9,25},{17,1},{25,9},{2,18},{10... | collective-permute-start | bytes 393224 | tf_op jit(solution)/shard_map/ppermute | solution.py:417
  6.4 6.0 %collective-permute-start.2 = (bf16[256,256]{1,0:T(8,128)(2,1)S(1)}, bf16[256,256]{1,0:T(8,128)(2,1)S(1)}, u32[]{:S(2)}, u32[]{:S(2)}) collective-permute-start(bf16[256,256]{1,0:T(8,128)(2,1)S(1)} %get-tuple-element.49), channel_id=1, source_target_pairs={{0,24},{8,0},{16,8},{24,16},{1,25},{9,1},{17,9},{25,17},{2,26},{10... | collective-permute-start | bytes 393224 | tf_op jit(solution)/shard_map/ppermute | solution.py:417
  8.8 18.0 %all-to-all-start = ((bf16[4,256,256]{2,1,0:T(8,128)(2,1)}), bf16[4,256,256]{2,1,0:T(8,128)(2,1)S(1)}, u32[]{:S(2)}, u32[]{:S(2)}) async-start(bf16[4,256,256]{2,1,0:T(8,128)(2,1)} %bitcast), calls=%async_computation | async-start | bytes 1048576 | tf_op jit(solution)/shard_map/all_to_all | solution.py:422
  13.2 9.6 %collective-permute-start.3 = (bf16[256,256]{1,0:T(8,128)(2,1)S(1)}, bf16[256,256]{1,0:T(8,128)(2,1)S(1)}, u32[]{:S(2)}, u32[]{:S(2)}) collective-permute-start(bf16[256,256]{1,0:T(8,128)(2,1)S(1)} %get-tuple-element.50), channel_id=1, source_target_pairs={{0,32},{32,0},{64,96},{96,64},{128,160},{160,128},{192,224},{224,1... | collective-permute-start | bytes 393224 | tf_op jit(solution)/shard_map/ppermute | solution.py:426
  15.2 7.4 %collective-permute-start.6 = (bf16[64,256]{1,0:T(8,128)(2,1)S(1)}, bf16[64,256]{1,0:T(8,128)(2,1)S(1)}, u32[]{:S(2)}, u32[]{:S(2)}) collective-permute-start(bf16[64,256]{1,0:T(8,128)(2,1)S(1)} %get-tuple-element.52.refs_0_), channel_id=1, source_target_pairs={{0,96},{32,64},{64,32},{96,0},{128,224},{160,192},{192,160},{224,1... | collective-permute-start | bytes 98312 | tf_op jit(solution)/shard_map/ppermute | solution.py:426
  18.0 4.8 %collective-permute-start.5 = (bf16[64,256]{1,0:T(8,128)(2,1)S(1)}, bf16[64,256]{1,0:T(8,128)(2,1)S(1)}, u32[]{:S(2)}, u32[]{:S(2)}) collective-permute-start(bf16[64,256]{1,0:T(8,128)(2,1)S(1)} %get-tuple-element.52.refs_0_), channel_id=1, source_target_pairs={{0,64},{32,96},{64,0},{96,32},{128,192},{160,224},{192,128},{224,1... | collective-permute-start | bytes 98312 | tf_op jit(solution)/shard_map/ppermute | solution.py:426
  18.4 10.3 %collective-permute-start.4 = (bf16[128,256]{1,0:T(8,128)(2,1)S(1)}, bf16[128,256]{1,0:T(8,128)(2,1)S(1)}, u32[]{:S(2)}, u32[]{:S(2)}) collective-permute-start(bf16[128,256]{1,0:T(8,128)(2,1)S(1)} %get-tuple-element.51), channel_id=1, source_target_pairs={{0,224},{32,64},{64,32},{96,128},{128,96},{160,192},{192,160},{224... | collective-permute-start | bytes 196616 | tf_op jit(solution)/shard_map/ppermute | solution.py:453
  23.1 6.6 %collective-permute-start.7 = (bf16[128,256]{1,0:T(8,128)(2,1)S(1)}, bf16[128,256]{1,0:T(8,128)(2,1)S(1)}, u32[]{:S(2)}, u32[]{:S(2)}) collective-permute-start(bf16[128,256]{1,0:T(8,128)(2,1)S(1)} %shard_map.79), channel_id=1, source_target_pairs={{0,192},{32,224},{64,128},{96,160},{128,64},{160,96},{192,0},{224,... | collective-permute-start | bytes 196616 | tf_op jit(solution)/shard_map/ppermute | solution.py:455
  30.6 7.9 %collective-permute-start.8 = (bf16[256,256]{1,0:T(8,128)(2,1)S(1)}, bf16[256,256]{1,0:T(8,128)(2,1)S(1)}, u32[]{:S(2)}, u32[]{:S(2)}) collective-permute-start(bf16[256,256]{1,0:T(8,128)(2,1)S(1)} %get-tuple-element.55), channel_id=1, source_target_pairs={{0,224},{32,192},{64,160},{96,128},{128,96},{160,64},{192,32},{224... | collective-permute-start | bytes 393224 | tf_op jit(solution)/shard_map/ppermute | solution.py:426
  38.7 9.6 %collective-permute-start.9 = (bf16[256,256]{1,0:T(8,128)(2,1)S(1)}, bf16[256,256]{1,0:T(8,128)(2,1)S(1)}, u32[]{:S(2)}, u32[]{:S(2)}) collective-permute-start(bf16[256,256]{1,0:T(8,128)(2,1)S(1)} %get-tuple-element.78), channel_id=1, source_target_pairs={{0,32},{32,0},{64,96},{96,64},{128,160},{160,128},{192,224},{224,1... | collective-permute-start | bytes 393224 | tf_op jit(solution)/shard_map/ppermute | solution.py:426
  41.2 7.1 %collective-permute-start.11 = (bf16[192,256]{1,0:T(8,128)(2,1)S(1)}, bf16[192,256]{1,0:T(8,128)(2,1)S(1)}, u32[]{:S(2)}, u32[]{:S(2)}) collective-permute-start(bf16[192,256]{1,0:T(8,128)(2,1)S(1)} %get-tuple-element.80), channel_id=1, source_target_pairs={{0,96},{32,64},{64,32},{96,0},{128,224},{160,192},{192,160},{224,1... | collective-permute-start | bytes 294920 | tf_op jit(solution)/shard_map/ppermute | solution.py:426
  43.2 5.1 %collective-permute-start.10 = (bf16[64,256]{1,0:T(8,128)(2,1)S(1)}, bf16[64,256]{1,0:T(8,128)(2,1)S(1)}, u32[]{:S(2)}, u32[]{:S(2)}) collective-permute-start(bf16[64,256]{1,0:T(8,128)(2,1)S(1)} %get-tuple-element.79), channel_id=1, source_target_pairs={{0,64},{32,96},{64,0},{96,32},{128,192},{160,224},{192,128},{224,1... | collective-permute-start | bytes 98312 | tf_op jit(solution)/shard_map/ppermute | solution.py:426
  43.2 12.7 %all-to-all-start.1 = ((bf16[4,256,256]{2,1,0:T(8,128)(2,1)}), bf16[4,256,256]{2,1,0:T(8,128)(2,1)S(1)}, u32[]{:S(2)}, u32[]{:S(2)}) async-start(bf16[4,256,256]{2,1,0:T(8,128)(2,1)} %bitcast.2), calls=%async_computation.1 | async-start | bytes 1048576 | tf_op jit(solution)/shard_map/all_to_all | solution.py:422
  49.0 7.9 %collective-permute-start.12 = (bf16[256,256]{1,0:T(8,128)(2,1)S(1)}, bf16[256,256]{1,0:T(8,128)(2,1)S(1)}, u32[]{:S(2)}, u32[]{:S(2)}) collective-permute-start(bf16[256,256]{1,0:T(8,128)(2,1)S(1)} %get-tuple-element.82), channel_id=1, source_target_pairs={{0,8},{8,16},{16,24},{24,0},{1,9},{9,17},{17,25},{25,1},{2,10},{10... | collective-permute-start | bytes 393224 | tf_op jit(solution)/shard_map/ppermute | solution.py:417
  51.0 7.7 %collective-permute-start.13 = (bf16[256,256]{1,0:T(8,128)(2,1)S(1)}, bf16[256,256]{1,0:T(8,128)(2,1)S(1)}, u32[]{:S(2)}, u32[]{:S(2)}) collective-permute-start(bf16[256,256]{1,0:T(8,128)(2,1)S(1)} %get-tuple-element.83), channel_id=1, source_target_pairs={{0,16},{8,24},{16,0},{24,8},{1,17},{9,25},{17,1},{25,9},{2,18},{10... | collective-permute-start | bytes 393224 | tf_op jit(solution)/shard_map/ppermute | solution.py:417
  53.7 5.0 %collective-permute-start.14 = (bf16[256,256]{1,0:T(8,128)(2,1)S(1)}, bf16[256,256]{1,0:T(8,128)(2,1)S(1)}, u32[]{:S(2)}, u32[]{:S(2)}) collective-permute-start(bf16[256,256]{1,0:T(8,128)(2,1)S(1)} %get-tuple-element.84), channel_id=1, source_target_pairs={{0,24},{8,0},{16,8},{24,16},{1,25},{9,1},{17,9},{25,17},{2,26},{10... | collective-permute-start | bytes 393224 | tf_op jit(solution)/shard_map/ppermute | solution.py:417
